TPU v7x, 32 devices: a whole 2x2x4 slice. The times are simulated.
32 devices in a mesh: groups: 1, slab: 8 (over z, y), temp: 2 (over x), pen: 2 (over core).
Axes of the slice: x: 2, y: 2, z: 4, core: 2. Of those that a mesh axis runs over, the one named last changes fastest.
Arguments:
- moments: float32 [2, 3, 128, 128, 128], P(('groups', 'temp'), None, ('slab', 'pen')), may hold values from -1 to 1, as said below
- couplings: bfloat16 [3, 128, 128, 128], P('groups', ('slab', 'pen')), may hold values from -6 to 6
- noise: bfloat16 [2, 2, 3, 128, 128, 128], P(None, ('groups', 'temp'), None, ('slab', 'pen')), may hold values from -6 to 6
- kernel: float32 [6, 128, 128, 128], P(None, None, ('slab', 'pen')), may hold values from -2.5 to 2.5, as said below
- temps: float32 [2], replicated, may hold values from 0.05 to 2
- order: int32 [2], P('groups'), may hold values from 0 to 1, each once
- accept: int32 [2], P('groups'), may hold values 0 or 1
Outputs:
- moments_out: float32 [2, 3, 128, 128, 128], P(('groups', 'temp'), None, ('slab', 'pen'))
- labels: int32 [2], P('groups')
Inputs may be any that keep to these rules, and one draw needn't show every extreme that they name: `moments`: every moment vector (the three entries of one replica at one cell) has length one up to float32 rounding. kernel[c, i, j, l] equals kernel[c, (128 - i) % 128, (128 - j) % 128, (128 - l) % 128]. `order`: each temperature index appears once.
All inputs are finite; a program needn't handle non-finite values.
Results may differ from a plain program's by a relative error of at most 0.0003.
Values sent between devices are 32-bit elements; how exact they have to be, the bound alone decides.
No kernel may reach another device: no remote copies, remote signals or barrier semaphores. Data moves between devices by JAX's collectives and lax.ppermute only.
A program may use at most 128 MiB of HBM per device.

v0:
```python
import math

import jax
import jax.numpy as jnp
from jax import lax
from jax.sharding import PartitionSpec as P

TIME_STEP = 0.1
DAMPING = 0.5


def shifted(block, axis, distance):
    devices = range(lax.axis_size(axis))
    route = [((i - distance) % len(devices), i) for i in devices]
    return lax.ppermute(block, axis, route)


def cross(left, right, axis):
    left_parts = [lax.index_in_dim(left, component, axis, keepdims=False) for component in range(3)]
    right_parts = [
        lax.index_in_dim(right, component, axis, keepdims=False) for component in range(3)
    ]
    result = [
        left_parts[1] * right_parts[2] - left_parts[2] * right_parts[1],
        left_parts[2] * right_parts[0] - left_parts[0] * right_parts[2],
        left_parts[0] * right_parts[1] - left_parts[1] * right_parts[0],
    ]
    return jnp.stack(result, axis=axis)


def pair_labels(order, accept):
    slot_index = jnp.arange(order.shape[0], dtype=jnp.int32)
    position = jnp.sum(
        jnp.where(order[None, :] == slot_index[:, None], slot_index[None, :], 0), axis=1
    )
    mate_position = position + 1 - 2 * (position % 2)
    partner = jnp.sum(
        jnp.where(slot_index[None, :] == mate_position[:, None], order[None, :], 0), axis=1
    )
    partner_flag = jnp.sum(
        jnp.where(slot_index[None, :] == partner[:, None], accept[None, :], 0), axis=1
    )
    accepted = accept * partner_flag
    return jnp.where(accepted == 1, partner, slot_index)


def slot_sigma(labels, temps):
    slot_index = jnp.arange(temps.shape[0], dtype=jnp.int32)
    picked = jnp.sum(
        jnp.where(
            labels[:, None] == slot_index[None, :], temps[None, :], jnp.zeros_like(temps)[None, :]
        ),
        axis=1,
    )
    return jnp.sqrt(2.0 * DAMPING * picked / TIME_STEP)


def angle_tables(length):
    positions = jnp.arange(length, dtype=jnp.int32)
    product = positions[:, None] * positions[None, :] % length
    angles = 2.0 * math.pi / length * product.astype(jnp.float32)
    return (jnp.cos(angles), jnp.sin(angles))


def twist(packed, cosine_table, sine_table, pattern, orientation):
    cosine_part = jnp.einsum(pattern, packed, cosine_table, precision=lax.Precision.HIGHEST)
    sine_part = jnp.einsum(pattern, packed, sine_table, precision=lax.Precision.HIGHEST)
    middle = packed.shape[-1] // 2
    turned = jnp.concatenate([sine_part[..., middle:], -sine_part[..., :middle]], axis=-1)
    return cosine_part + orientation * turned


def pair_twist(stacked, cosine_table, sine_table, pattern, orientation):
    real_part = stacked[:, 0]
    imag_part = stacked[:, 1]
    real_cos = jnp.einsum(pattern, real_part, cosine_table, precision=lax.Precision.HIGHEST)
    real_sin = jnp.einsum(pattern, real_part, sine_table, precision=lax.Precision.HIGHEST)
    imag_cos = jnp.einsum(pattern, imag_part, cosine_table, precision=lax.Precision.HIGHEST)
    imag_sin = jnp.einsum(pattern, imag_part, sine_table, precision=lax.Precision.HIGHEST)
    return jnp.stack([real_cos + orientation * imag_sin, imag_cos - orientation * real_sin], axis=1)


def apply_kernel(spectrum, widened, replicas):
    shaped = spectrum.reshape((replicas, 3) + spectrum.shape[1:])
    comp_one, comp_two, comp_three = (shaped[:, 0], shaped[:, 1], shaped[:, 2])
    result = [
        -(widened[0] * comp_one + widened[3] * comp_two + widened[4] * comp_three),
        -(widened[3] * comp_one + widened[1] * comp_two + widened[5] * comp_three),
        -(widened[4] * comp_one + widened[5] * comp_two + widened[2] * comp_three),
    ]
    return jnp.stack(result, axis=1).reshape(spectrum.shape)


def advance(moment_field, local_field, noise_scale, noise_step):
    effective = local_field + noise_scale[:, None, None, None, None] * noise_step.astype(
        jnp.float32
    )
    torque = cross(moment_field, effective, 1)
    stepped = moment_field - TIME_STEP * (torque + DAMPING * cross(moment_field, torque, 1))
    return stepped * lax.rsqrt(jnp.sum(stepped * stepped, axis=1, keepdims=True))


def neighbor_sum(moment_field, bond_field):
    coupling_first = bond_field[0]
    carried = coupling_first * moment_field
    above = shifted(moment_field[:, :, :1], ("slab", "pen"), -1)
    below = shifted(carried[:, :, -1:], ("slab", "pen"), 1)
    upward = jnp.concatenate([moment_field[:, :, 1:], above], axis=2)
    downward = jnp.concatenate([below, carried[:, :, :-1]], axis=2)
    summed = coupling_first * upward + downward
    for grid_axis in (1, 2):
        coupling = bond_field[grid_axis]
        summed = (
            summed
            + coupling * jnp.roll(moment_field, -1, grid_axis + 2)
            + jnp.roll(coupling * moment_field, 1, grid_axis + 2)
        )
    return summed


def on_device(moments, couplings, noise, kernel, temps, order, accept):
    replicas = moments.shape[0]
    planes = moments.shape[2]
    grid_width = moments.shape[3]
    grid_depth = moments.shape[4]
    slab_count = lax.axis_size("slab")
    pen_count = lax.axis_size("pen")
    slices = slab_count * pen_count
    row_block = grid_width // slices
    channels = 3 * replicas
    low_count = grid_depth // 2
    cosine_depth, sine_depth = angle_tables(grid_depth)
    cosine_width, sine_width = angle_tables(grid_width)
    inverse_cosine = cosine_width / grid_width
    inverse_sine = sine_width / grid_width
    low_weights = jnp.where(jnp.arange(low_count) == 0, 1.0, 2.0).astype(jnp.float32)
    forward_lower = jnp.concatenate(
        [cosine_depth[:, :low_count], -sine_depth[:, :low_count]], axis=1
    )
    backward_lower = (
        jnp.concatenate(
            [
                low_weights[:, None] * cosine_depth[:low_count],
                -low_weights[:, None] * sine_depth[:low_count],
            ],
            axis=0,
        )
        / grid_depth
    )
    kernel_lower = jnp.concatenate([kernel[..., :low_count], kernel[..., :low_count]], axis=-1)
    edge_column = cosine_depth[:, low_count]
    edge_row = cosine_depth[low_count] / grid_depth
    edge_kernel = jnp.swapaxes(kernel[..., low_count], 1, 2)[:, None]
    bond_field = couplings.astype(jnp.float32)
    labels = pair_labels(order, accept)
    slot_index = jnp.arange(temps.shape[0], dtype=jnp.int32)
    offset = lax.axis_index("temp") * replicas
    own_slots = lax.dynamic_slice_in_dim(slot_index, offset, replicas)
    own_labels = lax.dynamic_slice_in_dim(labels, offset, replicas)
    scales = (slot_sigma(own_slots, temps), slot_sigma(own_labels, temps))
    moment_field = moments
    for step_index in range(2):
        flattened = moment_field.reshape(channels, planes, grid_width, grid_depth)
        dipole_lower_part = jnp.dot(flattened, forward_lower, precision=lax.Precision.HIGHEST)
        dipole_lower_part = twist(dipole_lower_part, cosine_width, sine_width, "cxyw,yk->cxkw", 1.0)
        edge = jnp.dot(flattened, edge_column, precision=lax.Precision.HIGHEST)
        edge_real = jnp.einsum("cxy,yk->ckx", edge, cosine_width, precision=lax.Precision.HIGHEST)
        edge_imag = -jnp.einsum("cxy,yk->ckx", edge, sine_width, precision=lax.Precision.HIGHEST)
        edge_edge_in = jnp.stack([edge_real, edge_imag], axis=1).reshape(
            channels, 2, slices, row_block, 1, planes
        )
        edge_edge_moved = lax.all_to_all(
            edge_edge_in, ("slab", "pen"), split_axis=2, concat_axis=4, tiled=True
        )
        dipole_edge_pair = edge_edge_moved.reshape(channels, 2, row_block, grid_width)
        lower_lower_in = dipole_lower_part.reshape(
            channels, 1, planes, slices, row_block, dipole_lower_part.shape[-1]
        )
        lower_lower_out = lax.all_to_all(
            lower_lower_in, ("slab", "pen"), split_axis=3, concat_axis=1, tiled=True
        )
        dipole_lower_part = lower_lower_out.reshape(
            channels, grid_width, row_block, dipole_lower_part.shape[-1]
        )
        dipole_edge_pair = pair_twist(
            dipole_edge_pair, cosine_width, sine_width, "cyx,xk->cyk", 1.0
        )
        dipole_edge_pair = apply_kernel(dipole_edge_pair, edge_kernel, replicas)
        dipole_edge_pair = pair_twist(
            dipole_edge_pair, inverse_cosine, inverse_sine, "cyx,xk->cyk", -1.0
        )
        dipole_lower_part = twist(dipole_lower_part, cosine_width, sine_width, "cxyw,xk->ckyw", 1.0)
        dipole_lower_part = apply_kernel(dipole_lower_part, kernel_lower, replicas)
        dipole_lower_part = twist(
            dipole_lower_part, inverse_cosine, inverse_sine, "cxyw,xk->ckyw", -1.0
        )
        edge_in = dipole_edge_pair.reshape(channels, 2, 1, row_block, slices, planes)
        edge_moved = lax.all_to_all(
            edge_in, ("slab", "pen"), split_axis=4, concat_axis=2, tiled=True
        )
        dipole_edge_pair = edge_moved.reshape(channels, 2, grid_width, planes)
        lower_in = dipole_lower_part.reshape(
            channels, slices, planes, 1, row_block, dipole_lower_part.shape[-1]
        )
        lower_out = lax.all_to_all(
            lower_in, ("slab", "pen"), split_axis=1, concat_axis=3, tiled=True
        )
        dipole_lower_part = lower_out.reshape(
            channels, planes, grid_width, dipole_lower_part.shape[-1]
        )
        dipole_lower_part = twist(
            dipole_lower_part, inverse_cosine, inverse_sine, "cxyw,yk->cxkw", -1.0
        )
        edge_field = jnp.einsum(
            "ckx,ky->cxy", dipole_edge_pair[:, 0], inverse_cosine, precision=lax.Precision.HIGHEST
        ) - jnp.einsum(
            "ckx,ky->cxy", dipole_edge_pair[:, 1], inverse_sine, precision=lax.Precision.HIGHEST
        )
        summed = (
            jnp.dot(dipole_lower_part, backward_lower, precision=lax.Precision.HIGHEST)
            + edge_field[..., None] * edge_row
        )
        local_field = neighbor_sum(moment_field, bond_field) + summed.reshape(moment_field.shape)
        moment_field = advance(moment_field, local_field, scales[step_index], noise[step_index])
    return (moment_field, labels)


def solution(mesh):
    return jax.shard_map(
        on_device,
        mesh=mesh,
        in_specs=(
            P(("groups", "temp"), None, ("slab", "pen"), None, None),
            P("groups", ("slab", "pen"), None, None),
            P(None, ("groups", "temp"), None, ("slab", "pen"), None, None),
            P(None, None, ("slab", "pen"), None),
            P(),
            P("groups"),
            P("groups"),
        ),
        out_specs=(P(("groups", "temp"), None, ("slab", "pen"), None, None), P("groups")),
        check_vma=False,
    )
```

profile of v0, /device:TPU:13, one launch (start us, length us, event | category | flops | bytes accessed | tf_op | source)
XLA Modules:
  0.0 361.3 jit_solution(16124733584084486758)
XLA Ops:
  6.0 6.6 %all-to-all-start.2 = ((f32[16,1,384]{2,1,0:T(1,128)}), f32[16,1,384]{2,1,0:T(1,128)S(1)}, u32[]{:S(2)}, u32[]{:S(2)}) async-start(f32[16,1,384]{2,1,0:T(1,128)} %reshape.743), calls=%async_computation.2 | async-start | bytes 49152 | tf_op jit(solution)/shard_map/all_to_all | solution.py:172
  32.0 5.0 %fusion.8 = f32[3,1,8,16,8,128]{5,4,3,2,0,1:T(8,128)} fusion(f32[3,8,128,64]{3,2,1,0:T(8,128)} %get-tuple-element.47, f32[3,8,128,64]{3,2,1,0:T(8,128)} %get-tuple-element.46, f32[128,3,8,128]{3,0,2,1:T(8,128)S(1)} %fusion.58), kind=kOutput, calls=%fused_computation.39 | convolution fusion | flops 604995584 | bytes 4718592 | tf_op jit(solution)/shard_map/cxyw,yk->cxkw/dot_general | solution.py:66
  42.9 18.9 %all-to-all-start = ((f32[3,1,8,16,8,128]{5,4,2,0,1,3:T(8,128)}), f32[3,1,8,16,8,128]{5,4,2,0,1,3:T(8,128)S(1)}, u32[]{:S(2)}, u32[]{:S(2)}) async-start(f32[3,1,8,16,8,128]{5,4,2,0,1,3:T(8,128)} %copy.268), calls=%async_computation | async-start | bytes 3145728 | tf_op jit(solution)/shard_map/all_to_all | solution.py:179
  79.4 18.5 %all-to-all-done = f32[3,1,8,16,8,128]{5,4,2,0,1,3:T(8,128)S(1)} async-done(((f32[3,1,8,16,8,128]{5,4,2,0,1,3:T(8,128)}), f32[3,1,8,16,8,128]{5,4,2,0,1,3:T(8,128)S(1)}, u32[]{:S(2)}, u32[]{:S(2)}) %all-to-all-start) | async-done | bytes 1572896 | tf_op jit(solution)/shard_map/all_to_all | solution.py:179
  97.8 4.9 %all-to-all-start.3 = ((f32[16,1,384]{2,1,0:T(1,128)}), f32[16,1,384]{2,1,0:T(1,128)S(1)}, u32[]{:S(2)}, u32[]{:S(2)}) async-start(f32[16,1,384]{2,1,0:T(1,128)} %reshape.745), calls=%async_computation.3 | async-start | bytes 49152 | tf_op jit(solution)/shard_map/all_to_all | solution.py:198
  104.1 3.1 copy.271
  107.3 4.2 %fusion.171 = f32[128,3072]{0,1} fusion(f32[128,3072]{0,1:T(8,128)} %bitcast.556), kind=kOutput, calls=%fused_computation.265 | convolution fusion | flops 604209152 | bytes 3145728
  111.4 3.1 copy.272
  136.7 6.2 %all-to-all-start.1 = ((f32[3,16,8,1,8,128]{5,4,2,0,3,1:T(8,128)}), f32[3,16,8,1,8,128]{5,4,2,0,3,1:T(8,128)S(1)}, u32[]{:S(2)}, u32[]{:S(2)}) async-start(f32[3,16,8,1,8,128]{5,4,2,0,3,1:T(8,128)} %copy.276), calls=%async_computation.1 | async-start | bytes 3145728 | tf_op jit(solution)/shard_map/all_to_all | solution.py:205
  166.8 12.2 %all-to-all-done.1 = f32[3,16,8,1,8,128]{5,4,2,0,3,1:T(8,128)S(1)} async-done(((f32[3,16,8,1,8,128]{5,4,2,0,3,1:T(8,128)}), f32[3,16,8,1,8,128]{5,4,2,0,3,1:T(8,128)S(1)}, u32[]{:S(2)}, u32[]{:S(2)}) %all-to-all-start.1) | async-done | bytes 1572896 | tf_op jit(solution)/shard_map/all_to_all | solution.py:205
  184.6 5.3 %fusion.7 = f32[1,3,8,128,128]{4,3,2,1,0:T(8,128)S(1)} fusion(f32[3,1,128,128]{3,2,1,0:T(8,128)} %bitcast.2, f32[3,7,128,128]{3,2,1,0:T(8,128)S(1)} %copy-done.33, f32[3,7,128,128]{3,2,1,0:T(8,128)} %slice_bitcast_fusion.13, f32[3,1,128,128]{3,2,1,0:T(8,128)} %bitcast.3, f32[3,8,1,128]{3,2,1,0:T(1,128)S(1)} %slice_bitcast_fusion.46, ...), kind=kOutput, calls=%fused_computation.35 | convolution fusion | flops 613056512 | bytes 16593412 | tf_op jit(solution)/shard_map/dot_general | solution.py:220
  200.7 4.9 %all-to-all-start.6 = ((f32[16,1,384]{2,1,0:T(1,128)}), f32[16,1,384]{2,1,0:T(1,128)S(1)}, u32[]{:S(2)}, u32[]{:S(2)}) async-start(f32[16,1,384]{2,1,0:T(1,128)} %reshape.747), calls=%async_computation.6 | async-start | bytes 49152 | tf_op jit(solution)/shard_map/all_to_all | solution.py:172
  213.6 6.0 %all-to-all-start.4 = ((f32[3,1,8,16,8,128]{5,4,2,0,1,3:T(8,128)}), f32[3,1,8,16,8,128]{5,4,2,0,1,3:T(8,128)}, u32[]{:S(2)}, u32[]{:S(2)}) async-start(f32[3,1,8,16,8,128]{5,4,2,0,1,3:T(8,128)} %copy.313), calls=%async_computation.4 | async-start | bytes 3145728 | tf_op jit(solution)/shard_map/all_to_all | solution.py:179
  240.7 17.4 %all-to-all-done.4 = f32[3,1,8,16,8,128]{5,4,2,0,1,3:T(8,128)} async-done(((f32[3,1,8,16,8,128]{5,4,2,0,1,3:T(8,128)}), f32[3,1,8,16,8,128]{5,4,2,0,1,3:T(8,128)}, u32[]{:S(2)}, u32[]{:S(2)}) %all-to-all-start.4) | async-done | bytes 1572896 | tf_op jit(solution)/shard_map/all_to_all | solution.py:179
  258.1 5.3 %all-to-all-start.7 = ((f32[16,1,384]{2,1,0:T(1,128)}), f32[16,1,384]{2,1,0:T(1,128)S(1)}, u32[]{:S(2)}, u32[]{:S(2)}) async-start(f32[16,1,384]{2,1,0:T(1,128)} %reshape.749), calls=%async_computation.7 | async-start | bytes 49152 | tf_op jit(solution)/shard_map/all_to_all | solution.py:198
  266.2 3.1 copy.316
  269.3 4.2 %fusion.168 = f32[128,3072]{0,1} fusion(f32[128,3072]{0,1:T(8,128)} %bitcast.560), kind=kOutput, calls=%fused_computation.264 | convolution fusion | flops 604209152 | bytes 3145728
  279.2 3.7 %fusion.28 = f32[1,3,128,8,128]{4,2,3,1,0:T(8,128)S(1)} fusion(f32[3,128,8,64]{3,1,2,0:T(8,128)S(1)} %get-tuple-element.35, f32[3,128,8,64]{3,1,2,0:T(8,128)S(1)} %get-tuple-element.34, f32[3,16,1,8,1,8,128]{6,5,3,0,1,4,2:T(8,128)} %bitcast.125), kind=kOutput, calls=%fused_computation.69 | convolution fusion | flops 604995584 | bytes 4718592 | tf_op jit(solution)/shard_map/cxyw,xk->ckyw/dot_general | solution.py:66
  289.3 4.2 %fusion.174 = f32[128,3072]{0,1} fusion(f32[128,3072]{0,1:T(8,128)} %bitcast.562), kind=kOutput, calls=%fused_computation.266 | convolution fusion | flops 604225536 | bytes 3145728
  303.5 6.2 %all-to-all-start.5 = ((f32[3,16,8,1,8,128]{5,4,2,0,3,1:T(8,128)}), f32[3,16,8,1,8,128]{5,4,2,0,3,1:T(8,128)}, u32[]{:S(2)}, u32[]{:S(2)}) async-start(f32[3,16,8,1,8,128]{5,4,2,0,3,1:T(8,128)} %copy.321), calls=%async_computation.5 | async-start | bytes 3145728 | tf_op jit(solution)/shard_map/all_to_all | solution.py:205
  329.1 16.9 %all-to-all-done.5 = f32[3,16,8,1,8,128]{5,4,2,0,3,1:T(8,128)} async-done(((f32[3,16,8,1,8,128]{5,4,2,0,3,1:T(8,128)}), f32[3,16,8,1,8,128]{5,4,2,0,3,1:T(8,128)}, u32[]{:S(2)}, u32[]{:S(2)}) %all-to-all-start.5) | async-done | bytes 1572896 | tf_op jit(solution)/shard_map/all_to_all | solution.py:205
  346.0 3.2 fusion.72
  349.9 3.4 fusion.40
  353.6 4.9 %fusion.26 = f32[1,3,8,128,128]{4,3,2,1,0:T(8,128)S(1)} fusion(f32[3,1,128,128]{3,2,1,0:T(8,128)} %bitcast.105, f32[3,7,128,128]{3,2,1,0:T(8,128)S(1)} %copy-done.31, f32[3,7,128,128]{3,2,1,0:T(8,128)S(1)} %copy-done.32, f32[3,1,128,128]{3,2,1,0:T(8,128)} %bitcast.107, f32[3,8,1,128]{3,2,1,0:T(1,128)S(1)} %slice_bitcast_fusion.36, ...), kind=kOutput, calls=%fused_computation.63 | convolution fusion | flops 613056512 | bytes 16593412 | tf_op jit(solution)/shard_map/dot_general | solution.py:220
  (325 shorter events, 186.3 us)
Async XLA Ops:
  0.9 62.4 %copy-start.53 = (f32[128,128]{0,1:T(8,128)}, f32[128,128]{0,1:T(8,128)S(1)}, u32[]{:S(2)}) copy-start(f32[128,128]{0,1:T(8,128)S(1)} %fusion.151) | copy-start | bytes 196612
  3.7 8.8 %copy-start = (f32[1,3,8,128,128]{4,3,2,1,0:T(8,128)S(1)}, f32[1,3,8,128,128]{4,3,2,1,0:T(8,128)}, u32[]{:S(2)}) copy-start(f32[1,3,8,128,128]{4,3,2,1,0:T(8,128)} %param.7) | copy-start | bytes 4718596
  4.2 9.4 %copy-start.55 = (bf16[3,8,128,128]{3,2,1,0:T(8,128)(2,1)S(1)}, bf16[3,8,128,128]{3,2,1,0:T(8,128)(2,1)}, u32[]{:S(2)}) copy-start(bf16[3,8,128,128]{3,2,1,0:T(8,128)(2,1)} %param.8) | copy-start | bytes 2359300
  6.0 36.9 %all-to-all-start.2 = ((f32[16,1,384]{2,1,0:T(1,128)}), f32[16,1,384]{2,1,0:T(1,128)S(1)}, u32[]{:S(2)}, u32[]{:S(2)}) async-start(f32[16,1,384]{2,1,0:T(1,128)} %reshape.743), calls=%async_computation.2 | async-start | bytes 49152 | tf_op jit(solution)/shard_map/all_to_all | solution.py:172
  13.2 169.9 %collective-permute-start = (f32[1,3,1,128,128]{4,3,1,2,0:T(8,128)}, f32[1,3,1,128,128]{4,3,1,2,0:T(8,128)}, u32[]{:S(2)}, u32[]{:S(2)}) collective-permute-start(f32[1,3,1,128,128]{4,3,1,2,0:T(8,128)} %slice_bitcast_fusion.26), channel_id=1, source_target_pairs={{1,0},{4,1},{5,4},{8,5},{9,8},{12,9},{13,12},{16,13},{17,16},{20,1... | collective-permute-start | bytes 589832 | tf_op jit(solution)/shard_map/ppermute | solution.py:15
  13.9 6.1 %copy-start.71 = (s32[2]{0:T(128)S(1)}, s32[2]{0:T(128)}, u32[]{:S(2)}) copy-start(s32[2]{0:T(128)} %param.12) | copy-start | bytes 28
  13.9 6.4 %copy-start.69 = (s32[2]{0:T(128)S(1)}, s32[2]{0:T(128)}, u32[]{:S(2)}) copy-start(s32[2]{0:T(128)} %param.13) | copy-start | bytes 28
  17.1 166.1 %collective-permute-start.1 = (f32[1,3,1,128,128]{4,3,1,2,0:T(8,128)}, f32[1,3,1,128,128]{4,3,1,2,0:T(8,128)}, u32[]{:S(2)}, u32[]{:S(2)}) collective-permute-start(f32[1,3,1,128,128]{4,3,1,2,0:T(8,128)} %slice_bitcast_fusion.25), channel_id=1, source_target_pairs={{29,0},{0,1},{1,4},{4,5},{5,8},{8,9},{9,12},{12,13},{13,16},{16,17... | collective-permute-start | bytes 589832 | tf_op jit(solution)/shard_map/ppermute | solution.py:15
  20.5 16.5 %copy-start.70 = (s32[2]{0:T(128)}, s32[2]{0:T(128)S(1)}, u32[]{:S(2)}) copy-start(s32[2]{0:T(128)S(1)} %compare_select_fusion.3) | copy-start | bytes 28
  42.9 55.0 %all-to-all-start = ((f32[3,1,8,16,8,128]{5,4,2,0,1,3:T(8,128)}), f32[3,1,8,16,8,128]{5,4,2,0,1,3:T(8,128)S(1)}, u32[]{:S(2)}, u32[]{:S(2)}) async-start(f32[3,1,8,16,8,128]{5,4,2,0,1,3:T(8,128)} %copy.268), calls=%async_computation | async-start | bytes 3145728 | tf_op jit(solution)/shard_map/all_to_all | solution.py:179
  97.8 38.9 %all-to-all-start.3 = ((f32[16,1,384]{2,1,0:T(1,128)}), f32[16,1,384]{2,1,0:T(1,128)S(1)}, u32[]{:S(2)}, u32[]{:S(2)}) async-start(f32[16,1,384]{2,1,0:T(1,128)} %reshape.745), calls=%async_computation.3 | async-start | bytes 49152 | tf_op jit(solution)/shard_map/all_to_all | solution.py:198
  136.7 6.2 %copy-start.68 = (f32[2]{0:T(128)S(1)}, f32[2]{0:T(128)}, u32[]{:S(2)}) copy-start(f32[2]{0:T(128)} %param.11) | copy-start | bytes 28
  136.7 42.3 %all-to-all-start.1 = ((f32[3,16,8,1,8,128]{5,4,2,0,3,1:T(8,128)}), f32[3,16,8,1,8,128]{5,4,2,0,3,1:T(8,128)S(1)}, u32[]{:S(2)}, u32[]{:S(2)}) async-start(f32[3,16,8,1,8,128]{5,4,2,0,3,1:T(8,128)} %copy.276), calls=%async_computation.1 | async-start | bytes 3145728 | tf_op jit(solution)/shard_map/all_to_all | solution.py:205
  200.7 12.9 %all-to-all-start.6 = ((f32[16,1,384]{2,1,0:T(1,128)}), f32[16,1,384]{2,1,0:T(1,128)S(1)}, u32[]{:S(2)}, u32[]{:S(2)}) async-start(f32[16,1,384]{2,1,0:T(1,128)} %reshape.747), calls=%async_computation.6 | async-start | bytes 49152 | tf_op jit(solution)/shard_map/all_to_all | solution.py:172
  213.6 44.5 %all-to-all-start.4 = ((f32[3,1,8,16,8,128]{5,4,2,0,1,3:T(8,128)}), f32[3,1,8,16,8,128]{5,4,2,0,1,3:T(8,128)}, u32[]{:S(2)}, u32[]{:S(2)}) async-start(f32[3,1,8,16,8,128]{5,4,2,0,1,3:T(8,128)} %copy.313), calls=%async_computation.4 | async-start | bytes 3145728 | tf_op jit(solution)/shard_map/all_to_all | solution.py:179
  220.3 133.0 %collective-permute-start.2 = (f32[1,3,1,128,128]{4,3,1,2,0:T(8,128)}, f32[1,3,1,128,128]{4,3,1,2,0:T(8,128)}, u32[]{:S(2)}, u32[]{:S(2)}) collective-permute-start(f32[1,3,1,128,128]{4,3,1,2,0:T(8,128)} %slice_bitcast_fusion.24), channel_id=1, source_target_pairs={{1,0},{4,1},{5,4},{8,5},{9,8},{12,9},{13,12},{16,13},{17,16},{20,1... | collective-permute-start | bytes 589832 | tf_op jit(solution)/shard_map/ppermute | solution.py:15
  222.3 131.0 %collective-permute-start.3 = (f32[1,3,1,128,128]{4,3,2,1,0:T(8,128)}, f32[1,3,1,128,128]{4,3,2,1,0:T(8,128)}, u32[]{:S(2)}, u32[]{:S(2)}) collective-permute-start(f32[1,3,1,128,128]{4,3,2,1,0:T(8,128)} %slice.513), channel_id=1, source_target_pairs={{29,0},{0,1},{1,4},{4,5},{5,8},{8,9},{9,12},{12,13},{13,16},{16,17... | collective-permute-start | bytes 589832 | tf_op jit(solution)/shard_map/ppermute | solution.py:15
  258.1 45.4 %all-to-all-start.7 = ((f32[16,1,384]{2,1,0:T(1,128)}), f32[16,1,384]{2,1,0:T(1,128)S(1)}, u32[]{:S(2)}, u32[]{:S(2)}) async-start(f32[16,1,384]{2,1,0:T(1,128)} %reshape.749), calls=%async_computation.7 | async-start | bytes 49152 | tf_op jit(solution)/shard_map/all_to_all | solution.py:198
  303.5 42.5 %all-to-all-start.5 = ((f32[3,16,8,1,8,128]{5,4,2,0,3,1:T(8,128)}), f32[3,16,8,1,8,128]{5,4,2,0,3,1:T(8,128)}, u32[]{:S(2)}, u32[]{:S(2)}) async-start(f32[3,16,8,1,8,128]{5,4,2,0,3,1:T(8,128)} %copy.321), calls=%async_computation.5 | async-start | bytes 3145728 | tf_op jit(solution)/shard_map/all_to_all | solution.py:205
  345.9 7.4 %copy-start.31 = (f32[3,7,128,128]{3,2,1,0:T(8,128)S(1)}, f32[3,7,128,128]{3,2,1,0:T(8,128)}, u32[]{:S(2)}) copy-start(f32[3,7,128,128]{3,2,1,0:T(8,128)} %slice_bitcast_fusion.12) | copy-start | bytes 4128772
  345.9 7.4 %copy-start.32 = (f32[3,7,128,128]{3,2,1,0:T(8,128)S(1)}, f32[3,7,128,128]{3,2,1,0:T(8,128)}, u32[]{:S(2)}) copy-start(f32[3,7,128,128]{3,2,1,0:T(8,128)} %slice_bitcast_fusion.11) | copy-start | bytes 4128772
  345.9 7.4 %copy-start.57 = (f32[64,128]{0,1:T(8,128)S(1)}, f32[64,128]{0,1:T(8,128)}, u32[]{:S(2)}) copy-start(f32[64,128]{0,1:T(8,128)} %get-tuple-element.66) | copy-start | bytes 98308
  346.0 7.4 %copy-start.59 = (f32[64,128]{0,1:T(8,128)S(1)}, f32[64,128]{0,1:T(8,128)}, u32[]{:S(2)}) copy-start(f32[64,128]{0,1:T(8,128)} %get-tuple-element.67) | copy-start | bytes 98308
  346.0 7.4 %copy-start.65 = (f32[3,8,1,128]{3,2,1,0:T(1,128)S(1)}, f32[3,8,1,128]{3,2,1,0:T(1,128)}, u32[]{:S(2)}) copy-start(f32[3,8,1,128]{3,2,1,0:T(1,128)} %slice_bitcast_fusion.35) | copy-start | bytes 36868
  (60 other events, 162.7 us)
where the time goes:
time: 367 us; the launch traced here: 361 us
  local copies, waits for them, and re-layouts  104 us (28%)
  matrix products  87.2 us (24%)
  waiting for transfers between devices  64.9 us (18%)
  starting transfers between devices  64.5 us (18%)
  other arithmetic  36.8 us (10%)
  between operations  3.87 us (1%)
    all_to_all x2, waiting for transfers between devices, on_device(): lax.all_to_all(lower_lower_in, ('slab', 'pen'), split_axis=3, concat_axis...  35.8 us
    all_to_all x2, waiting for transfers between devices, on_device(): lax.all_to_all(lower_in, ('slab', 'pen'), split_axis=1, concat_axis=3, ti...  29.1 us
    all_to_all x2, starting transfers between devices, on_device(): lax.all_to_all(lower_lower_in, ('slab', 'pen'), split_axis=3, concat_axis...  24.9 us
    unnamed x158, local copies, waits for them, and re-layouts  22.6 us
    dot_general x8, matrix products, twist(): jnp.einsum(pattern, packed, cosine_table, precision=lax.Precision.HIGHEST)  22.4 us
    unnamed x4, matrix products  15.5 us
    all_to_all x2, starting transfers between devices, on_device(): lax.all_to_all(lower_in, ('slab', 'pen'), split_axis=1, concat_axis=3, ti...  12.3 us
    slice x8, other arithmetic, twist(): sine_part[..., middle:]  12.3 us
  transfers between devices with their start and end apart: 12, of which 4 were waited for; matrix products, arithmetic and copies ran while one was open for 53% of the time, Pallas kernels for 0%

commit v1 on v0

--- a/solution.py
+++ b/solution.py
@@ -1,12 +1,18 @@
+import functools
 import math
 
 import jax
 import jax.numpy as jnp
 from jax import lax
+from jax.experimental import pallas as pl
+from jax.experimental.pallas import tpu as pltpu
 from jax.sharding import PartitionSpec as P
 
 TIME_STEP = 0.1
 DAMPING = 0.5
+AXES = ("slab", "pen")
+CHUNKS = 2
+VMEM_BYTES = 40 * 1024 * 1024
 
 
 def shifted(block, axis, distance):
@@ -118,7 +124,7 @@
     return summed
 
 
-def on_device(moments, couplings, noise, kernel, temps, order, accept):
+def plain_on_device(moments, couplings, noise, kernel, temps, order, accept):
     replicas = moments.shape[0]
     planes = moments.shape[2]
     grid_width = moments.shape[3]
@@ -225,6 +231,388 @@
     return (moment_field, labels)
 
 
+def split(value):
+    high = value.astype(jnp.bfloat16)
+    low = (value - high.astype(jnp.float32)).astype(jnp.bfloat16)
+    return high, low
+
+
+def stacked_parts(value):
+    high, low = split(value)
+    return jnp.concatenate([high, high, low], axis=0)
+
+
+def product(left, right):
+    return jnp.dot(left, right, preferred_element_type=jnp.float32)
+
+
+def table_parts(table):
+    high = lax.reduce_precision(table, 8, 7)
+    return jnp.concatenate([high, lax.reduce_precision(table - high, 8, 7), high], axis=1).astype(
+        jnp.bfloat16
+    )
+
+
+def turn(value):
+    return pltpu.roll(value, value.shape[-1] // 2, value.ndim - 1)
+
+
+def lane_index(shape):
+    return lax.broadcasted_iota(jnp.int32, shape, len(shape) - 1)
+
+
+def forward_kernel(field_ref, depth_ref, table_ref, mask_ref, *out_refs):
+    _, planes, width, depth = field_ref.shape
+    half = depth // 2
+    lane = lane_index((width, depth))
+    signs = jnp.where(lane == 0, 0.0, jnp.where(lane < half, 1.0, -1.0))
+    own = mask_ref[0]
+    other = mask_ref[1] > 0.5
+    part = table_ref.shape[0] // len(out_refs)
+    for component in range(3):
+        high, low = split(field_ref[component].reshape(planes * width, depth))
+        lines = product(jnp.concatenate([high, high, low], axis=1), depth_ref[...])
+        extra = jnp.zeros((width, depth), jnp.float32)
+        columns = []
+        for plane in range(planes):
+            line = lines[plane * width : (plane + 1) * width]
+            turned = turn(line)
+            moved = pltpu.roll(turned, plane, 1) if plane else turned
+            extra = jnp.where(lane == plane, moved, extra)
+            columns.append(stacked_parts(jnp.concatenate([line, turned * signs], axis=0)))
+        columns.append(stacked_parts(jnp.concatenate([extra, -turn(extra)], axis=0)))
+        mixed = product(table_ref[...], jnp.concatenate(columns, axis=1))
+        extra = mixed[:, planes * depth :]
+        for plane in range(planes):
+            value = mixed[:, plane * depth : (plane + 1) * depth]
+            value = value - own * pltpu.roll(extra, half - plane, 1)
+            back = pltpu.roll(extra, depth - plane, 1) if plane else extra
+            value = jnp.where(other, back, value)
+            for index, out_ref in enumerate(out_refs):
+                out_ref[component, pl.ds(plane, part, stride=planes), :] = value[
+                    index * part : (index + 1) * part
+                ]
+
+
+def middle_kernel(start, inner, kernel_ref, weight_ref, table_ref, inverse_ref, *refs):
+    in_refs, out_refs = refs[:inner], refs[inner:]
+    outer, _, rows, planes, depth = in_refs[0].shape
+    half = depth // 2
+    count = inner * outer * planes
+    row_block = kernel_ref.shape[1] // count
+    lane = lane_index((count, depth))
+    signs = jnp.where(lane < half, 1.0, -1.0)
+    order = ((0, 3, 4), (3, 1, 5), (4, 5, 2))
+    weights = [weight_ref[i : i + 1, :] for i in range(6)]
+    for row in range(rows):
+        spectrum, columns = [], []
+        edge = start + row == 0
+        for component in range(3):
+            block = jnp.concatenate(
+                [ref[:, component, row].reshape(outer * planes, depth) for ref in in_refs], axis=0
+            )
+            turned = turn(block)
+            columns.append(stacked_parts(jnp.concatenate([block, turned * signs], axis=0)))
+            if edge:
+                mirror = jnp.concatenate([block * signs, -turned], axis=0)
+                spectrum.append(stacked_parts(mirror))
+        mixed = product(table_ref[...], jnp.concatenate(columns + spectrum, axis=1))
+        spectrum = [mixed[:, i * depth : (i + 1) * depth] for i in range(mixed.shape[1] // depth)]
+        totals = [None] * 3
+        for entry in range(6):
+            raw = kernel_ref[entry, pl.ds(start + row, count, stride=row_block), :]
+            raw_turned = turn(raw)
+            pick = 2 if edge else 0
+            value = raw * weights[pick] + raw_turned * weights[pick + 1]
+            for i in range(3):
+                for j in range(3):
+                    if order[i][j] == entry:
+                        term = value * spectrum[j]
+                        totals[i] = term if totals[i] is None else totals[i] + term
+            if edge:
+                value = raw * weights[4] + raw_turned * weights[5]
+                for i in range(3):
+                    for j in range(3):
+                        if order[i][j] == entry:
+                            totals[i] = totals[i] + value * spectrum[3 + j]
+        columns = [
+            stacked_parts(jnp.concatenate([total, turn(total) * signs], axis=0)) for total in totals
+        ]
+        mixed = product(inverse_ref[...], jnp.concatenate(columns, axis=1))
+        for component in range(3):
+            value = mixed[:, component * depth : (component + 1) * depth]
+            for index, out_ref in enumerate(out_refs):
+                size = outer * planes
+                out_ref[:, component, row] = value[index * size : (index + 1) * size].reshape(
+                    outer, planes, depth
+                )
+
+
+def gathered_columns(component, in_refs, mask_ref, table_ref, planes):
+    part = in_refs[0].shape[1] // planes
+    columns = []
+    for plane in range(planes):
+        value = jnp.concatenate(
+            [ref[component, pl.ds(plane, part, stride=planes), :] for ref in in_refs], axis=0
+        )
+        turned = turn(value)
+        top = value * mask_ref[0] + turned * mask_ref[1]
+        bottom = value * mask_ref[2] + turned * mask_ref[3]
+        columns.append(stacked_parts(jnp.concatenate([top, bottom], axis=0)))
+    return product(table_ref[...], jnp.concatenate(columns, axis=1))
+
+
+def backward_kernel(table_ref, mask_ref, *refs):
+    in_refs, out_ref = refs[:-1], refs[-1]
+    _, planes, _, depth = out_ref.shape
+    for component in range(3):
+        mixed = gathered_columns(component, in_refs, mask_ref, table_ref, planes)
+        for plane in range(planes):
+            out_ref[component, plane] = mixed[:, plane * depth : (plane + 1) * depth]
+
+
+def cross_parts(left, right):
+    return [
+        left[1] * right[2] - left[2] * right[1],
+        left[2] * right[0] - left[0] * right[2],
+        left[0] * right[1] - left[1] * right[0],
+    ]
+
+
+def advance_kernel(table_ref, mask_ref, depth_ref, partial_ref, local_ref, field_ref, *refs):
+    in_refs, out_ref, dipole_ref = refs[:-2], refs[-2], refs[-1]
+    _, planes, width, depth = out_ref.shape
+    for component in range(3):
+        mixed = gathered_columns(component, in_refs, mask_ref, table_ref, planes)
+        lines = jnp.concatenate(
+            [
+                mixed[:, plane * depth : (plane + 1) * depth] + partial_ref[component, plane]
+                for plane in range(planes)
+            ],
+            axis=0,
+        )
+        high, low = split(lines)
+        field = product(jnp.concatenate([high, high, low], axis=1), depth_ref[...])
+        dipole_ref[component] = field.reshape(planes, width, depth)
+    for plane in range(planes):
+        moment = [field_ref[component, plane] for component in range(3)]
+        effective = [local_ref[c, plane] + dipole_ref[c, plane] for c in range(3)]
+        torque = cross_parts(moment, effective)
+        twice = cross_parts(moment, torque)
+        stepped = [moment[c] - TIME_STEP * (torque[c] + DAMPING * twice[c]) for c in range(3)]
+        scale = lax.rsqrt(
+            stepped[0] * stepped[0] + stepped[1] * stepped[1] + stepped[2] * stepped[2]
+        )
+        for component in range(3):
+            out_ref[component, plane] = stepped[component] * scale
+
+
+def local_kernel(scale_ref, field_ref, above_ref, below_ref, bond_ref, noise_ref, out_ref):
+    _, planes, width, depth = out_ref.shape
+    scale = scale_ref[0]
+    for plane in range(planes):
+        bonds = [bond_ref[d, plane].astype(jnp.float32) for d in range(3)]
+        if plane:
+            bond_before = bond_ref[0, plane - 1].astype(jnp.float32)
+        for component in range(3):
+            value = field_ref[component, plane]
+            upper = field_ref[component, plane + 1] if plane + 1 < planes else above_ref[component]
+            if plane:
+                lower = bond_before * field_ref[component, plane - 1]
+            else:
+                lower = below_ref[component]
+            total = bonds[0] * upper + lower
+            total = total + bonds[1] * pltpu.roll(value, width - 1, 0)
+            total = total + pltpu.roll(bonds[1] * value, 1, 0)
+            total = total + bonds[2] * pltpu.roll(value, depth - 1, 1)
+            total = total + pltpu.roll(bonds[2] * value, 1, 1)
+            out_ref[component, plane] = total + scale * noise_ref[component, plane].astype(
+                jnp.float32
+            )
+
+
+def call(kernel, outs, operands, flops, scratch=(), scalars=0):
+    whole = pl.BlockSpec(memory_space=pltpu.VMEM)
+    moved = sum(math.prod(a.shape) * a.dtype.itemsize for a in list(operands) + list(outs))
+    return pl.pallas_call(
+        kernel,
+        out_shape=list(outs),
+        in_specs=[pl.BlockSpec(memory_space=pltpu.SMEM)] * scalars
+        + [whole] * (len(operands) - scalars),
+        out_specs=[whole] * len(outs),
+        scratch_shapes=list(scratch),
+        cost_estimate=pl.CostEstimate(flops=flops, bytes_accessed=moved, transcendentals=0),
+        compiler_params=pltpu.CompilerParams(vmem_limit_bytes=VMEM_BYTES),
+    )(*operands)
+
+
+def angles(left, right, length):
+    product_of = left[:, None] * right[None, :] % length
+    angle = 2.0 * math.pi / length * product_of.astype(jnp.float32)
+    return jnp.cos(angle), jnp.sin(angle)
+
+
+def shape_of(*shape):
+    return jax.ShapeDtypeStruct(shape, jnp.float32)
+
+
+def on_device(moments, couplings, noise, kernel, temps, order, accept):
+    planes, width, depth = moments.shape[2:]
+    row_block = kernel.shape[2]
+    count = lax.axis_size("slab") * lax.axis_size("pen")
+    if planes % 8 or row_block % 8 or depth % 128 or count & (count - 1) or moments.shape[0] > 1:
+        return plain_on_device(moments, couplings, noise, kernel, temps, order, accept)
+    inner = 1 << ((count.bit_length() - 1) // 2)
+    outer = count // inner
+    half = depth // 2
+    rows = row_block // CHUNKS
+    me = lax.axis_index(AXES)
+    numbers = functools.partial(jnp.arange, dtype=jnp.int32)
+
+    def partner(outer_first):
+        near, far = numbers(inner), numbers(outer) * inner
+        pair = far[:, None] + near[None, :] if outer_first else far[None, :] + near[:, None]
+        return me ^ pair.reshape(-1)
+
+    def spread(block_index, size, start, step):
+        return (block_index[:, None] * step + start + numbers(size)[None, :]).reshape(-1)
+
+    lane = numbers(depth)[None, :]
+    lower_lane = lane < half
+    cosine, sine = angles(numbers(depth), numbers(half), depth)
+    middle = (1 - 2 * (numbers(depth) % 2)).astype(jnp.float32)[:, None]
+    into_depth = jnp.concatenate([cosine, middle, -sine[:, 1:]], axis=1)
+    weight = jnp.where((lane == 0) | (lane == half), 1.0, 2.0) / depth
+    out_of_depth = (into_depth * weight).T
+    into_depth = table_parts(into_depth.T).T
+    out_of_depth = table_parts(out_of_depth.T).T
+    into_width, out_of_width, into_masks, out_masks = [], [], [], []
+    for chunk in range(CHUNKS):
+        wave = spread(partner(True), rows, chunk * rows, row_block)
+        cosine, sine = angles(wave, numbers(width), width)
+        into_width.append(table_parts(jnp.concatenate([cosine, sine], axis=1)))
+        back = jnp.concatenate([cosine, sine], axis=0).T / width
+        out_of_width.append(table_parts(back))
+        wave = wave[:, None]
+        below = (wave > 0) & (wave < width // 2)
+        above = wave > width // 2
+        ends = (wave == 0) | (wave == width // 2)
+        pair = (lane == 0) | (lane == half)
+        into_masks.append(
+            jnp.stack([below & (lane == half), above & pair]).astype(jnp.float32)
+        )
+        zero, sign = jnp.zeros((wave.shape[0], depth)), jnp.where(lower_lane, -1.0, 1.0)
+        first, last = lane == 0, lane == half
+        out_masks.append(
+            jnp.stack(
+                [
+                    jnp.where(pair, jnp.where(ends, 1.0, jnp.where(below & first, 2.0, 0.0)), 1.0)
+                    + zero,
+                    jnp.where(above & last, 2.0, 0.0) + zero,
+                    jnp.where(above & last, -2.0, 0.0) + zero,
+                    jnp.where(pair, jnp.where(below & first, -2.0, 0.0), sign) + zero,
+                ]
+            )
+        )
+    cell = spread(partner(False), planes, 0, planes)
+    cosine, sine = angles(numbers(count * planes), cell, count * planes)
+    into_first = table_parts(jnp.concatenate([cosine, sine], axis=1))
+    out_of_first = table_parts(
+        jnp.concatenate([-cosine.T, sine.T], axis=1) / (count * planes)
+    )
+    lane = lane[0]
+    ends = (me == 0) | (me == count // 2)
+    upper = me >= count // 2
+    direct = jnp.where(lane == 0, ~upper, jnp.where(lane == half, upper, lane < half))
+    direct = direct.astype(jnp.float32)
+    pair = ends & ((lane == 0) | (lane == half))
+    both = jnp.where(pair, 0.5, 0.0)
+    flip = jnp.where(lane == 0, 1.0, -1.0) * both
+    kinds = [
+        direct,
+        1.0 - direct,
+        jnp.where(pair, 0.5, direct),
+        jnp.where(pair, 0.5, 1.0 - direct),
+        flip,
+        -flip,
+    ]
+    weights = jnp.stack(kinds)
+
+    labels = pair_labels(order, accept)
+    slot_index = jnp.arange(temps.shape[0], dtype=jnp.int32)
+    offset = lax.axis_index("temp")
+    own_slots = lax.dynamic_slice_in_dim(slot_index, offset, 1)
+    own_labels = lax.dynamic_slice_in_dim(labels, offset, 1)
+    scales = (slot_sigma(own_slots, temps), slot_sigma(own_labels, temps))
+
+    kernel_rows = kernel.reshape(6, width * row_block, depth)
+    field = moments[0]
+
+    def swap(block, distance):
+        if distance == 0:
+            return block
+        return lax.ppermute(block, AXES, [(i, i ^ distance) for i in range(count)])
+
+    flat = shape_of(3, inner * rows * planes, depth)
+    piled = shape_of(outer, 3, rows, planes, depth)
+    whole = shape_of(*field.shape)
+    far_order = sorted(range(outer), key=lambda i: -(i.bit_length()))
+    near_order = range(inner)
+
+    for step_index in range(2):
+        above = shifted(field[:, 0], AXES, -1)
+        below = shifted(couplings[0, -1].astype(jnp.float32) * field[:, -1], AXES, 1)
+        sums = None
+        for chunk in range(CHUNKS):
+            sent = call(
+                forward_kernel,
+                [flat] * outer,
+                [field, into_depth, into_width[chunk], into_masks[chunk]],
+                200_000_000,
+            )
+            arrived = [None] * outer
+            for far in far_order:
+                arrived[far] = swap(sent[far], far * inner)
+            arrived = [a.reshape(3, inner, rows, planes, depth) for a in arrived]
+            spectra = [
+                swap(jnp.stack([a[:, near] for a in arrived]), near) for near in near_order
+            ]
+            spectra = call(
+                functools.partial(middle_kernel, chunk * rows, inner),
+                [piled] * inner,
+                [kernel_rows, weights, into_first, out_of_first]
+                + spectra,
+                400_000_000,
+            )
+            spectra = [swap(spectra[near], near) for near in near_order]
+            returned = [None] * outer
+            for far in far_order:
+                block = jnp.stack([s[far] for s in spectra], axis=1).reshape(flat.shape)
+                returned[far] = swap(block, far * inner)
+            if chunk == 0:
+                (sums,) = call(
+                    backward_kernel,
+                    [whole],
+                    [out_of_width[chunk], out_masks[chunk]] + returned,
+                    200_000_000,
+                )
+        (local,) = call(
+            local_kernel,
+            [whole],
+            [scales[step_index], field, above, below, couplings, noise[step_index, 0]],
+            20_000_000,
+            scalars=1,
+        )
+        (field,) = call(
+            advance_kernel,
+            [whole],
+            [out_of_width[-1], out_masks[-1], out_of_depth, sums, local, field] + returned,
+            300_000_000,
+            scratch=[pltpu.VMEM(whole.shape, jnp.float32)],
+        )
+    return (field[None], labels)
+
+
 def solution(mesh):
     return jax.shard_map(
         on_device,

time: 367 us -> 229 us (0.62)
  the two profiles are of different devices: /device:TPU:13 before, /device:TPU:0 now
where the time goes in v1:
time: 229 us; the launch traced here: 227 us
  waiting for transfers between devices  103 us (45%)
  starting transfers between devices  61 us (27%)
  Pallas kernels  30.7 us (13%)
  other arithmetic  14.9 us (7%)
  local copies, waits for them, and re-layouts  13.6 us (6%)
  between operations  3.47 us (2%)
    ppermute x48, waiting for transfers between devices, swap(): return lax.ppermute(block, AXES, [(i, i ^ distance) for i in range(count)])  103 us
    ppermute x48, starting transfers between devices, swap(): return lax.ppermute(block, AXES, [(i, i ^ distance) for i in range(count)])  54.4 us
    pallas_call x14, Pallas kernels, call(): pl.pallas_call(kernel, out_shape=list(outs), in_specs=[pl.BlockSpec(memor...  30.7 us
    ppermute x4, starting transfers between devices, shifted(): return lax.ppermute(block, axis, route)  6.54 us
    another operation x16, local copies, waits for them, and re-layouts, on_device(): jnp.stack([a[:, near] for a in arrived])  6.26 us
  transfers between devices with their start and end apart: 52, of which 25 were waited for; matrix products, arithmetic and copies ran while one was open for 11% of the time, Pallas kernels for 7%

profile of v1, /device:TPU:0, one launch (start us, length us, event | category | flops | bytes accessed | tf_op | source)
XLA Modules:
  0.0 226.9 jit_solution(1722283406035553564)
XLA Ops:
  4.1 3.3 %shard_map.86 = (f32[3,128,128]{2,1,0:T(8,128)S(1)}, f32[3,128,128]{2,1,0:T(8,128)}, f32[3,128,128]{2,1,0:T(8,128)}, f32[3,128,128]{2,1,0:T(8,128)}) custom-call(f32[3,8,128,128]{3,2,1,0:T(8,128)S(1)} %bitcast.471, bf16[384,128]{1,0:T(8,128)(2,1)S(1)} %copy.137.depth_ref, bf16[64,768]{1,0:T(8,128)(2,1)S(1)} %copy.138.table_ref, ...), custom_call_target="tpu_custom_call" | custom-call | flops 200000000 | bytes 2621440 | tf_op jit(solution)/shard_map/pallas_call | solution.py:437
  7.4 3.0 %collective-permute-start = (f32[3,128,128]{2,1,0:T(8,128)}, f32[3,128,128]{2,1,0:T(8,128)}, u32[]{:S(2)}, u32[]{:S(2)}) collective-permute-start(f32[3,128,128]{2,1,0:T(8,128)} %get-tuple-element.35), channel_id=1, source_target_pairs={{0,8},{1,9},{4,12},{5,13},{8,0},{9,1},{12,4},{13,5},{16,24},{17,25... | collective-permute-start | bytes 589832 | tf_op jit(solution)/shard_map/ppermute | solution.py:554
  13.6 3.3 %shard_map.90 = (f32[3,128,128]{2,1,0:T(8,128)S(1)}, f32[3,128,128]{2,1,0:T(8,128)}, f32[3,128,128]{2,1,0:T(8,128)}, f32[3,128,128]{2,1,0:T(8,128)S(1)}) custom-call(f32[3,8,128,128]{3,2,1,0:T(8,128)S(1)} %bitcast.472, bf16[384,128]{1,0:T(8,128)(2,1)S(1)} %copy.137.depth_ref, bf16[64,768]{1,0:T(8,128)(2,1)S(1)} %copy.162.table_ref, ...), custom_call_target="tpu_custom_call" | custom-call | flops 200000000 | bytes 2621440 | tf_op jit(solution)/shard_map/pallas_call | solution.py:437
  17.8 3.5 %collective-permute-start.15 = (f32[3,128,128]{2,1,0:T(8,128)}, f32[3,128,128]{2,1,0:T(8,128)}, u32[]{:S(2)}, u32[]{:S(2)}) collective-permute-start(f32[3,128,128]{2,1,0:T(8,128)} %get-tuple-element.44), channel_id=1, source_target_pairs={{0,16},{1,17},{4,20},{5,21},{8,24},{9,25},{12,28},{13,29},{16,0},{... | collective-permute-start | bytes 589832 | tf_op jit(solution)/shard_map/ppermute | solution.py:554
  43.9 4.6 %collective-permute-start.12 = (f32[3,128,128]{2,1,0:T(8,128)}, f32[3,128,128]{2,1,0:T(8,128)S(1)}, u32[]{:S(2)}, u32[]{:S(2)}) collective-permute-start(f32[3,128,128]{2,1,0:T(8,128)} %slice_bitcast_fusion.5), channel_id=1, source_target_pairs={{1,0},{4,1},{5,4},{8,5},{9,8},{12,9},{13,12},{16,13},{17,16},{20,1... | collective-permute-start | bytes 589832 | tf_op jit(solution)/shard_map/ppermute | solution.py:21
  58.4 3.3 %collective-permute-done.5.refs_3_ = f32[4,3,4,8,128]{4,3,2,1,0:T(8,128)S(1)} collective-permute-done((f32[4,3,4,8,128]{4,3,2,1,0:T(8,128)S(1)}, f32[4,3,4,8,128]{4,3,2,1,0:T(8,128)S(1)}, u32[]{:S(2)}, u32[]{:S(2)}) %collective-permute-start.5) | collective-permute-done | bytes 196640 | tf_op jit(solution)/shard_map/ppermute | solution.py:554
  66.9 3.3 %collective-permute-done.19.refs_3_ = f32[4,3,4,8,128]{4,3,2,1,0:T(8,128)S(1)} collective-permute-done((f32[4,3,4,8,128]{4,3,2,1,0:T(8,128)S(1)}, f32[4,3,4,8,128]{4,3,2,1,0:T(8,128)S(1)}, u32[]{:S(2)}, u32[]{:S(2)}) %collective-permute-start.19) | collective-permute-done | bytes 196640 | tf_op jit(solution)/shard_map/ppermute | solution.py:554
  75.3 3.2 %collective-permute-done.8 = f32[4,3,4,8,128]{4,3,2,1,0:T(8,128)S(1)} collective-permute-done((f32[4,3,4,8,128]{4,3,2,1,0:T(8,128)S(1)}, f32[4,3,4,8,128]{4,3,2,1,0:T(8,128)S(1)}, u32[]{:S(2)}, u32[]{:S(2)}) %collective-permute-start.8) | collective-permute-done | bytes 196640 | tf_op jit(solution)/shard_map/ppermute | solution.py:554
  78.8 2.8 %collective-permute-start.10 = (f32[3,128,128]{2,1,0:T(8,128)S(1)}, f32[3,128,128]{2,1,0:T(8,128)S(1)}, u32[]{:S(2)}, u32[]{:S(2)}) collective-permute-start(f32[3,128,128]{2,1,0:T(8,128)S(1)} %bitcast.490), channel_id=1, source_target_pairs={{0,16},{1,17},{4,20},{5,21},{8,24},{9,25},{12,28},{13,29},{16,0},{... | collective-permute-start | bytes 589832 | tf_op jit(solution)/shard_map/ppermute | solution.py:554
  83.7 3.2 %collective-permute-done.22 = f32[4,3,4,8,128]{4,3,2,1,0:T(8,128)S(1)} collective-permute-done((f32[4,3,4,8,128]{4,3,2,1,0:T(8,128)S(1)}, f32[4,3,4,8,128]{4,3,2,1,0:T(8,128)S(1)}, u32[]{:S(2)}, u32[]{:S(2)}) %collective-permute-start.22) | collective-permute-done | bytes 196640 | tf_op jit(solution)/shard_map/ppermute | solution.py:554
  87.2 2.8 %collective-permute-start.24 = (f32[3,128,128]{2,1,0:T(8,128)S(1)}, f32[3,128,128]{2,1,0:T(8,128)S(1)}, u32[]{:S(2)}, u32[]{:S(2)}) collective-permute-start(f32[3,128,128]{2,1,0:T(8,128)S(1)} %bitcast.494), channel_id=1, source_target_pairs={{0,16},{1,17},{4,20},{5,21},{8,24},{9,25},{12,28},{13,29},{16,0},{... | collective-permute-start | bytes 589832 | tf_op jit(solution)/shard_map/ppermute | solution.py:554
  91.7 4.3 %collective-permute-done.10.refs_2_ = f32[3,128,128]{2,1,0:T(8,128)S(1)} collective-permute-done((f32[3,128,128]{2,1,0:T(8,128)S(1)}, f32[3,128,128]{2,1,0:T(8,128)S(1)}, u32[]{:S(2)}, u32[]{:S(2)}) %collective-permute-start.10) | collective-permute-done | bytes 196640 | tf_op jit(solution)/shard_map/ppermute | solution.py:554
  99.3 13.6 %collective-permute-done.24.refs_2_ = f32[3,128,128]{2,1,0:T(8,128)S(1)} collective-permute-done((f32[3,128,128]{2,1,0:T(8,128)S(1)}, f32[3,128,128]{2,1,0:T(8,128)S(1)}, u32[]{:S(2)}, u32[]{:S(2)}) %collective-permute-start.24) | collective-permute-done | bytes 196640 | tf_op jit(solution)/shard_map/ppermute | solution.py:554
  115.3 2.8 %shard_map.97 = (f32[3,128,128]{2,1,0:T(8,128)S(1)}, f32[3,128,128]{2,1,0:T(8,128)S(1)}, f32[3,128,128]{2,1,0:T(8,128)S(1)}, f32[3,128,128]{2,1,0:T(8,128)S(1)}) custom-call(f32[3,8,128,128]{3,2,1,0:T(8,128)S(1)} %shard_map.92.field_ref, bf16[384,128]{1,0:T(8,128)(2,1)S(1)} %copy-done.5, bf16[64,768]{1,0:T(8,128)(2,1)S(1)} %copy-done.14, ...), custom_call_target="tpu_custom_call" | custom-call | flops 200000000 | bytes 2621440 | tf_op jit(solution)/shard_map/pallas_call | solution.py:437
  122.5 3.4 %collective-permute-start.40 = (f32[3,128,128]{2,1,0:T(8,128)S(1)}, f32[3,128,128]{2,1,0:T(8,128)S(1)}, u32[]{:S(2)}, u32[]{:S(2)}) collective-permute-start(f32[3,128,128]{2,1,0:T(8,128)S(1)} %get-tuple-element.59), channel_id=1, source_target_pairs={{0,8},{1,9},{4,12},{5,13},{8,0},{9,1},{12,4},{13,5},{16,24},{17,25... | collective-permute-start | bytes 589832 | tf_op jit(solution)/shard_map/ppermute | solution.py:554
  128.4 9.0 %collective-permute-done.40 = f32[3,128,128]{2,1,0:T(8,128)S(1)} collective-permute-done((f32[3,128,128]{2,1,0:T(8,128)S(1)}, f32[3,128,128]{2,1,0:T(8,128)S(1)}, u32[]{:S(2)}, u32[]{:S(2)}) %collective-permute-start.40) | collective-permute-done | bytes 196640 | tf_op jit(solution)/shard_map/ppermute | solution.py:554
  138.7 6.1 %collective-permute-done.42 = f32[3,128,128]{2,1,0:T(8,128)S(1)} collective-permute-done((f32[3,128,128]{2,1,0:T(8,128)S(1)}, f32[3,128,128]{2,1,0:T(8,128)S(1)}, u32[]{:S(2)}, u32[]{:S(2)}) %collective-permute-start.42) | collective-permute-done | bytes 196640 | tf_op jit(solution)/shard_map/ppermute | solution.py:554
  147.2 12.7 %collective-permute-done.27 = f32[3,128,128]{2,1,0:T(8,128)S(1)} collective-permute-done((f32[3,128,128]{2,1,0:T(8,128)S(1)}, f32[3,128,128]{2,1,0:T(8,128)S(1)}, u32[]{:S(2)}, u32[]{:S(2)}) %collective-permute-start.27) | collective-permute-done | bytes 196640 | tf_op jit(solution)/shard_map/ppermute | solution.py:554
  167.7 2.9 %collective-permute-done.45.refs_3_ = f32[4,3,4,8,128]{4,3,2,1,0:T(8,128)S(1)} collective-permute-done((f32[4,3,4,8,128]{4,3,2,1,0:T(8,128)S(1)}, f32[4,3,4,8,128]{4,3,2,1,0:T(8,128)S(1)}, u32[]{:S(2)}, u32[]{:S(2)}) %collective-permute-start.45) | collective-permute-done | bytes 196640 | tf_op jit(solution)/shard_map/ppermute | solution.py:554
  176.1 2.9 %collective-permute-done.31.refs_3_ = f32[4,3,4,8,128]{4,3,2,1,0:T(8,128)S(1)} collective-permute-done((f32[4,3,4,8,128]{4,3,2,1,0:T(8,128)S(1)}, f32[4,3,4,8,128]{4,3,2,1,0:T(8,128)S(1)}, u32[]{:S(2)}, u32[]{:S(2)}) %collective-permute-start.31) | collective-permute-done | bytes 196640 | tf_op jit(solution)/shard_map/ppermute | solution.py:554
  184.6 2.9 %collective-permute-done.48 = f32[4,3,4,8,128]{4,3,2,1,0:T(8,128)S(1)} collective-permute-done((f32[4,3,4,8,128]{4,3,2,1,0:T(8,128)S(1)}, f32[4,3,4,8,128]{4,3,2,1,0:T(8,128)S(1)}, u32[]{:S(2)}, u32[]{:S(2)}) %collective-permute-start.48) | collective-permute-done | bytes 196640 | tf_op jit(solution)/shard_map/ppermute | solution.py:554
  198.4 9.5 %collective-permute-done.35.refs_1_ = f32[3,128,128]{2,1,0:T(8,128)S(1)} collective-permute-done((f32[3,128,128]{2,1,0:T(8,128)S(1)}, f32[3,128,128]{2,1,0:T(8,128)S(1)}, u32[]{:S(2)}, u32[]{:S(2)}) %collective-permute-start.35) | collective-permute-done | bytes 196640 | tf_op jit(solution)/shard_map/ppermute | solution.py:554
  210.4 12.2 %collective-permute-done.36.refs_2_ = f32[3,128,128]{2,1,0:T(8,128)S(1)} collective-permute-done((f32[3,128,128]{2,1,0:T(8,128)S(1)}, f32[3,128,128]{2,1,0:T(8,128)S(1)}, u32[]{:S(2)}, u32[]{:S(2)}) %collective-permute-start.36) | collective-permute-done | bytes 196640 | tf_op jit(solution)/shard_map/ppermute | solution.py:554
  223.5 3.4 %shard_map.99 = f32[3,8,128,128]{3,2,1,0:T(8,128)} custom-call(bf16[128,384]{1,0:T(8,128)(2,1)S(1)} %copy-done.9, f32[4,64,128]{2,1,0:T(8,128)S(1)} %copy-done.6, bf16[384,128]{1,0:T(8,128)(2,1)S(1)} %copy-done.8, f32[3,8,128,128]{3,2,1,0:T(8,128)S(1)} %shard_map.95.partial_ref, f32[3,8,128,128]{3,2,1,0:T(8,128)S(1)} %shard_map.96.local_ref, ...), custom_call_target="tpu_custom_call" | custom-call | flops 300000000 | bytes 7405568 | tf_op jit(solution)/shard_map/pallas_call | solution.py:437
  (335 shorter events, 101.5 us)
Async XLA Ops:
  7.4 34.5 %collective-permute-start = (f32[3,128,128]{2,1,0:T(8,128)}, f32[3,128,128]{2,1,0:T(8,128)}, u32[]{:S(2)}, u32[]{:S(2)}) collective-permute-start(f32[3,128,128]{2,1,0:T(8,128)} %get-tuple-element.35), channel_id=1, source_target_pairs={{0,8},{1,9},{4,12},{5,13},{8,0},{9,1},{12,4},{13,5},{16,24},{17,25... | collective-permute-start | bytes 589832 | tf_op jit(solution)/shard_map/ppermute | solution.py:554
  10.4 32.5 %collective-permute-start.1 = (f32[3,128,128]{2,1,0:T(8,128)}, f32[3,128,128]{2,1,0:T(8,128)}, u32[]{:S(2)}, u32[]{:S(2)}) collective-permute-start(f32[3,128,128]{2,1,0:T(8,128)} %get-tuple-element.36), channel_id=1, source_target_pairs={{0,16},{1,17},{4,20},{5,21},{8,24},{9,25},{12,28},{13,29},{16,0},{... | collective-permute-start | bytes 589832 | tf_op jit(solution)/shard_map/ppermute | solution.py:554
  13.0 30.9 %collective-permute-start.2 = (f32[3,128,128]{2,1,0:T(8,128)}, f32[3,128,128]{2,1,0:T(8,128)}, u32[]{:S(2)}, u32[]{:S(2)}) collective-permute-start(f32[3,128,128]{2,1,0:T(8,128)} %get-tuple-element.37), channel_id=1, source_target_pairs={{0,24},{1,25},{4,28},{5,29},{8,16},{9,17},{12,20},{13,21},{16,8},{... | collective-permute-start | bytes 589832 | tf_op jit(solution)/shard_map/ppermute | solution.py:554
  16.9 32.7 %collective-permute-start.14 = (f32[3,128,128]{2,1,0:T(8,128)}, f32[3,128,128]{2,1,0:T(8,128)}, u32[]{:S(2)}, u32[]{:S(2)}) collective-permute-start(f32[3,128,128]{2,1,0:T(8,128)} %get-tuple-element.43), channel_id=1, source_target_pairs={{0,8},{1,9},{4,12},{5,13},{8,0},{9,1},{12,4},{13,5},{16,24},{17,25... | collective-permute-start | bytes 589832 | tf_op jit(solution)/shard_map/ppermute | solution.py:554
  17.8 32.8 %collective-permute-start.15 = (f32[3,128,128]{2,1,0:T(8,128)}, f32[3,128,128]{2,1,0:T(8,128)}, u32[]{:S(2)}, u32[]{:S(2)}) collective-permute-start(f32[3,128,128]{2,1,0:T(8,128)} %get-tuple-element.44), channel_id=1, source_target_pairs={{0,16},{1,17},{4,20},{5,21},{8,24},{9,25},{12,28},{13,29},{16,0},{... | collective-permute-start | bytes 589832 | tf_op jit(solution)/shard_map/ppermute | solution.py:554
  55.4 14.7 %collective-permute-start.19 = (f32[4,3,4,8,128]{4,3,2,1,0:T(8,128)S(1)}, f32[4,3,4,8,128]{4,3,2,1,0:T(8,128)S(1)}, u32[]{:S(2)}, u32[]{:S(2)}) collective-permute-start(f32[4,3,4,8,128]{4,3,2,1,0:T(8,128)S(1)} %pad_maximum_fusion.15), channel_id=1, source_target_pairs={{0,5},{1,4},{4,1},{5,0},{8,13},{9,12},{12,9},{13,8},{16,21},{17,20... | collective-permute-start | bytes 589832 | tf_op jit(solution)/shard_map/ppermute | solution.py:554
  78.8 17.3 %collective-permute-start.10 = (f32[3,128,128]{2,1,0:T(8,128)S(1)}, f32[3,128,128]{2,1,0:T(8,128)S(1)}, u32[]{:S(2)}, u32[]{:S(2)}) collective-permute-start(f32[3,128,128]{2,1,0:T(8,128)S(1)} %bitcast.490), channel_id=1, source_target_pairs={{0,16},{1,17},{4,20},{5,21},{8,24},{9,25},{12,28},{13,29},{16,0},{... | collective-permute-start | bytes 589832 | tf_op jit(solution)/shard_map/ppermute | solution.py:554
  81.6 14.5 %collective-permute-start.11 = (f32[3,128,128]{2,1,0:T(8,128)S(1)}, f32[3,128,128]{2,1,0:T(8,128)S(1)}, u32[]{:S(2)}, u32[]{:S(2)}) collective-permute-start(f32[3,128,128]{2,1,0:T(8,128)S(1)} %bitcast.488), channel_id=1, source_target_pairs={{0,24},{1,25},{4,28},{5,29},{8,16},{9,17},{12,20},{13,21},{16,8},{... | collective-permute-start | bytes 589832 | tf_op jit(solution)/shard_map/ppermute | solution.py:554
  87.2 25.7 %collective-permute-start.24 = (f32[3,128,128]{2,1,0:T(8,128)S(1)}, f32[3,128,128]{2,1,0:T(8,128)S(1)}, u32[]{:S(2)}, u32[]{:S(2)}) collective-permute-start(f32[3,128,128]{2,1,0:T(8,128)S(1)} %bitcast.494), channel_id=1, source_target_pairs={{0,16},{1,17},{4,20},{5,21},{8,24},{9,25},{12,28},{13,29},{16,0},{... | collective-permute-start | bytes 589832 | tf_op jit(solution)/shard_map/ppermute | solution.py:554
  90.0 22.9 %collective-permute-start.25 = (f32[3,128,128]{2,1,0:T(8,128)S(1)}, f32[3,128,128]{2,1,0:T(8,128)S(1)}, u32[]{:S(2)}, u32[]{:S(2)}) collective-permute-start(f32[3,128,128]{2,1,0:T(8,128)S(1)} %bitcast.492), channel_id=1, source_target_pairs={{0,24},{1,25},{4,28},{5,29},{8,16},{9,17},{12,20},{13,21},{16,8},{... | collective-permute-start | bytes 589832 | tf_op jit(solution)/shard_map/ppermute | solution.py:554
  120.7 40.7 %collective-permute-start.38 = (f32[3,128,128]{2,1,0:T(8,128)S(1)}, f32[3,128,128]{2,1,0:T(8,128)S(1)}, u32[]{:S(2)}, u32[]{:S(2)}) collective-permute-start(f32[3,128,128]{2,1,0:T(8,128)S(1)} %slice_bitcast_fusion.3), channel_id=1, source_target_pairs={{1,0},{4,1},{5,4},{8,5},{9,8},{12,9},{13,12},{16,13},{17,16},{20,1... | collective-permute-start | bytes 589832 | tf_op jit(solution)/shard_map/ppermute | solution.py:21
  122.5 39.8 %collective-permute-start.39 = (f32[3,128,128]{2,1,0:T(8,128)S(1)}, f32[3,128,128]{2,1,0:T(8,128)S(1)}, u32[]{:S(2)}, u32[]{:S(2)}) collective-permute-start(f32[3,128,128]{2,1,0:T(8,128)S(1)} %fusion), channel_id=1, source_target_pairs={{29,0},{0,1},{1,4},{4,5},{5,8},{8,9},{9,12},{12,13},{13,16},{16,17... | collective-permute-start | bytes 589832 | tf_op jit(solution)/shard_map/ppermute | solution.py:21
  122.5 14.9 %collective-permute-start.40 = (f32[3,128,128]{2,1,0:T(8,128)S(1)}, f32[3,128,128]{2,1,0:T(8,128)S(1)}, u32[]{:S(2)}, u32[]{:S(2)}) collective-permute-start(f32[3,128,128]{2,1,0:T(8,128)S(1)} %get-tuple-element.59), channel_id=1, source_target_pairs={{0,8},{1,9},{4,12},{5,13},{8,0},{9,1},{12,4},{13,5},{16,24},{17,25... | collective-permute-start | bytes 589832 | tf_op jit(solution)/shard_map/ppermute | solution.py:554
  127.9 16.8 %collective-permute-start.42 = (f32[3,128,128]{2,1,0:T(8,128)S(1)}, f32[3,128,128]{2,1,0:T(8,128)S(1)}, u32[]{:S(2)}, u32[]{:S(2)}) collective-permute-start(f32[3,128,128]{2,1,0:T(8,128)S(1)} %get-tuple-element.61), channel_id=1, source_target_pairs={{0,24},{1,25},{4,28},{5,29},{8,16},{9,17},{12,20},{13,21},{16,8},{... | collective-permute-start | bytes 589832 | tf_op jit(solution)/shard_map/ppermute | solution.py:554
  137.4 22.5 %collective-permute-start.27 = (f32[3,128,128]{2,1,0:T(8,128)S(1)}, f32[3,128,128]{2,1,0:T(8,128)S(1)}, u32[]{:S(2)}, u32[]{:S(2)}) collective-permute-start(f32[3,128,128]{2,1,0:T(8,128)S(1)} %get-tuple-element.52), channel_id=1, source_target_pairs={{0,16},{1,17},{4,20},{5,21},{8,24},{9,25},{12,28},{13,29},{16,0},{... | collective-permute-start | bytes 589832 | tf_op jit(solution)/shard_map/ppermute | solution.py:554
  144.8 16.3 %collective-permute-start.28 = (f32[3,128,128]{2,1,0:T(8,128)S(1)}, f32[3,128,128]{2,1,0:T(8,128)S(1)}, u32[]{:S(2)}, u32[]{:S(2)}) collective-permute-start(f32[3,128,128]{2,1,0:T(8,128)S(1)} %get-tuple-element.53), channel_id=1, source_target_pairs={{0,24},{1,25},{4,28},{5,29},{8,16},{9,17},{12,20},{13,21},{16,8},{... | collective-permute-start | bytes 589832 | tf_op jit(solution)/shard_map/ppermute | solution.py:554
  147.2 17.8 %collective-permute-start.43 = (f32[4,3,4,8,128]{4,3,2,1,0:T(8,128)S(1)}, f32[4,3,4,8,128]{4,3,2,1,0:T(8,128)S(1)}, u32[]{:S(2)}, u32[]{:S(2)}) collective-permute-start(f32[4,3,4,8,128]{4,3,2,1,0:T(8,128)S(1)} %pad_maximum_fusion.29), channel_id=1, source_target_pairs={{0,1},{1,0},{4,5},{5,4},{8,9},{9,8},{12,13},{13,12},{16,17},{17,16... | collective-permute-start | bytes 589832 | tf_op jit(solution)/shard_map/ppermute | solution.py:554
  162.3 13.8 %collective-permute-start.30 = (f32[4,3,4,8,128]{4,3,2,1,0:T(8,128)S(1)}, f32[4,3,4,8,128]{4,3,2,1,0:T(8,128)S(1)}, u32[]{:S(2)}, u32[]{:S(2)}) collective-permute-start(f32[4,3,4,8,128]{4,3,2,1,0:T(8,128)S(1)} %pad_maximum_fusion.22), channel_id=1, source_target_pairs={{0,4},{1,5},{4,0},{5,1},{8,12},{9,13},{12,8},{13,9},{16,20},{17,21... | collective-permute-start | bytes 589832 | tf_op jit(solution)/shard_map/ppermute | solution.py:554
  164.9 14.1 %collective-permute-start.31 = (f32[4,3,4,8,128]{4,3,2,1,0:T(8,128)S(1)}, f32[4,3,4,8,128]{4,3,2,1,0:T(8,128)S(1)}, u32[]{:S(2)}, u32[]{:S(2)}) collective-permute-start(f32[4,3,4,8,128]{4,3,2,1,0:T(8,128)S(1)} %pad_maximum_fusion.23), channel_id=1, source_target_pairs={{0,5},{1,4},{4,1},{5,0},{8,13},{9,12},{12,9},{13,8},{16,21},{17,20... | collective-permute-start | bytes 589832 | tf_op jit(solution)/shard_map/ppermute | solution.py:554
  187.6 35.9 %collective-permute-start.49 = (f32[3,128,128]{2,1,0:T(8,128)S(1)}, f32[3,128,128]{2,1,0:T(8,128)S(1)}, u32[]{:S(2)}, u32[]{:S(2)}) collective-permute-start(f32[3,128,128]{2,1,0:T(8,128)S(1)} %bitcast.489), channel_id=1, source_target_pairs={{0,8},{1,9},{4,12},{5,13},{8,0},{9,1},{12,4},{13,5},{16,24},{17,25... | collective-permute-start | bytes 589832 | tf_op jit(solution)/shard_map/ppermute | solution.py:554
  188.7 34.8 %collective-permute-start.50 = (f32[3,128,128]{2,1,0:T(8,128)S(1)}, f32[3,128,128]{2,1,0:T(8,128)S(1)}, u32[]{:S(2)}, u32[]{:S(2)}) collective-permute-start(f32[3,128,128]{2,1,0:T(8,128)S(1)} %bitcast.487), channel_id=1, source_target_pairs={{0,16},{1,17},{4,20},{5,21},{8,24},{9,25},{12,28},{13,29},{16,0},{... | collective-permute-start | bytes 589832 | tf_op jit(solution)/shard_map/ppermute | solution.py:554
  190.8 32.7 %collective-permute-start.51 = (f32[3,128,128]{2,1,0:T(8,128)S(1)}, f32[3,128,128]{2,1,0:T(8,128)S(1)}, u32[]{:S(2)}, u32[]{:S(2)}) collective-permute-start(f32[3,128,128]{2,1,0:T(8,128)S(1)} %bitcast.486), channel_id=1, source_target_pairs={{0,24},{1,25},{4,28},{5,29},{8,16},{9,17},{12,20},{13,21},{16,8},{... | collective-permute-start | bytes 589832 | tf_op jit(solution)/shard_map/ppermute | solution.py:554
  197.1 25.6 %collective-permute-start.36 = (f32[3,128,128]{2,1,0:T(8,128)S(1)}, f32[3,128,128]{2,1,0:T(8,128)S(1)}, u32[]{:S(2)}, u32[]{:S(2)}) collective-permute-start(f32[3,128,128]{2,1,0:T(8,128)S(1)} %bitcast.502), channel_id=1, source_target_pairs={{0,16},{1,17},{4,20},{5,21},{8,24},{9,25},{12,28},{13,29},{16,0},{... | collective-permute-start | bytes 589832 | tf_op jit(solution)/shard_map/ppermute | solution.py:554
  207.9 14.8 %collective-permute-start.37 = (f32[3,128,128]{2,1,0:T(8,128)S(1)}, f32[3,128,128]{2,1,0:T(8,128)S(1)}, u32[]{:S(2)}, u32[]{:S(2)}) collective-permute-start(f32[3,128,128]{2,1,0:T(8,128)S(1)} %bitcast.500), channel_id=1, source_target_pairs={{0,24},{1,25},{4,28},{5,29},{8,16},{9,17},{12,20},{13,21},{16,8},{... | collective-permute-start | bytes 589832 | tf_op jit(solution)/shard_map/ppermute | solution.py:554
  (75 other events, 593.8 us)

commit v2 on v1

--- a/solution.py
+++ b/solution.py
@@ -3,6 +3,7 @@
 
 import jax
 import jax.numpy as jnp
+import numpy as np
 from jax import lax
 from jax.experimental import pallas as pl
 from jax.experimental.pallas import tpu as pltpu
@@ -11,8 +12,7 @@
 TIME_STEP = 0.1
 DAMPING = 0.5
 AXES = ("slab", "pen")
-CHUNKS = 2
-VMEM_BYTES = 40 * 1024 * 1024
+SCALARS = pl.BlockSpec(memory_space=pltpu.SMEM)
 
 
 def shifted(block, axis, distance):
@@ -246,13 +246,6 @@
     return jnp.dot(left, right, preferred_element_type=jnp.float32)
 
 
-def table_parts(table):
-    high = lax.reduce_precision(table, 8, 7)
-    return jnp.concatenate([high, lax.reduce_precision(table - high, 8, 7), high], axis=1).astype(
-        jnp.bfloat16
-    )
-
-
 def turn(value):
     return pltpu.roll(value, value.shape[-1] // 2, value.ndim - 1)
 
@@ -261,14 +254,12 @@
     return lax.broadcasted_iota(jnp.int32, shape, len(shape) - 1)
 
 
-def forward_kernel(field_ref, depth_ref, table_ref, mask_ref, *out_refs):
+def forward_kernel(groups, field_ref, depth_ref, *refs):
+    table_refs, out_refs = refs[: 2 * len(groups)], refs[2 * len(groups) :]
     _, planes, width, depth = field_ref.shape
     half = depth // 2
     lane = lane_index((width, depth))
     signs = jnp.where(lane == 0, 0.0, jnp.where(lane < half, 1.0, -1.0))
-    own = mask_ref[0]
-    other = mask_ref[1] > 0.5
-    part = table_ref.shape[0] // len(out_refs)
     for component in range(3):
         high, low = split(field_ref[component].reshape(planes * width, depth))
         lines = product(jnp.concatenate([high, high, low], axis=1), depth_ref[...])
@@ -281,21 +272,27 @@
             extra = jnp.where(lane == plane, moved, extra)
             columns.append(stacked_parts(jnp.concatenate([line, turned * signs], axis=0)))
         columns.append(stacked_parts(jnp.concatenate([extra, -turn(extra)], axis=0)))
-        mixed = product(table_ref[...], jnp.concatenate(columns, axis=1))
-        extra = mixed[:, planes * depth :]
-        for plane in range(planes):
-            value = mixed[:, plane * depth : (plane + 1) * depth]
-            value = value - own * pltpu.roll(extra, half - plane, 1)
-            back = pltpu.roll(extra, depth - plane, 1) if plane else extra
-            value = jnp.where(other, back, value)
-            for index, out_ref in enumerate(out_refs):
-                out_ref[component, pl.ds(plane, part, stride=planes), :] = value[
-                    index * part : (index + 1) * part
-                ]
+        columns = jnp.concatenate(columns, axis=1)
+        outs = list(out_refs)
+        for chunk, group in enumerate(groups):
+            table_ref, mask_ref = table_refs[2 * chunk : 2 * chunk + 2]
+            part = table_ref.shape[0] // group
+            mixed = product(table_ref[...], columns)
+            extra = mixed[:, planes * depth :]
+            for plane in range(planes):
+                value = mixed[:, plane * depth : (plane + 1) * depth]
+                value = value - mask_ref[0] * pltpu.roll(extra, half - plane, 1)
+                back = pltpu.roll(extra, depth - plane, 1) if plane else extra
+                value = jnp.where(mask_ref[1] > 0.5, back, value)
+                for index, out_ref in enumerate(outs[:group]):
+                    out_ref[component, pl.ds(plane, part, stride=planes), :] = value[
+                        index * part : (index + 1) * part
+                    ]
+            outs = outs[group:]
 
 
 def middle_kernel(start, inner, kernel_ref, weight_ref, table_ref, inverse_ref, *refs):
-    in_refs, out_refs = refs[:inner], refs[inner:]
+    in_refs, out_refs = in_order(refs[:inner]), refs[inner:]
     outer, _, rows, planes, depth = in_refs[0].shape
     half = depth // 2
     count = inner * outer * planes
@@ -363,7 +360,7 @@
 
 
 def backward_kernel(table_ref, mask_ref, *refs):
-    in_refs, out_ref = refs[:-1], refs[-1]
+    in_refs, out_ref = in_order(refs[:-1]), refs[-1]
     _, planes, _, depth = out_ref.shape
     for component in range(3):
         mixed = gathered_columns(component, in_refs, mask_ref, table_ref, planes)
@@ -379,8 +376,17 @@
     ]
 
 
-def advance_kernel(table_ref, mask_ref, depth_ref, partial_ref, local_ref, field_ref, *refs):
-    in_refs, out_ref, dipole_ref = refs[:-2], refs[-2], refs[-1]
+def edge_planes(field_ref, bond_ref, first_ref, carried_ref):
+    bond = bond_ref[0, 0].astype(jnp.float32)
+    for component in range(3):
+        first_ref[component] = field_ref[component, 0]
+        carried_ref[component] = bond * field_ref[component, field_ref.shape[1] - 1]
+
+
+def advance_kernel(edges, *refs):
+    refs, (out_ref, *edge_refs, dipole_ref) = refs[: -2 - 2 * edges], refs[-2 - 2 * edges :]
+    in_refs, refs = in_order(refs[:-7]), refs[-7:]
+    table_ref, mask_ref, depth_ref, partial_ref, local_ref, field_ref, bond_ref = refs
     _, planes, width, depth = out_ref.shape
     for component in range(3):
         mixed = gathered_columns(component, in_refs, mask_ref, table_ref, planes)
@@ -405,11 +411,18 @@
         )
         for component in range(3):
             out_ref[component, plane] = stepped[component] * scale
-
-
-def local_kernel(scale_ref, field_ref, above_ref, below_ref, bond_ref, noise_ref, out_ref):
+    if edges:
+        edge_planes(out_ref, bond_ref, *edge_refs)
+
+
+def local_kernel(
+    step, scale_ref, field_ref, above_ref, below_ref, bond_ref, noise_ref, out_ref, held_ref, sem
+):
     _, planes, width, depth = out_ref.shape
-    scale = scale_ref[0]
+    copy = pltpu.make_async_copy(noise_ref.at[step], held_ref, sem)
+    copy.start()
+    copy.wait()
+    scale = scale_ref[step : step + 1, :]
     for plane in range(planes):
         bonds = [bond_ref[d, plane].astype(jnp.float32) for d in range(3)]
         if plane:
@@ -426,34 +439,192 @@
             total = total + pltpu.roll(bonds[1] * value, 1, 0)
             total = total + bonds[2] * pltpu.roll(value, depth - 1, 1)
             total = total + pltpu.roll(bonds[2] * value, 1, 1)
-            out_ref[component, plane] = total + scale * noise_ref[component, plane].astype(
+            out_ref[component, plane] = total + scale * held_ref[component, plane].astype(
                 jnp.float32
             )
 
 
-def call(kernel, outs, operands, flops, scratch=(), scalars=0):
+def call(kernel, outs, operands, scratch=(), specs=None, out_specs=None, before=(), after=(), mib=16):
+    specs = {} if specs is None else specs
+    out_specs = {} if out_specs is None else out_specs
     whole = pl.BlockSpec(memory_space=pltpu.VMEM)
-    moved = sum(math.prod(a.shape) * a.dtype.itemsize for a in list(operands) + list(outs))
+    unread = pl.BlockSpec(memory_space=pl.ANY)
+
+    def body(*refs):
+        refs = refs[len(before) :]
+        kernel(*refs[: len(operands)], *refs[len(operands) + len(after) :])
+
     return pl.pallas_call(
-        kernel,
+        body,
         out_shape=list(outs),
-        in_specs=[pl.BlockSpec(memory_space=pltpu.SMEM)] * scalars
-        + [whole] * (len(operands) - scalars),
-        out_specs=[whole] * len(outs),
+        in_specs=[unread] * len(before)
+        + [specs.get(i, whole) for i in range(len(operands))]
+        + [unread] * len(after),
+        out_specs=[out_specs.get(i, whole) for i in range(len(outs))],
         scratch_shapes=list(scratch),
-        cost_estimate=pl.CostEstimate(flops=flops, bytes_accessed=moved, transcendentals=0),
-        compiler_params=pltpu.CompilerParams(vmem_limit_bytes=VMEM_BYTES),
-    )(*operands)
+        cost_estimate=pl.CostEstimate(flops=1, bytes_accessed=1, transcendentals=0),
+        compiler_params=pltpu.CompilerParams(vmem_limit_bytes=mib * 1024 * 1024),
+    )(*before, *operands, *after)
+
+
+def shape_of(*shape, dtype=jnp.float32):
+    return jax.ShapeDtypeStruct(shape, dtype)
+
+
+def log2(size):
+    return size.bit_length() - 1
+
+
+class Route:
+    def __init__(self, start, rows, first, second):
+        self.start, self.rows, self.first, self.second = start, rows, first, second
+
+    def distance(self, index, second_leads):
+        lead, last = (self.second, self.first) if second_leads else (self.first, self.second)
+        return (index >> log2(last[0])) * lead[1] + (index & (last[0] - 1)) * last[1]
+
+    def waves(self, me, index, row_block):
+        block = me ^ self.distance(index >> log2(self.rows), False)
+        return block * row_block + self.start + (index & (self.rows - 1))
+
+    def cells(self, me, index, planes):
+        block = me ^ self.distance(index >> log2(planes), True)
+        return block * planes + (index & (planes - 1))
 
 
 def angles(left, right, length):
-    product_of = left[:, None] * right[None, :] % length
-    angle = 2.0 * math.pi / length * product_of.astype(jnp.float32)
+    angle = (2.0 * math.pi / length) * ((left * right) & (length - 1)).astype(jnp.float32)
     return jnp.cos(angle), jnp.sin(angle)
 
 
-def shape_of(*shape):
-    return jax.ShapeDtypeStruct(shape, jnp.float32)
+def table_parts(table):
+    high, low = split(table)
+    return jnp.concatenate([high, low, high], axis=1)
+
+
+def iota(shape, axis):
+    return lax.broadcasted_iota(jnp.int32, shape, axis)
+
+
+def forward_tables(routes, row_block, me_ref, *out_refs):
+    me = me_ref[0]
+    for route, table_ref, mask_ref in zip(routes, out_refs[0::2], out_refs[1::2]):
+        _, count, depth = mask_ref.shape
+        width = table_ref.shape[1] // 6
+        wave = route.waves(me, iota((count, width), 0), row_block)
+        cosine, sine = angles(wave, iota((count, width), 1), width)
+        table_ref[...] = table_parts(jnp.concatenate([cosine, sine], axis=1))
+        wave = route.waves(me, iota((count, depth), 0), row_block)
+        lane = iota((count, depth), 1)
+        below = (wave > 0) & (wave < width // 2) & (lane == depth // 2)
+        above = (wave > width // 2) & ((lane == 0) | (lane == depth // 2))
+        mask_ref[0] = jnp.where(below, 1.0, 0.0)
+        mask_ref[1] = jnp.where(above, 1.0, 0.0)
+
+
+def other_tables(routes, row_block, planes, me_ref, temps_ref, order_ref, accept_ref, *out_refs):
+    labels_ref, scale_ref, weight_ref, *out_refs = out_refs
+    me = me_ref[0]
+    for pair in range(order_ref.shape[0] // 2):
+        left, right = order_ref[2 * pair], order_ref[2 * pair + 1]
+        swapped = (accept_ref[left] == 1) & (accept_ref[right] == 1)
+        labels_ref[left] = jnp.where(swapped, right, left)
+        labels_ref[right] = jnp.where(swapped, left, right)
+    for step, slot in enumerate((me_ref[1], labels_ref[me_ref[1]])):
+        picked = jnp.full((1, scale_ref.shape[1]), temps_ref[slot], jnp.float32)
+        scale_ref[step : step + 1, :] = jnp.sqrt(2.0 * DAMPING * picked / TIME_STEP)
+    depth = weight_ref.shape[1]
+    half = depth // 2
+    for index, route in enumerate(routes):
+        into_ref, out_ref, table_ref, mask_ref = out_refs[4 * index : 4 * index + 4]
+        cells = into_ref.shape[0]
+        shape = (cells, cells)
+        cosine, sine = angles(route.cells(me, iota(shape, 1), planes), iota(shape, 0), cells)
+        into_ref[...] = table_parts(jnp.concatenate([cosine, sine], axis=1))
+        cosine, sine = angles(route.cells(me, iota(shape, 0), planes), iota(shape, 1), cells)
+        out_ref[...] = table_parts(jnp.concatenate([-cosine, sine], axis=1) / cells)
+        count = mask_ref.shape[1]
+        width = table_ref.shape[0]
+        shape = (width, count)
+        wave = route.waves(me, iota(shape, 1), row_block)
+        cosine, sine = angles(wave, iota(shape, 0), width)
+        table_ref[...] = table_parts(jnp.concatenate([cosine, sine], axis=1) / width)
+        shape = (count, depth)
+        wave = route.waves(me, iota(shape, 0), row_block)
+        lane = iota(shape, 1)
+        first, last = lane == 0, lane == half
+        pair = first | last
+        below = (wave > 0) & (wave < width // 2) & first
+        above = (wave > width // 2) & last
+        ends = (wave == 0) | (wave == width // 2)
+        sign = jnp.where(lane < half, -1.0, 1.0)
+        mask_ref[0] = jnp.where(pair, jnp.where(ends, 1.0, jnp.where(below, 2.0, 0.0)), 1.0)
+        mask_ref[1] = jnp.where(above, 2.0, 0.0)
+        mask_ref[2] = jnp.where(above, -2.0, 0.0)
+        mask_ref[3] = jnp.where(pair, jnp.where(below, -2.0, 0.0), sign)
+    blocks = width // row_block
+    ends = jnp.where((me & (blocks // 2 - 1)) == 0, 1.0, 0.0)
+    upper = jnp.where(me >= blocks // 2, 1.0, 0.0)
+    lane = iota((1, depth), 1)
+    first, last = lane == 0, lane == half
+    direct = jnp.where(first, 1.0 - upper, jnp.where(last, upper, jnp.where(lane < half, 1.0, 0.0)))
+    both = jnp.where(first | last, 0.5 * ends, 0.0)
+    keep = jnp.where(first | last, 1.0 - ends, 1.0)
+    flip = jnp.where(first, both, -both)
+    kinds = [
+        direct,
+        1.0 - direct,
+        direct * keep + both,
+        (1.0 - direct) * keep + both,
+        flip,
+        -flip,
+    ]
+    for index, kind in enumerate(kinds):
+        weight_ref[index : index + 1, :] = kind
+
+
+def visiting(count):
+    return sorted(range(count), key=lambda i: (i < count // 2, i))
+
+
+def in_order(refs):
+    ordered = [None] * len(refs)
+    for place, ref in zip(visiting(len(refs)), refs):
+        ordered[place] = ref
+    return ordered
+
+
+def leaving(blocks):
+    return [blocks[i] for i in visiting(len(blocks))]
+
+
+def repack_forward(count, *refs):
+    in_refs, out_refs = in_order(refs[:count]), refs[count:]
+    for out_index, out_ref in enumerate(out_refs):
+        for in_index, in_ref in enumerate(in_refs):
+            out_ref[in_index] = in_ref[:, out_index]
+
+
+def repack_backward(count, *refs):
+    in_refs, out_refs = in_order(refs[:count]), refs[count:]
+    for out_index, out_ref in enumerate(out_refs):
+        for in_index, in_ref in enumerate(in_refs):
+            out_ref[:, in_index] = in_ref[out_index]
+
+
+def depth_tables(depth):
+    half = depth // 2
+    angle = 2.0 * np.pi / depth * np.outer(np.arange(depth), np.arange(half)) % (2.0 * np.pi)
+    middle = np.where(np.arange(depth) % 2 == 0, 1.0, -1.0)[:, None]
+    into = np.concatenate([np.cos(angle), middle, -np.sin(angle[:, 1:])], axis=1)
+    lane = np.arange(depth)
+    out_of = (into * np.where(lane % half == 0, 1.0, 2.0) / depth).T
+    tables = []
+    for table in (into, out_of):
+        high = table.astype(jnp.bfloat16)
+        low = (table - high.astype(np.float64)).astype(jnp.bfloat16)
+        tables.append(jnp.asarray(np.concatenate([high, low, high], axis=0)))
+    return tables
 
 
 def on_device(moments, couplings, noise, kernel, temps, order, accept):
@@ -462,154 +633,137 @@
     count = lax.axis_size("slab") * lax.axis_size("pen")
     if planes % 8 or row_block % 8 or depth % 128 or count & (count - 1) or moments.shape[0] > 1:
         return plain_on_device(moments, couplings, noise, kernel, temps, order, accept)
-    inner = 1 << ((count.bit_length() - 1) // 2)
-    outer = count // inner
-    half = depth // 2
-    rows = row_block // CHUNKS
-    me = lax.axis_index(AXES)
-    numbers = functools.partial(jnp.arange, dtype=jnp.int32)
-
-    def partner(outer_first):
-        near, far = numbers(inner), numbers(outer) * inner
-        pair = far[:, None] + near[None, :] if outer_first else far[None, :] + near[:, None]
-        return me ^ pair.reshape(-1)
-
-    def spread(block_index, size, start, step):
-        return (block_index[:, None] * step + start + numbers(size)[None, :]).reshape(-1)
-
-    lane = numbers(depth)[None, :]
-    lower_lane = lane < half
-    cosine, sine = angles(numbers(depth), numbers(half), depth)
-    middle = (1 - 2 * (numbers(depth) % 2)).astype(jnp.float32)[:, None]
-    into_depth = jnp.concatenate([cosine, middle, -sine[:, 1:]], axis=1)
-    weight = jnp.where((lane == 0) | (lane == half), 1.0, 2.0) / depth
-    out_of_depth = (into_depth * weight).T
-    into_depth = table_parts(into_depth.T).T
-    out_of_depth = table_parts(out_of_depth.T).T
-    into_width, out_of_width, into_masks, out_masks = [], [], [], []
-    for chunk in range(CHUNKS):
-        wave = spread(partner(True), rows, chunk * rows, row_block)
-        cosine, sine = angles(wave, numbers(width), width)
-        into_width.append(table_parts(jnp.concatenate([cosine, sine], axis=1)))
-        back = jnp.concatenate([cosine, sine], axis=0).T / width
-        out_of_width.append(table_parts(back))
-        wave = wave[:, None]
-        below = (wave > 0) & (wave < width // 2)
-        above = wave > width // 2
-        ends = (wave == 0) | (wave == width // 2)
-        pair = (lane == 0) | (lane == half)
-        into_masks.append(
-            jnp.stack([below & (lane == half), above & pair]).astype(jnp.float32)
-        )
-        zero, sign = jnp.zeros((wave.shape[0], depth)), jnp.where(lower_lane, -1.0, 1.0)
-        first, last = lane == 0, lane == half
-        out_masks.append(
-            jnp.stack(
-                [
-                    jnp.where(pair, jnp.where(ends, 1.0, jnp.where(below & first, 2.0, 0.0)), 1.0)
-                    + zero,
-                    jnp.where(above & last, 2.0, 0.0) + zero,
-                    jnp.where(above & last, -2.0, 0.0) + zero,
-                    jnp.where(pair, jnp.where(below & first, -2.0, 0.0), sign) + zero,
-                ]
+    near = (1 << (log2(count) // 2), 1)
+    far = (count // near[0], near[0])
+    rows = row_block // 2
+    routes = [Route(0, rows, far, near), Route(rows, rows, near, far)]
+    me = jnp.stack([lax.axis_index(AXES), lax.axis_index("temp")]).astype(jnp.int32)
+    into_depth, out_of_depth = depth_tables(depth)
+    lines = count * rows
+    field = moments[0]
+    whole = shape_of(*field.shape)
+    plane_shape = shape_of(3, width, depth)
+    forward = call(
+        functools.partial(forward_tables, routes, row_block),
+        [shape_of(lines, 6 * width, dtype=jnp.bfloat16), shape_of(2, lines, depth)] * 2,
+        [me],
+        specs={0: SCALARS},
+    )
+    square = shape_of(width, 6 * width, dtype=jnp.bfloat16)
+    labels, scales, weights, *others = call(
+        functools.partial(other_tables, routes, row_block, planes),
+        [shape_of(*order.shape, dtype=jnp.int32), shape_of(2, depth), shape_of(6, depth)]
+        + [square, square, shape_of(width, 6 * lines, dtype=jnp.bfloat16), shape_of(4, lines, depth)]
+        * 2,
+        [me, temps, order, accept],
+        specs={i: SCALARS for i in range(4)},
+        out_specs={0: SCALARS},
+    )
+    others = [others[:4], others[4:]]
+    kernel_rows = kernel.reshape(6, width * row_block, depth)
+    noise = noise[:, 0]
+    unread = pl.BlockSpec(memory_space=pl.ANY)
+
+    def exchange(blocks, stage):
+        size, stride = stage
+        moved = list(blocks)
+        for index in leaving(range(size)):
+            if not index:
+                continue
+            distance = index * stride
+            moved[index] = lax.ppermute(
+                blocks[index], AXES, [(i, i ^ distance) for i in range(count)]
             )
-        )
-    cell = spread(partner(False), planes, 0, planes)
-    cosine, sine = angles(numbers(count * planes), cell, count * planes)
-    into_first = table_parts(jnp.concatenate([cosine, sine], axis=1))
-    out_of_first = table_parts(
-        jnp.concatenate([-cosine.T, sine.T], axis=1) / (count * planes)
-    )
-    lane = lane[0]
-    ends = (me == 0) | (me == count // 2)
-    upper = me >= count // 2
-    direct = jnp.where(lane == 0, ~upper, jnp.where(lane == half, upper, lane < half))
-    direct = direct.astype(jnp.float32)
-    pair = ends & ((lane == 0) | (lane == half))
-    both = jnp.where(pair, 0.5, 0.0)
-    flip = jnp.where(lane == 0, 1.0, -1.0) * both
-    kinds = [
-        direct,
-        1.0 - direct,
-        jnp.where(pair, 0.5, direct),
-        jnp.where(pair, 0.5, 1.0 - direct),
-        flip,
-        -flip,
-    ]
-    weights = jnp.stack(kinds)
-
-    labels = pair_labels(order, accept)
-    slot_index = jnp.arange(temps.shape[0], dtype=jnp.int32)
-    offset = lax.axis_index("temp")
-    own_slots = lax.dynamic_slice_in_dim(slot_index, offset, 1)
-    own_labels = lax.dynamic_slice_in_dim(labels, offset, 1)
-    scales = (slot_sigma(own_slots, temps), slot_sigma(own_labels, temps))
-
-    kernel_rows = kernel.reshape(6, width * row_block, depth)
-    field = moments[0]
-
-    def swap(block, distance):
-        if distance == 0:
-            return block
-        return lax.ppermute(block, AXES, [(i, i ^ distance) for i in range(count)])
-
-    flat = shape_of(3, inner * rows * planes, depth)
-    piled = shape_of(outer, 3, rows, planes, depth)
-    whole = shape_of(*field.shape)
-    far_order = sorted(range(outer), key=lambda i: -(i.bit_length()))
-    near_order = range(inner)
-
-    for step_index in range(2):
-        above = shifted(field[:, 0], AXES, -1)
-        below = shifted(couplings[0, -1].astype(jnp.float32) * field[:, -1], AXES, 1)
-        sums = None
-        for chunk in range(CHUNKS):
-            sent = call(
-                forward_kernel,
-                [flat] * outer,
-                [field, into_depth, into_width[chunk], into_masks[chunk]],
-                200_000_000,
-            )
-            arrived = [None] * outer
-            for far in far_order:
-                arrived[far] = swap(sent[far], far * inner)
-            arrived = [a.reshape(3, inner, rows, planes, depth) for a in arrived]
-            spectra = [
-                swap(jnp.stack([a[:, near] for a in arrived]), near) for near in near_order
-            ]
-            spectra = call(
-                functools.partial(middle_kernel, chunk * rows, inner),
-                [piled] * inner,
-                [kernel_rows, weights, into_first, out_of_first]
-                + spectra,
-                400_000_000,
-            )
-            spectra = [swap(spectra[near], near) for near in near_order]
-            returned = [None] * outer
-            for far in far_order:
-                block = jnp.stack([s[far] for s in spectra], axis=1).reshape(flat.shape)
-                returned[far] = swap(block, far * inner)
-            if chunk == 0:
-                (sums,) = call(
-                    backward_kernel,
-                    [whole],
-                    [out_of_width[chunk], out_masks[chunk]] + returned,
-                    200_000_000,
-                )
+        return moved
+
+    def forward_part(field):
+        groups = [route.first[0] for route in routes]
+        outs = []
+        for route in routes:
+            shape = shape_of(3, route.second[0] * rows * planes, depth)
+            outs += [shape] * route.first[0]
+        blocks = call(
+            functools.partial(forward_kernel, groups),
+            outs,
+            [field, into_depth, *forward],
+        )
+        return blocks[: groups[0]], blocks[groups[0] :]
+
+    def forward_repack(chunk, blocks, **order):
+        first, second = routes[chunk].first[0], routes[chunk].second[0]
+        return call(
+            functools.partial(repack_forward, first),
+            [shape_of(first, 3, rows * planes, depth)] * second,
+            [block.reshape(3, second, rows * planes, depth) for block in leaving(blocks)],
+            **order,
+        )
+
+    def middle_part(chunk, blocks, **order):
+        first, second = routes[chunk].first[0], routes[chunk].second[0]
+        into_first, out_of_first = others[chunk][:2]
+        shape = shape_of(first, 3, rows, planes, depth)
+        return call(
+            functools.partial(middle_kernel, routes[chunk].start, second),
+            [shape] * second,
+            [kernel_rows, weights, into_first, out_of_first]
+            + [block.reshape(shape.shape) for block in leaving(blocks)],
+            **order,
+        )
+
+    def backward_repack(chunk, blocks, **order):
+        first, second = routes[chunk].first[0], routes[chunk].second[0]
+        blocks = call(
+            functools.partial(repack_backward, second),
+            [shape_of(3, second, rows * planes, depth)] * first,
+            [block.reshape(first, 3, rows * planes, depth) for block in leaving(blocks)],
+            **order,
+        )
+        return [block.reshape(3, -1, depth) for block in blocks]
+
+    first_plane = field[:, 0]
+    carried = couplings[0, -1].astype(jnp.float32) * field[:, -1]
+    for step in range(2):
+        a_out, b_out = forward_part(field)
+        a_far = exchange(a_out, far)
+        b_near = exchange(b_out, near)
+        b_packed = forward_repack(1, b_near)
+        a_packed = forward_repack(0, a_far, after=b_packed[:1])
+        b_far = exchange(b_packed, far)
+        a_near = exchange(a_packed, near)
+        a_mid = middle_part(0, a_near)
+        b_mid = middle_part(1, b_far, before=a_mid[:1])
+        above = shifted(first_plane, AXES, -1)
+        below = shifted(carried, AXES, 1)
+        b_back = exchange(b_mid, far)
+        a_back = exchange(a_mid, near)
+        a_home = backward_repack(0, a_back, before=b_mid[:1], after=[above, below])
+        b_home = backward_repack(1, b_back, before=a_home[:1])
+        a_done = exchange(a_home, far)
+        b_done = exchange(b_home, near)
         (local,) = call(
-            local_kernel,
+            functools.partial(local_kernel, step),
             [whole],
-            [scales[step_index], field, above, below, couplings, noise[step_index, 0]],
-            20_000_000,
-            scalars=1,
-        )
-        (field,) = call(
-            advance_kernel,
+            [scales, field, above, below, couplings, noise],
+            scratch=[pltpu.VMEM(field.shape, noise.dtype), pltpu.SemaphoreType.DMA(())],
+            specs={5: unread},
+            before=a_home[:1],
+        )
+        (sums,) = call(
+            backward_kernel,
             [whole],
-            [out_of_width[-1], out_masks[-1], out_of_depth, sums, local, field] + returned,
-            300_000_000,
+            [others[1][2], others[1][3]] + leaving(b_done),
+            after=[local],
+        )
+        edges = step == 0
+        field, *planes_out = call(
+            functools.partial(advance_kernel, edges),
+            [whole] + [plane_shape] * 2 * edges,
+            leaving(a_done)
+            + [others[0][2], others[0][3], out_of_depth, sums, local, field, couplings[:1, -1:]],
             scratch=[pltpu.VMEM(whole.shape, jnp.float32)],
         )
+        if edges:
+            first_plane, carried = planes_out
     return (field[None], labels)
 
 

time: 229 us -> 192 us (0.84)
  waiting for transfers between devices: 103 us -> 76.1 us
  starting transfers between devices: 61 us -> 80.9 us
  other arithmetic: 14.9 us -> 1.79 us
  local copies, waits for them, and re-layouts: 13.6 us -> 3.28 us
  between operations: 3.47 us -> 1.01 us
  Pallas kernels: 30.7 us -> 28.4 us
    ppermute x48, waiting for transfers between devices: 103 us -> 76.1 us  [exchange(): lax.ppermute(blocks[index], AXES, [(i, i ^ distance) for i in range(count)])]
    ppermute x48, starting transfers between devices: 54.4 us -> 74.9 us  [exchange(): lax.ppermute(blocks[index], AXES, [(i, i ^ distance) for i in range(count)])]
    another operation x49 -> x0, local copies, waits for them, and re-layouts: 7.41 us -> none  [the longest x16 6.26 us: on_device(): jnp.stack([a[:, near] for a in arrived])]
    another operation x41 -> x1, other arithmetic: 3.49 us -> 0.08 us  [on_device(): jnp.stack([lax.axis_index(AXES), lax.axis_index('temp')]).astype(jnp.int32)]
    pallas_call x14 -> x22, Pallas kernels: 30.7 us -> 28.4 us  [call(): pl.pallas_call(body, out_shape=list(outs), in_specs=[unread] * len(before...]
  transfers between devices with their start and end apart: 52 -> 52, of which waited for: 25 -> 17; matrix products, arithmetic and copies ran while one was open for 11% -> 1% of each run, Pallas kernels for 7% -> 8%
where the time goes in v2:
time: 192 us; the launch traced here: 191 us
  starting transfers between devices  80.9 us (42%)
  waiting for transfers between devices  76.1 us (40%)
  Pallas kernels  28.4 us (15%)
  local copies, waits for them, and re-layouts  3.28 us (2%)
    ppermute x48, waiting for transfers between devices, exchange(): lax.ppermute(blocks[index], AXES, [(i, i ^ distance) for i in range(count)])  76.1 us
    ppermute x48, starting transfers between devices, exchange(): lax.ppermute(blocks[index], AXES, [(i, i ^ distance) for i in range(count)])  74.9 us
    pallas_call x22, Pallas kernels, call(): pl.pallas_call(body, out_shape=list(outs), in_specs=[unread] * len(before...  28.4 us
    ppermute x4, starting transfers between devices, shifted(): return lax.ppermute(block, axis, route)  5.94 us
  transfers between devices with their start and end apart: 52, of which 17 were waited for; matrix products, arithmetic and copies ran while one was open for 1% of the time, Pallas kernels for 8%

profile of v2, /device:TPU:0, one launch (start us, length us, event | category | flops | bytes accessed | tf_op | source)
XLA Modules:
  0.0 191.5 jit_solution(12981667911295117918)
XLA Ops:
  3.9 3.2 %shard_map.106 = (f32[3,128,128]{2,1,0:T(8,128)S(1)}, f32[3,128,128]{2,1,0:T(8,128)S(1)}, f32[3,128,128]{2,1,0:T(8,128)S(1)}, f32[3,128,128]{2,1,0:T(8,128)S(1)}...) custom-call(f32[3,8,128,128]{3,2,1,0:T(8,128)S(1)} %bitcast.85, ...), custom_call_target="tpu_custom_call" | custom-call | flops 1 | bytes 1 | tf_op jit(solution)/shard_map/pallas_call | solution.py:457
  7.1 4.1 %collective-permute-start = (f32[3,128,128]{2,1,0:T(8,128)S(1)}, f32[3,128,128]{2,1,0:T(8,128)S(1)}, u32[]{:S(2)}, u32[]{:S(2)}) collective-permute-start(f32[3,128,128]{2,1,0:T(8,128)S(1)} %get-tuple-element.91), channel_id=1, source_target_pairs={{0,16},{1,17},{4,20},{5,21},{8,24},{9,25},{12,28},{13,29},{16,0},{... | collective-permute-start | bytes 589832 | tf_op jit(solution)/shard_map/ppermute | solution.py:674
  17.6 2.9 %collective-permute-done.3 = f32[3,128,128]{2,1,0:T(8,128)S(1)} collective-permute-done((f32[3,128,128]{2,1,0:T(8,128)S(1)}, f32[3,128,128]{2,1,0:T(8,128)S(1)}, u32[]{:S(2)}, u32[]{:S(2)}) %collective-permute-start.3) | collective-permute-done | bytes 196640 | tf_op jit(solution)/shard_map/ppermute | solution.py:674
  22.2 3.2 %collective-permute-done = f32[3,128,128]{2,1,0:T(8,128)S(1)} collective-permute-done((f32[3,128,128]{2,1,0:T(8,128)S(1)}, f32[3,128,128]{2,1,0:T(8,128)S(1)}, u32[]{:S(2)}, u32[]{:S(2)}) %collective-permute-start) | collective-permute-done | bytes 196640 | tf_op jit(solution)/shard_map/ppermute | solution.py:674
  28.2 5.5 %collective-permute-start.9 = (f32[4,3,32,128]{3,2,1,0:T(8,128)S(1)}, f32[4,3,32,128]{3,2,1,0:T(8,128)S(1)}, u32[]{:S(2)}, u32[]{:S(2)}) collective-permute-start(f32[4,3,32,128]{3,2,1,0:T(8,128)S(1)} %get-tuple-element.107), channel_id=1, source_target_pairs={{0,16},{1,17},{4,20},{5,21},{8,24},{9,25},{12,28},{13,29},{16,0},{... | collective-permute-start | bytes 589832 | tf_op jit(solution)/shard_map/ppermute | solution.py:674
  42.4 5.1 %collective-permute-done.9 = f32[4,3,32,128]{3,2,1,0:T(8,128)S(1)} collective-permute-done((f32[4,3,32,128]{3,2,1,0:T(8,128)S(1)}, f32[4,3,32,128]{3,2,1,0:T(8,128)S(1)}, u32[]{:S(2)}, u32[]{:S(2)}) %collective-permute-start.9) | collective-permute-done | bytes 196640 | tf_op jit(solution)/shard_map/ppermute | solution.py:674
  52.5 4.5 %collective-permute-start.20 = (f32[4,3,4,8,128]{4,3,2,1,0:T(8,128)S(1)}, f32[4,3,4,8,128]{4,3,2,1,0:T(8,128)S(1)}, u32[]{:S(2)}, u32[]{:S(2)}) collective-permute-start(f32[4,3,4,8,128]{4,3,2,1,0:T(8,128)S(1)} %get-tuple-element.122), channel_id=1, source_target_pairs={{0,16},{1,17},{4,20},{5,21},{8,24},{9,25},{12,28},{13,29},{16,0},{... | collective-permute-start | bytes 589832 | tf_op jit(solution)/shard_map/ppermute | solution.py:674
  57.0 3.4 %collective-permute-start.21 = (f32[4,3,4,8,128]{4,3,2,1,0:T(8,128)S(1)}, f32[4,3,4,8,128]{4,3,2,1,0:T(8,128)S(1)}, u32[]{:S(2)}, u32[]{:S(2)}) collective-permute-start(f32[4,3,4,8,128]{4,3,2,1,0:T(8,128)S(1)} %get-tuple-element.123), channel_id=1, source_target_pairs={{0,24},{1,25},{4,28},{5,29},{8,16},{9,17},{12,20},{13,21},{16,8},{... | collective-permute-start | bytes 589832 | tf_op jit(solution)/shard_map/ppermute | solution.py:674
  60.5 10.7 %collective-permute-done.20 = f32[4,3,4,8,128]{4,3,2,1,0:T(8,128)S(1)} collective-permute-done((f32[4,3,4,8,128]{4,3,2,1,0:T(8,128)S(1)}, f32[4,3,4,8,128]{4,3,2,1,0:T(8,128)S(1)}, u32[]{:S(2)}, u32[]{:S(2)}) %collective-permute-start.20) | collective-permute-done | bytes 196640 | tf_op jit(solution)/shard_map/ppermute | solution.py:674
  73.9 3.4 %collective-permute-start.18 = (f32[3,128,128]{2,1,0:T(8,128)S(1)}, f32[3,128,128]{2,1,0:T(8,128)S(1)}, u32[]{:S(2)}, u32[]{:S(2)}) collective-permute-start(f32[3,128,128]{2,1,0:T(8,128)S(1)} %bitcast.151), channel_id=1, source_target_pairs={{0,24},{1,25},{4,28},{5,29},{8,16},{9,17},{12,20},{13,21},{16,8},{... | collective-permute-start | bytes 589832 | tf_op jit(solution)/shard_map/ppermute | solution.py:674
  79.2 3.3 %collective-permute-start.19 = (f32[3,128,128]{2,1,0:T(8,128)S(1)}, f32[3,128,128]{2,1,0:T(8,128)S(1)}, u32[]{:S(2)}, u32[]{:S(2)}) collective-permute-start(f32[3,128,128]{2,1,0:T(8,128)S(1)} %bitcast.147), channel_id=1, source_target_pairs={{0,8},{1,9},{4,12},{5,13},{8,0},{9,1},{12,4},{13,5},{16,24},{17,25... | collective-permute-start | bytes 589832 | tf_op jit(solution)/shard_map/ppermute | solution.py:674
  84.7 10.7 %collective-permute-done.17.refs_0_ = f32[3,128,128]{2,1,0:T(8,128)S(1)} collective-permute-done((f32[3,128,128]{2,1,0:T(8,128)S(1)}, f32[3,128,128]{2,1,0:T(8,128)S(1)}, u32[]{:S(2)}, u32[]{:S(2)}) %collective-permute-start.17) | collective-permute-done | bytes 196640 | tf_op jit(solution)/shard_map/ppermute | solution.py:674
  97.5 3.2 %shard_map.116 = (f32[3,128,128]{2,1,0:T(8,128)S(1)}, f32[3,128,128]{2,1,0:T(8,128)S(1)}, f32[3,128,128]{2,1,0:T(8,128)S(1)}, f32[3,128,128]{2,1,0:T(8,128)S(1)}...) custom-call(f32[3,8,128,128]{3,2,1,0:T(8,128)S(1)} %get-tuple-elemen, ...), custom_call_target="tpu_custom_call" | custom-call | flops 1 | bytes 1 | tf_op jit(solution)/shard_map/pallas_call | solution.py:457
  102.9 3.1 %collective-permute-start.27 = (f32[3,128,128]{2,1,0:T(8,128)S(1)}, f32[3,128,128]{2,1,0:T(8,128)S(1)}, u32[]{:S(2)}, u32[]{:S(2)}) collective-permute-start(f32[3,128,128]{2,1,0:T(8,128)S(1)} %get-tuple-element.132), channel_id=1, source_target_pairs={{0,24},{1,25},{4,28},{5,29},{8,16},{9,17},{12,20},{13,21},{16,8},{... | collective-permute-start | bytes 589832 | tf_op jit(solution)/shard_map/ppermute | solution.py:674
  111.0 8.6 %collective-permute-done.26 = f32[3,128,128]{2,1,0:T(8,128)S(1)} collective-permute-done((f32[3,128,128]{2,1,0:T(8,128)S(1)}, f32[3,128,128]{2,1,0:T(8,128)S(1)}, u32[]{:S(2)}, u32[]{:S(2)}) %collective-permute-start.26) | collective-permute-done | bytes 196640 | tf_op jit(solution)/shard_map/ppermute | solution.py:674
  128.5 3.3 %collective-permute-start.37 = (f32[4,3,32,128]{3,2,1,0:T(8,128)S(1)}, f32[4,3,32,128]{3,2,1,0:T(8,128)S(1)}, u32[]{:S(2)}, u32[]{:S(2)}) collective-permute-start(f32[4,3,32,128]{3,2,1,0:T(8,128)S(1)} %get-tuple-element.147), channel_id=1, source_target_pairs={{0,8},{1,9},{4,12},{5,13},{8,0},{9,1},{12,4},{13,5},{16,24},{17,25... | collective-permute-start | bytes 589832 | tf_op jit(solution)/shard_map/ppermute | solution.py:674
  131.8 3.3 %collective-permute-start.41 = (f32[3,128,128]{2,1,0:T(8,128)S(1)}, f32[3,128,128]{2,1,0:T(8,128)S(1)}, u32[]{:S(2)}, u32[]{:S(2)}) collective-permute-start(f32[3,128,128]{2,1,0:T(8,128)S(1)} %get-tuple-element.152), channel_id=1, source_target_pairs={{1,0},{4,1},{5,4},{8,5},{9,8},{12,9},{13,12},{16,13},{17,16},{20,1... | collective-permute-start | bytes 589832 | tf_op jit(solution)/shard_map/ppermute | solution.py:21
  137.4 3.5 %collective-permute-done.35 = f32[4,3,32,128]{3,2,1,0:T(8,128)S(1)} collective-permute-done((f32[4,3,32,128]{3,2,1,0:T(8,128)S(1)}, f32[4,3,32,128]{3,2,1,0:T(8,128)S(1)}, u32[]{:S(2)}, u32[]{:S(2)}) %collective-permute-start.35) | collective-permute-done | bytes 196640 | tf_op jit(solution)/shard_map/ppermute | solution.py:674
  145.5 5.1 %collective-permute-start.46 = (f32[4,3,4,8,128]{4,3,2,1,0:T(8,128)S(1)}, f32[4,3,4,8,128]{4,3,2,1,0:T(8,128)S(1)}, u32[]{:S(2)}, u32[]{:S(2)}) collective-permute-start(f32[4,3,4,8,128]{4,3,2,1,0:T(8,128)S(1)} %get-tuple-element.158), channel_id=1, source_target_pairs={{0,16},{1,17},{4,20},{5,21},{8,24},{9,25},{12,28},{13,29},{16,0},{... | collective-permute-start | bytes 589832 | tf_op jit(solution)/shard_map/ppermute | solution.py:674
  153.3 11.4 %collective-permute-done.46 = f32[4,3,4,8,128]{4,3,2,1,0:T(8,128)S(1)} collective-permute-done((f32[4,3,4,8,128]{4,3,2,1,0:T(8,128)S(1)}, f32[4,3,4,8,128]{4,3,2,1,0:T(8,128)S(1)}, u32[]{:S(2)}, u32[]{:S(2)}) %collective-permute-start.46) | collective-permute-done | bytes 196640 | tf_op jit(solution)/shard_map/ppermute | solution.py:674
  169.8 2.8 %collective-permute-start.43 = (f32[3,128,128]{2,1,0:T(8,128)S(1)}, f32[3,128,128]{2,1,0:T(8,128)S(1)}, u32[]{:S(2)}, u32[]{:S(2)}) collective-permute-start(f32[3,128,128]{2,1,0:T(8,128)S(1)} %bitcast.148), channel_id=1, source_target_pairs={{0,16},{1,17},{4,20},{5,21},{8,24},{9,25},{12,28},{13,29},{16,0},{... | collective-permute-start | bytes 589832 | tf_op jit(solution)/shard_map/ppermute | solution.py:674
  173.0 3.5 %collective-permute-start.45 = (f32[3,128,128]{2,1,0:T(8,128)S(1)}, f32[3,128,128]{2,1,0:T(8,128)S(1)}, u32[]{:S(2)}, u32[]{:S(2)}) collective-permute-start(f32[3,128,128]{2,1,0:T(8,128)S(1)} %bitcast.146), channel_id=1, source_target_pairs={{0,8},{1,9},{4,12},{5,13},{8,0},{9,1},{12,4},{13,5},{16,24},{17,25... | collective-permute-start | bytes 589832 | tf_op jit(solution)/shard_map/ppermute | solution.py:674
  178.5 9.8 %collective-permute-done.43.refs_0_ = f32[3,128,128]{2,1,0:T(8,128)S(1)} collective-permute-done((f32[3,128,128]{2,1,0:T(8,128)S(1)}, f32[3,128,128]{2,1,0:T(8,128)S(1)}, u32[]{:S(2)}, u32[]{:S(2)}) %collective-permute-start.43) | collective-permute-done | bytes 196640 | tf_op jit(solution)/shard_map/ppermute | solution.py:674
  188.3 3.2 %shard_map.125 = f32[3,8,128,128]{3,2,1,0:T(8,128)} custom-call(f32[3,128,128]{2,1,0:T(8,128)S(1)} %collective-permute-done.43.refs_0_, f32[3,128,128]{2,1,0:T(8,128)S(1)} %collective-permute-done.44.refs_1_, f32[3,128,128]{2,1,0:T(8,128)S(1)} %bitcast.95, f32[3,128,128]{2,1,0:T(8,128)S(1)} %collective-permute-done.45.refs_3_, ...), custom_call_target="tpu_custom_call" | custom-call | flops 1 | bytes 1 | tf_op jit(solution)/shard_map/pallas_call | solution.py:457
  (128 shorter events, 69.7 us)
Async XLA Ops:
  7.1 18.3 %collective-permute-start = (f32[3,128,128]{2,1,0:T(8,128)S(1)}, f32[3,128,128]{2,1,0:T(8,128)S(1)}, u32[]{:S(2)}, u32[]{:S(2)}) collective-permute-start(f32[3,128,128]{2,1,0:T(8,128)S(1)} %get-tuple-element.91), channel_id=1, source_target_pairs={{0,16},{1,17},{4,20},{5,21},{8,24},{9,25},{12,28},{13,29},{16,0},{... | collective-permute-start | bytes 589832 | tf_op jit(solution)/shard_map/ppermute | solution.py:674
  11.2 14.2 %collective-permute-start.1 = (f32[3,128,128]{2,1,0:T(8,128)S(1)}, f32[3,128,128]{2,1,0:T(8,128)S(1)}, u32[]{:S(2)}, u32[]{:S(2)}) collective-permute-start(f32[3,128,128]{2,1,0:T(8,128)S(1)} %get-tuple-element.92), channel_id=1, source_target_pairs={{0,24},{1,25},{4,28},{5,29},{8,16},{9,17},{12,20},{13,21},{16,8},{... | collective-permute-start | bytes 589832 | tf_op jit(solution)/shard_map/ppermute | solution.py:674
  12.6 13.4 %collective-permute-start.2 = (f32[3,128,128]{2,1,0:T(8,128)S(1)}, f32[3,128,128]{2,1,0:T(8,128)S(1)}, u32[]{:S(2)}, u32[]{:S(2)}) collective-permute-start(f32[3,128,128]{2,1,0:T(8,128)S(1)} %get-tuple-element.94), channel_id=1, source_target_pairs={{0,8},{1,9},{4,12},{5,13},{8,0},{9,1},{12,4},{13,5},{16,24},{17,25... | collective-permute-start | bytes 589832 | tf_op jit(solution)/shard_map/ppermute | solution.py:674
  28.2 19.3 %collective-permute-start.9 = (f32[4,3,32,128]{3,2,1,0:T(8,128)S(1)}, f32[4,3,32,128]{3,2,1,0:T(8,128)S(1)}, u32[]{:S(2)}, u32[]{:S(2)}) collective-permute-start(f32[4,3,32,128]{3,2,1,0:T(8,128)S(1)} %get-tuple-element.107), channel_id=1, source_target_pairs={{0,16},{1,17},{4,20},{5,21},{8,24},{9,25},{12,28},{13,29},{16,0},{... | collective-permute-start | bytes 589832 | tf_op jit(solution)/shard_map/ppermute | solution.py:674
  34.6 15.5 %collective-permute-start.10 = (f32[4,3,32,128]{3,2,1,0:T(8,128)S(1)}, f32[4,3,32,128]{3,2,1,0:T(8,128)S(1)}, u32[]{:S(2)}, u32[]{:S(2)}) collective-permute-start(f32[4,3,32,128]{3,2,1,0:T(8,128)S(1)} %get-tuple-element.108), channel_id=1, source_target_pairs={{0,24},{1,25},{4,28},{5,29},{8,16},{9,17},{12,20},{13,21},{16,8},{... | collective-permute-start | bytes 589832 | tf_op jit(solution)/shard_map/ppermute | solution.py:674
  35.2 15.0 %collective-permute-start.11 = (f32[4,3,32,128]{3,2,1,0:T(8,128)S(1)}, f32[4,3,32,128]{3,2,1,0:T(8,128)S(1)}, u32[]{:S(2)}, u32[]{:S(2)}) collective-permute-start(f32[4,3,32,128]{3,2,1,0:T(8,128)S(1)} %get-tuple-element.109), channel_id=1, source_target_pairs={{0,8},{1,9},{4,12},{5,13},{8,0},{9,1},{12,4},{13,5},{16,24},{17,25... | collective-permute-start | bytes 589832 | tf_op jit(solution)/shard_map/ppermute | solution.py:674
  37.4 15.1 %collective-permute-start.15 = (f32[3,128,128]{2,1,0:T(8,128)S(1)}, f32[3,128,128]{2,1,0:T(8,128)S(1)}, u32[]{:S(2)}, u32[]{:S(2)}) collective-permute-start(f32[3,128,128]{2,1,0:T(8,128)S(1)} %slice_bitcast_fusion.1), channel_id=1, source_target_pairs={{1,0},{4,1},{5,4},{8,5},{9,8},{12,9},{13,12},{16,13},{17,16},{20,1... | collective-permute-start | bytes 589832 | tf_op jit(solution)/shard_map/ppermute | solution.py:21
  40.1 17.0 %collective-permute-start.16 = (f32[3,128,128]{2,1,0:T(8,128)S(1)}, f32[3,128,128]{2,1,0:T(8,128)S(1)}, u32[]{:S(2)}, u32[]{:S(2)}) collective-permute-start(f32[3,128,128]{2,1,0:T(8,128)S(1)} %fusion), channel_id=1, source_target_pairs={{29,0},{0,1},{1,4},{4,5},{5,8},{8,9},{9,12},{12,13},{13,16},{16,17... | collective-permute-start | bytes 589832 | tf_op jit(solution)/shard_map/ppermute | solution.py:21
  52.5 18.7 %collective-permute-start.20 = (f32[4,3,4,8,128]{4,3,2,1,0:T(8,128)S(1)}, f32[4,3,4,8,128]{4,3,2,1,0:T(8,128)S(1)}, u32[]{:S(2)}, u32[]{:S(2)}) collective-permute-start(f32[4,3,4,8,128]{4,3,2,1,0:T(8,128)S(1)} %get-tuple-element.122), channel_id=1, source_target_pairs={{0,16},{1,17},{4,20},{5,21},{8,24},{9,25},{12,28},{13,29},{16,0},{... | collective-permute-start | bytes 589832 | tf_op jit(solution)/shard_map/ppermute | solution.py:674
  57.0 14.2 %collective-permute-start.21 = (f32[4,3,4,8,128]{4,3,2,1,0:T(8,128)S(1)}, f32[4,3,4,8,128]{4,3,2,1,0:T(8,128)S(1)}, u32[]{:S(2)}, u32[]{:S(2)}) collective-permute-start(f32[4,3,4,8,128]{4,3,2,1,0:T(8,128)S(1)} %get-tuple-element.123), channel_id=1, source_target_pairs={{0,24},{1,25},{4,28},{5,29},{8,16},{9,17},{12,20},{13,21},{16,8},{... | collective-permute-start | bytes 589832 | tf_op jit(solution)/shard_map/ppermute | solution.py:674
  77.3 18.2 %collective-permute-start.17 = (f32[3,128,128]{2,1,0:T(8,128)S(1)}, f32[3,128,128]{2,1,0:T(8,128)S(1)}, u32[]{:S(2)}, u32[]{:S(2)}) collective-permute-start(f32[3,128,128]{2,1,0:T(8,128)S(1)} %bitcast.149), channel_id=1, source_target_pairs={{0,16},{1,17},{4,20},{5,21},{8,24},{9,25},{12,28},{13,29},{16,0},{... | collective-permute-start | bytes 589832 | tf_op jit(solution)/shard_map/ppermute | solution.py:674
  79.2 16.2 %collective-permute-start.19 = (f32[3,128,128]{2,1,0:T(8,128)S(1)}, f32[3,128,128]{2,1,0:T(8,128)S(1)}, u32[]{:S(2)}, u32[]{:S(2)}) collective-permute-start(f32[3,128,128]{2,1,0:T(8,128)S(1)} %bitcast.147), channel_id=1, source_target_pairs={{0,8},{1,9},{4,12},{5,13},{8,0},{9,1},{12,4},{13,5},{16,24},{17,25... | collective-permute-start | bytes 589832 | tf_op jit(solution)/shard_map/ppermute | solution.py:674
  102.9 16.7 %collective-permute-start.26 = (f32[3,128,128]{2,1,0:T(8,128)S(1)}, f32[3,128,128]{2,1,0:T(8,128)S(1)}, u32[]{:S(2)}, u32[]{:S(2)}) collective-permute-start(f32[3,128,128]{2,1,0:T(8,128)S(1)} %get-tuple-element.131), channel_id=1, source_target_pairs={{0,16},{1,17},{4,20},{5,21},{8,24},{9,25},{12,28},{13,29},{16,0},{... | collective-permute-start | bytes 589832 | tf_op jit(solution)/shard_map/ppermute | solution.py:674
  102.9 16.7 %collective-permute-start.27 = (f32[3,128,128]{2,1,0:T(8,128)S(1)}, f32[3,128,128]{2,1,0:T(8,128)S(1)}, u32[]{:S(2)}, u32[]{:S(2)}) collective-permute-start(f32[3,128,128]{2,1,0:T(8,128)S(1)} %get-tuple-element.132), channel_id=1, source_target_pairs={{0,24},{1,25},{4,28},{5,29},{8,16},{9,17},{12,20},{13,21},{16,8},{... | collective-permute-start | bytes 589832 | tf_op jit(solution)/shard_map/ppermute | solution.py:674
  108.5 13.0 %collective-permute-start.28 = (f32[3,128,128]{2,1,0:T(8,128)S(1)}, f32[3,128,128]{2,1,0:T(8,128)S(1)}, u32[]{:S(2)}, u32[]{:S(2)}) collective-permute-start(f32[3,128,128]{2,1,0:T(8,128)S(1)} %get-tuple-element.134), channel_id=1, source_target_pairs={{0,8},{1,9},{4,12},{5,13},{8,0},{9,1},{12,4},{13,5},{16,24},{17,25... | collective-permute-start | bytes 589832 | tf_op jit(solution)/shard_map/ppermute | solution.py:674
  123.8 17.1 %collective-permute-start.35 = (f32[4,3,32,128]{3,2,1,0:T(8,128)S(1)}, f32[4,3,32,128]{3,2,1,0:T(8,128)S(1)}, u32[]{:S(2)}, u32[]{:S(2)}) collective-permute-start(f32[4,3,32,128]{3,2,1,0:T(8,128)S(1)} %get-tuple-element.145), channel_id=1, source_target_pairs={{0,16},{1,17},{4,20},{5,21},{8,24},{9,25},{12,28},{13,29},{16,0},{... | collective-permute-start | bytes 589832 | tf_op jit(solution)/shard_map/ppermute | solution.py:674
  125.9 17.3 %collective-permute-start.36 = (f32[4,3,32,128]{3,2,1,0:T(8,128)S(1)}, f32[4,3,32,128]{3,2,1,0:T(8,128)S(1)}, u32[]{:S(2)}, u32[]{:S(2)}) collective-permute-start(f32[4,3,32,128]{3,2,1,0:T(8,128)S(1)} %get-tuple-element.146), channel_id=1, source_target_pairs={{0,24},{1,25},{4,28},{5,29},{8,16},{9,17},{12,20},{13,21},{16,8},{... | collective-permute-start | bytes 589832 | tf_op jit(solution)/shard_map/ppermute | solution.py:674
  128.5 14.7 %collective-permute-start.37 = (f32[4,3,32,128]{3,2,1,0:T(8,128)S(1)}, f32[4,3,32,128]{3,2,1,0:T(8,128)S(1)}, u32[]{:S(2)}, u32[]{:S(2)}) collective-permute-start(f32[4,3,32,128]{3,2,1,0:T(8,128)S(1)} %get-tuple-element.147), channel_id=1, source_target_pairs={{0,8},{1,9},{4,12},{5,13},{8,0},{9,1},{12,4},{13,5},{16,24},{17,25... | collective-permute-start | bytes 589832 | tf_op jit(solution)/shard_map/ppermute | solution.py:674
  131.8 13.6 %collective-permute-start.41 = (f32[3,128,128]{2,1,0:T(8,128)S(1)}, f32[3,128,128]{2,1,0:T(8,128)S(1)}, u32[]{:S(2)}, u32[]{:S(2)}) collective-permute-start(f32[3,128,128]{2,1,0:T(8,128)S(1)} %get-tuple-element.152), channel_id=1, source_target_pairs={{1,0},{4,1},{5,4},{8,5},{9,8},{12,9},{13,12},{16,13},{17,16},{20,1... | collective-permute-start | bytes 589832 | tf_op jit(solution)/shard_map/ppermute | solution.py:21
  135.1 15.4 %collective-permute-start.42 = (f32[3,128,128]{2,1,0:T(8,128)S(1)}, f32[3,128,128]{2,1,0:T(8,128)S(1)}, u32[]{:S(2)}, u32[]{:S(2)}) collective-permute-start(f32[3,128,128]{2,1,0:T(8,128)S(1)} %get-tuple-element.153), channel_id=1, source_target_pairs={{29,0},{0,1},{1,4},{4,5},{5,8},{8,9},{9,12},{12,13},{13,16},{16,17... | collective-permute-start | bytes 589832 | tf_op jit(solution)/shard_map/ppermute | solution.py:21
  145.5 19.3 %collective-permute-start.46 = (f32[4,3,4,8,128]{4,3,2,1,0:T(8,128)S(1)}, f32[4,3,4,8,128]{4,3,2,1,0:T(8,128)S(1)}, u32[]{:S(2)}, u32[]{:S(2)}) collective-permute-start(f32[4,3,4,8,128]{4,3,2,1,0:T(8,128)S(1)} %get-tuple-element.158), channel_id=1, source_target_pairs={{0,16},{1,17},{4,20},{5,21},{8,24},{9,25},{12,28},{13,29},{16,0},{... | collective-permute-start | bytes 589832 | tf_op jit(solution)/shard_map/ppermute | solution.py:674
  150.6 14.2 %collective-permute-start.47 = (f32[4,3,4,8,128]{4,3,2,1,0:T(8,128)S(1)}, f32[4,3,4,8,128]{4,3,2,1,0:T(8,128)S(1)}, u32[]{:S(2)}, u32[]{:S(2)}) collective-permute-start(f32[4,3,4,8,128]{4,3,2,1,0:T(8,128)S(1)} %get-tuple-element.159), channel_id=1, source_target_pairs={{0,24},{1,25},{4,28},{5,29},{8,16},{9,17},{12,20},{13,21},{16,8},{... | collective-permute-start | bytes 589832 | tf_op jit(solution)/shard_map/ppermute | solution.py:674
  169.8 18.5 %collective-permute-start.43 = (f32[3,128,128]{2,1,0:T(8,128)S(1)}, f32[3,128,128]{2,1,0:T(8,128)S(1)}, u32[]{:S(2)}, u32[]{:S(2)}) collective-permute-start(f32[3,128,128]{2,1,0:T(8,128)S(1)} %bitcast.148), channel_id=1, source_target_pairs={{0,16},{1,17},{4,20},{5,21},{8,24},{9,25},{12,28},{13,29},{16,0},{... | collective-permute-start | bytes 589832 | tf_op jit(solution)/shard_map/ppermute | solution.py:674
  173.0 15.3 %collective-permute-start.45 = (f32[3,128,128]{2,1,0:T(8,128)S(1)}, f32[3,128,128]{2,1,0:T(8,128)S(1)}, u32[]{:S(2)}, u32[]{:S(2)}) collective-permute-start(f32[3,128,128]{2,1,0:T(8,128)S(1)} %bitcast.146), channel_id=1, source_target_pairs={{0,8},{1,9},{4,12},{5,13},{8,0},{9,1},{12,4},{13,5},{16,24},{17,25... | collective-permute-start | bytes 589832 | tf_op jit(solution)/shard_map/ppermute | solution.py:674
  (39 other events, 455.0 us)

commit v3 on v2

--- a/solution.py
+++ b/solution.py
@@ -12,6 +12,10 @@
 TIME_STEP = 0.1
 DAMPING = 0.5
 AXES = ("slab", "pen")
+FAR_ORDER = (3, 1, 2, 0)
+NEAR_ORDER = (2, 3, 1, 0)
+FAR_EXTRA = (0, 1, 1, 1)
+NEAR_EXTRA = (0, 0, 0, 0)
 SCALARS = pl.BlockSpec(memory_space=pltpu.SMEM)
 
 
@@ -284,19 +288,24 @@
                 value = value - mask_ref[0] * pltpu.roll(extra, half - plane, 1)
                 back = pltpu.roll(extra, depth - plane, 1) if plane else extra
                 value = jnp.where(mask_ref[1] > 0.5, back, value)
+                start = component * part * planes + plane
                 for index, out_ref in enumerate(outs[:group]):
-                    out_ref[component, pl.ds(plane, part, stride=planes), :] = value[
+                    out_ref[pl.ds(start, part, stride=planes), :] = value[
                         index * part : (index + 1) * part
                     ]
             outs = outs[group:]
 
 
-def middle_kernel(start, inner, kernel_ref, weight_ref, table_ref, inverse_ref, *refs):
-    in_refs, out_refs = in_order(refs[:inner]), refs[inner:]
-    outer, _, rows, planes, depth = in_refs[0].shape
+def middle_kernel(start, rows, inner, planes, kernel_ref, weight_ref, table_ref, inverse_ref, *refs):
+    in_refs, out_refs = refs[:inner], refs[inner:]
+    count, depth = table_ref.shape[0], weight_ref.shape[1]
     half = depth // 2
-    count = inner * outer * planes
+    outer = count // (inner * planes)
     row_block = kernel_ref.shape[1] // count
+
+    def places(component, row):
+        return [((far * 3 + component) * rows + row) * planes for far in range(outer)]
+
     lane = lane_index((count, depth))
     signs = jnp.where(lane < half, 1.0, -1.0)
     order = ((0, 3, 4), (3, 1, 5), (4, 5, 2))
@@ -306,7 +315,12 @@
         edge = start + row == 0
         for component in range(3):
             block = jnp.concatenate(
-                [ref[:, component, row].reshape(outer * planes, depth) for ref in in_refs], axis=0
+                [
+                    ref[place : place + planes, :]
+                    for ref in in_refs
+                    for place in places(component, row)
+                ],
+                axis=0,
             )
             turned = turn(block)
             columns.append(stacked_parts(jnp.concatenate([block, turned * signs], axis=0)))
@@ -339,18 +353,18 @@
         for component in range(3):
             value = mixed[:, component * depth : (component + 1) * depth]
             for index, out_ref in enumerate(out_refs):
-                size = outer * planes
-                out_ref[:, component, row] = value[index * size : (index + 1) * size].reshape(
-                    outer, planes, depth
-                )
+                for far, place in enumerate(places(component, row)):
+                    begin = (index * outer + far) * planes
+                    out_ref[place : place + planes, :] = value[begin : begin + planes]
 
 
 def gathered_columns(component, in_refs, mask_ref, table_ref, planes):
-    part = in_refs[0].shape[1] // planes
+    part = mask_ref.shape[1] // len(in_refs)
     columns = []
     for plane in range(planes):
+        start = component * part * planes + plane
         value = jnp.concatenate(
-            [ref[component, pl.ds(plane, part, stride=planes), :] for ref in in_refs], axis=0
+            [ref[pl.ds(start, part, stride=planes), :] for ref in in_refs], axis=0
         )
         turned = turn(value)
         top = value * mask_ref[0] + turned * mask_ref[1]
@@ -360,7 +374,7 @@
 
 
 def backward_kernel(table_ref, mask_ref, *refs):
-    in_refs, out_ref = in_order(refs[:-1]), refs[-1]
+    in_refs, out_ref = refs[:-1], refs[-1]
     _, planes, _, depth = out_ref.shape
     for component in range(3):
         mixed = gathered_columns(component, in_refs, mask_ref, table_ref, planes)
@@ -385,7 +399,7 @@
 
 def advance_kernel(edges, *refs):
     refs, (out_ref, *edge_refs, dipole_ref) = refs[: -2 - 2 * edges], refs[-2 - 2 * edges :]
-    in_refs, refs = in_order(refs[:-7]), refs[-7:]
+    in_refs, refs = refs[:-7], refs[-7:]
     table_ref, mask_ref, depth_ref, partial_ref, local_ref, field_ref, bond_ref = refs
     _, planes, width, depth = out_ref.shape
     for component in range(3):
@@ -444,27 +458,32 @@
             )
 
 
-def call(kernel, outs, operands, scratch=(), specs=None, out_specs=None, before=(), after=(), mib=16):
+def call(
+    kernel, outs, operands, scratch=(), specs=None, out_specs=None, lead=(), before=(), after=(), mib=16
+):
     specs = {} if specs is None else specs
     out_specs = {} if out_specs is None else out_specs
     whole = pl.BlockSpec(memory_space=pltpu.VMEM)
     unread = pl.BlockSpec(memory_space=pl.ANY)
+    count = len(operands)
+    order = [*lead, *(i for i in range(count) if i not in lead)]
 
     def body(*refs):
         refs = refs[len(before) :]
-        kernel(*refs[: len(operands)], *refs[len(operands) + len(after) :])
+        taken = dict(zip(order, refs))
+        kernel(*(taken[i] for i in range(count)), *refs[count + len(after) :])
 
     return pl.pallas_call(
         body,
         out_shape=list(outs),
         in_specs=[unread] * len(before)
-        + [specs.get(i, whole) for i in range(len(operands))]
+        + [specs.get(i, whole) for i in order]
         + [unread] * len(after),
         out_specs=[out_specs.get(i, whole) for i in range(len(outs))],
         scratch_shapes=list(scratch),
         cost_estimate=pl.CostEstimate(flops=1, bytes_accessed=1, transcendentals=0),
         compiler_params=pltpu.CompilerParams(vmem_limit_bytes=mib * 1024 * 1024),
-    )(*before, *operands, *after)
+    )(*before, *(operands[i] for i in order), *after)
 
 
 def shape_of(*shape, dtype=jnp.float32):
@@ -583,33 +602,23 @@
         weight_ref[index : index + 1, :] = kind
 
 
-def visiting(count):
-    return sorted(range(count), key=lambda i: (i < count // 2, i))
-
-
-def in_order(refs):
-    ordered = [None] * len(refs)
-    for place, ref in zip(visiting(len(refs)), refs):
-        ordered[place] = ref
-    return ordered
-
-
-def leaving(blocks):
-    return [blocks[i] for i in visiting(len(blocks))]
-
-
-def repack_forward(count, *refs):
-    in_refs, out_refs = in_order(refs[:count]), refs[count:]
+def repack_forward(count, unit, *refs):
+    in_refs, out_refs = refs[:count], refs[count:]
+    outs = len(out_refs)
     for out_index, out_ref in enumerate(out_refs):
         for in_index, in_ref in enumerate(in_refs):
-            out_ref[in_index] = in_ref[:, out_index]
-
-
-def repack_backward(count, *refs):
-    in_refs, out_refs = in_order(refs[:count]), refs[count:]
+            for component in range(3):
+                place, start = (in_index * 3 + component) * unit, (component * outs + out_index) * unit
+                out_ref[place : place + unit, :] = in_ref[start : start + unit, :]
+
+
+def repack_backward(count, unit, *refs):
+    in_refs, out_refs = refs[:count], refs[count:]
     for out_index, out_ref in enumerate(out_refs):
         for in_index, in_ref in enumerate(in_refs):
-            out_ref[:, in_index] = in_ref[out_index]
+            for component in range(3):
+                place, start = (component * count + in_index) * unit, (out_index * 3 + component) * unit
+                out_ref[place : place + unit, :] = in_ref[start : start + unit, :]
 
 
 def depth_tables(depth):
@@ -667,58 +676,52 @@
     def exchange(blocks, stage):
         size, stride = stage
         moved = list(blocks)
-        for index in leaving(range(size)):
-            if not index:
-                continue
+        for index in range(1, size):
             distance = index * stride
             moved[index] = lax.ppermute(
                 blocks[index], AXES, [(i, i ^ distance) for i in range(count)]
             )
         return moved
 
+    unit = rows * planes
+
+    def waits(stage, place=0):
+        order = FAR_ORDER if stage is far else NEAR_ORDER
+        return [place + i for i in (order if len(order) == stage[0] else range(stage[0]))]
+
+    def blocks_of(stage):
+        size = 3 * (count // stage[0]) * unit
+        extras = FAR_EXTRA if stage is far else NEAR_EXTRA
+        return [shape_of(size + (extras[i] if i < len(extras) else 0), depth) for i in range(stage[0])]
+
     def forward_part(field):
         groups = [route.first[0] for route in routes]
-        outs = []
-        for route in routes:
-            shape = shape_of(3, route.second[0] * rows * planes, depth)
-            outs += [shape] * route.first[0]
         blocks = call(
             functools.partial(forward_kernel, groups),
-            outs,
+            blocks_of(routes[0].first) + blocks_of(routes[1].first),
             [field, into_depth, *forward],
         )
         return blocks[: groups[0]], blocks[groups[0] :]
 
     def forward_repack(chunk, blocks, **order):
-        first, second = routes[chunk].first[0], routes[chunk].second[0]
+        first, second = routes[chunk].first, routes[chunk].second
+        kernel_of = functools.partial(repack_forward, first[0], unit)
+        return call(kernel_of, blocks_of(second), blocks, lead=waits(first), **order)
+
+    def middle_part(chunk, blocks, **order):
+        second = routes[chunk].second
         return call(
-            functools.partial(repack_forward, first),
-            [shape_of(first, 3, rows * planes, depth)] * second,
-            [block.reshape(3, second, rows * planes, depth) for block in leaving(blocks)],
+            functools.partial(middle_kernel, routes[chunk].start, rows, second[0], planes),
+            blocks_of(second),
+            [kernel_rows, weights, *others[chunk][:2]] + list(blocks),
+            lead=waits(second, 4),
             **order,
         )
 
-    def middle_part(chunk, blocks, **order):
-        first, second = routes[chunk].first[0], routes[chunk].second[0]
-        into_first, out_of_first = others[chunk][:2]
-        shape = shape_of(first, 3, rows, planes, depth)
-        return call(
-            functools.partial(middle_kernel, routes[chunk].start, second),
-            [shape] * second,
-            [kernel_rows, weights, into_first, out_of_first]
-            + [block.reshape(shape.shape) for block in leaving(blocks)],
-            **order,
-        )
-
     def backward_repack(chunk, blocks, **order):
-        first, second = routes[chunk].first[0], routes[chunk].second[0]
-        blocks = call(
-            functools.partial(repack_backward, second),
-            [shape_of(3, second, rows * planes, depth)] * first,
-            [block.reshape(first, 3, rows * planes, depth) for block in leaving(blocks)],
-            **order,
-        )
-        return [block.reshape(3, -1, depth) for block in blocks]
+        first, second = routes[chunk].first, routes[chunk].second
+        kernel_of = functools.partial(repack_backward, second[0], unit)
+        return call(kernel_of, blocks_of(first), blocks, lead=waits(second), **order)
 
     first_plane = field[:, 0]
     carried = couplings[0, -1].astype(jnp.float32) * field[:, -1]
@@ -727,7 +730,7 @@
         a_far = exchange(a_out, far)
         b_near = exchange(b_out, near)
         b_packed = forward_repack(1, b_near)
-        a_packed = forward_repack(0, a_far, after=b_packed[:1])
+        a_packed = forward_repack(0, a_far)
         b_far = exchange(b_packed, far)
         a_near = exchange(a_packed, near)
         a_mid = middle_part(0, a_near)
@@ -736,7 +739,7 @@
         below = shifted(carried, AXES, 1)
         b_back = exchange(b_mid, far)
         a_back = exchange(a_mid, near)
-        a_home = backward_repack(0, a_back, before=b_mid[:1], after=[above, below])
+        a_home = backward_repack(0, a_back, after=[above, below])
         b_home = backward_repack(1, b_back, before=a_home[:1])
         a_done = exchange(a_home, far)
         b_done = exchange(b_home, near)
@@ -751,15 +754,17 @@
         (sums,) = call(
             backward_kernel,
             [whole],
-            [others[1][2], others[1][3]] + leaving(b_done),
+            [others[1][2], others[1][3]] + b_done,
+            lead=waits(near, 2),
             after=[local],
         )
         edges = step == 0
         field, *planes_out = call(
             functools.partial(advance_kernel, edges),
             [whole] + [plane_shape] * 2 * edges,
-            leaving(a_done)
+            a_done
             + [others[0][2], others[0][3], out_of_depth, sums, local, field, couplings[:1, -1:]],
+            lead=waits(far),
             scratch=[pltpu.VMEM(whole.shape, jnp.float32)],
         )
         if edges:

time: 192 us -> 177 us (0.922)
  starting transfers between devices: 80.9 us -> 53.4 us
  waiting for transfers between devices: 76.1 us -> 88.2 us
    ppermute x48, starting transfers between devices: 74.9 us -> 47.4 us  [exchange(): lax.ppermute(blocks[index], AXES, [(i, i ^ distance) for i in range(count)])]
    ppermute x48, waiting for transfers between devices: 76.1 us -> 88.2 us  [exchange(): lax.ppermute(blocks[index], AXES, [(i, i ^ distance) for i in range(count)])]
  transfers between devices with their start and end apart: 52 -> 52, of which waited for: 17 -> 25; matrix products, arithmetic and copies ran while one was open for 1% -> 1% of each run, Pallas kernels for 8% -> 9%
where the time goes in v3:
time: 177 us
  waiting for transfers between devices  88.2 us (50%)
  starting transfers between devices  53.4 us (30%)
  Pallas kernels  29.5 us (17%)
  local copies, waits for them, and re-layouts  3.28 us (2%)
  other arithmetic  1.79 us (1%)
    ppermute x48, waiting for transfers between devices, exchange(): lax.ppermute(blocks[index], AXES, [(i, i ^ distance) for i in range(count)])  88.2 us
    ppermute x48, starting transfers between devices, exchange(): lax.ppermute(blocks[index], AXES, [(i, i ^ distance) for i in range(count)])  47.4 us
    pallas_call x22, Pallas kernels, call(): pl.pallas_call(body, out_shape=list(outs), in_specs=[unread] * len(before...  29.5 us
    ppermute x4, starting transfers between devices, shifted(): return lax.ppermute(block, axis, route)  5.96 us
  transfers between devices with their start and end apart: 52, of which 25 were waited for; matrix products, arithmetic and copies ran while one was open for 1% of the time, Pallas kernels for 9%

profile of v3, /device:TPU:0, one launch (start us, length us, event | category | flops | bytes accessed | tf_op | source)
XLA Modules:
  0.0 177.2 jit_solution(12408106781470627835)
XLA Ops:
  3.9 3.2 %shard_map.105 = (f32[384,128]{1,0:T(8,128)S(1)}, f32[385,128]{1,0:T(8,128)S(1)}, f32[385,128]{1,0:T(8,128)S(1)}, f32[385,128]{1,0:T(8,128)S(1)}, f32[384,128]{1...) custom-call(f32[3,8,128,128]{3,2,1,0:T(8,128)S(1)} %bitcast.21, ...), custom_call_target="tpu_custom_call" | custom-call | flops 1 | bytes 1 | tf_op jit(solution)/shard_map/pallas_call | solution.py:476
  7.1 3.0 %collective-permute-start.14 = (f32[384,128]{1,0:T(8,128)S(1)}, f32[384,128]{1,0:T(8,128)S(1)}, u32[]{:S(2)}, u32[]{:S(2)}) collective-permute-start(f32[384,128]{1,0:T(8,128)S(1)} %get-tuple-element.109), channel_id=1, source_target_pairs={{0,4},{1,5},{4,0},{5,1},{8,12},{9,13},{12,8},{13,9},{16,20},{17,21... | collective-permute-start | bytes 589832 | tf_op jit(solution)/shard_map/ppermute | solution.py:681
  10.2 3.6 %collective-permute-start = (f32[385,128]{1,0:T(8,128)S(1)}, f32[385,128]{1,0:T(8,128)S(1)}, u32[]{:S(2)}, u32[]{:S(2)}) collective-permute-start(f32[385,128]{1,0:T(8,128)S(1)} %get-tuple-element.88), channel_id=1, source_target_pairs={{0,24},{1,25},{4,28},{5,29},{8,16},{9,17},{12,20},{13,21},{16,8},{... | collective-permute-start | bytes 591368 | tf_op jit(solution)/shard_map/ppermute | solution.py:681
  15.3 4.6 %collective-permute-done.refs_0_ = f32[385,128]{1,0:T(8,128)S(1)} collective-permute-done((f32[385,128]{1,0:T(8,128)S(1)}, f32[385,128]{1,0:T(8,128)S(1)}, u32[]{:S(2)}, u32[]{:S(2)}) %collective-permute-start) | collective-permute-done | bytes 197152 | tf_op jit(solution)/shard_map/ppermute | solution.py:681
  19.9 5.0 %collective-permute-done.1.refs_1_ = f32[385,128]{1,0:T(8,128)S(1)} collective-permute-done((f32[385,128]{1,0:T(8,128)S(1)}, f32[385,128]{1,0:T(8,128)S(1)}, u32[]{:S(2)}, u32[]{:S(2)}) %collective-permute-start.1) | collective-permute-done | bytes 197152 | tf_op jit(solution)/shard_map/ppermute | solution.py:681
  25.0 6.6 %collective-permute-done.2.refs_2_ = f32[385,128]{1,0:T(8,128)S(1)} collective-permute-done((f32[385,128]{1,0:T(8,128)S(1)}, f32[385,128]{1,0:T(8,128)S(1)}, u32[]{:S(2)}, u32[]{:S(2)}) %collective-permute-start.2) | collective-permute-done | bytes 197152 | tf_op jit(solution)/shard_map/ppermute | solution.py:681
  55.4 3.4 %collective-permute-start.20 = (f32[385,128]{1,0:T(8,128)S(1)}, f32[385,128]{1,0:T(8,128)S(1)}, u32[]{:S(2)}, u32[]{:S(2)}) collective-permute-start(f32[385,128]{1,0:T(8,128)S(1)} %get-tuple-element.119), channel_id=1, source_target_pairs={{0,24},{1,25},{4,28},{5,29},{8,16},{9,17},{12,20},{13,21},{16,8},{... | collective-permute-start | bytes 591368 | tf_op jit(solution)/shard_map/ppermute | solution.py:681
  60.2 5.9 %collective-permute-done.7.refs_1_ = f32[384,128]{1,0:T(8,128)S(1)} collective-permute-done((f32[384,128]{1,0:T(8,128)S(1)}, f32[384,128]{1,0:T(8,128)S(1)}, u32[]{:S(2)}, u32[]{:S(2)}) %collective-permute-start.7) | collective-permute-done | bytes 196640 | tf_op jit(solution)/shard_map/ppermute | solution.py:681
  66.2 4.8 %collective-permute-done.21.refs_2_ = f32[385,128]{1,0:T(8,128)S(1)} collective-permute-done((f32[385,128]{1,0:T(8,128)S(1)}, f32[385,128]{1,0:T(8,128)S(1)}, u32[]{:S(2)}, u32[]{:S(2)}) %collective-permute-start.21) | collective-permute-done | bytes 197152 | tf_op jit(solution)/shard_map/ppermute | solution.py:681
  71.0 3.1 %collective-permute-done.22.refs_3_ = f32[385,128]{1,0:T(8,128)S(1)} collective-permute-done((f32[385,128]{1,0:T(8,128)S(1)}, f32[385,128]{1,0:T(8,128)S(1)}, u32[]{:S(2)}, u32[]{:S(2)}) %collective-permute-start.22) | collective-permute-done | bytes 197152 | tf_op jit(solution)/shard_map/ppermute | solution.py:681
  82.4 3.1 %collective-permute-done.24.refs_1_ = f32[384,128]{1,0:T(8,128)S(1)} collective-permute-done((f32[384,128]{1,0:T(8,128)S(1)}, f32[384,128]{1,0:T(8,128)S(1)}, u32[]{:S(2)}, u32[]{:S(2)}) %collective-permute-start.24) | collective-permute-done | bytes 196640 | tf_op jit(solution)/shard_map/ppermute | solution.py:681
  87.5 5.2 %collective-permute-done.13.refs_2_ = f32[385,128]{1,0:T(8,128)S(1)} collective-permute-done((f32[385,128]{1,0:T(8,128)S(1)}, f32[385,128]{1,0:T(8,128)S(1)}, u32[]{:S(2)}, u32[]{:S(2)}) %collective-permute-start.13) | collective-permute-done | bytes 197152 | tf_op jit(solution)/shard_map/ppermute | solution.py:681
  94.9 3.3 %shard_map.116 = (f32[384,128]{1,0:T(8,128)S(1)}, f32[385,128]{1,0:T(8,128)S(1)}, f32[385,128]{1,0:T(8,128)S(1)}, f32[385,128]{1,0:T(8,128)S(1)}, f32[384,128]{1...) custom-call(f32[3,8,128,128]{3,2,1,0:T(8,128)S(1)} %get-tuple-element.130.refs_0_.refs_2_.re, ...), custom_call_target="tpu_custom_call" | custom-call | flops 1 | bytes 1 | tf_op jit(solution)/shard_map/pallas_call | solution.py:476
  104.0 4.0 %collective-permute-done.26.refs_0_ = f32[385,128]{1,0:T(8,128)S(1)} collective-permute-done((f32[385,128]{1,0:T(8,128)S(1)}, f32[385,128]{1,0:T(8,128)S(1)}, u32[]{:S(2)}, u32[]{:S(2)}) %collective-permute-start.26) | collective-permute-done | bytes 197152 | tf_op jit(solution)/shard_map/ppermute | solution.py:681
  108.0 4.3 %collective-permute-done.27.refs_1_ = f32[385,128]{1,0:T(8,128)S(1)} collective-permute-done((f32[385,128]{1,0:T(8,128)S(1)}, f32[385,128]{1,0:T(8,128)S(1)}, u32[]{:S(2)}, u32[]{:S(2)}) %collective-permute-start.27) | collective-permute-done | bytes 197152 | tf_op jit(solution)/shard_map/ppermute | solution.py:681
  112.3 3.8 %collective-permute-done.28.refs_2_ = f32[385,128]{1,0:T(8,128)S(1)} collective-permute-done((f32[385,128]{1,0:T(8,128)S(1)}, f32[385,128]{1,0:T(8,128)S(1)}, u32[]{:S(2)}, u32[]{:S(2)}) %collective-permute-start.28) | collective-permute-done | bytes 197152 | tf_op jit(solution)/shard_map/ppermute | solution.py:681
  122.9 3.2 %collective-permute-done.30.refs_1_ = f32[384,128]{1,0:T(8,128)S(1)} collective-permute-done((f32[384,128]{1,0:T(8,128)S(1)}, f32[384,128]{1,0:T(8,128)S(1)}, u32[]{:S(2)}, u32[]{:S(2)}) %collective-permute-start.30) | collective-permute-done | bytes 196640 | tf_op jit(solution)/shard_map/ppermute | solution.py:681
  136.8 5.0 %collective-permute-start.46 = (f32[385,128]{1,0:T(8,128)S(1)}, f32[385,128]{1,0:T(8,128)S(1)}, u32[]{:S(2)}, u32[]{:S(2)}) collective-permute-start(f32[385,128]{1,0:T(8,128)S(1)} %get-tuple-element.157), channel_id=1, source_target_pairs={{0,24},{1,25},{4,28},{5,29},{8,16},{9,17},{12,20},{13,21},{16,8},{... | collective-permute-start | bytes 591368 | tf_op jit(solution)/shard_map/ppermute | solution.py:681
  144.5 4.8 %collective-permute-done.33.refs_1_ = f32[384,128]{1,0:T(8,128)S(1)} collective-permute-done((f32[384,128]{1,0:T(8,128)S(1)}, f32[384,128]{1,0:T(8,128)S(1)}, u32[]{:S(2)}, u32[]{:S(2)}) %collective-permute-start.33) | collective-permute-done | bytes 196640 | tf_op jit(solution)/shard_map/ppermute | solution.py:681
  149.4 3.2 %collective-permute-done.47.refs_2_ = f32[385,128]{1,0:T(8,128)S(1)} collective-permute-done((f32[385,128]{1,0:T(8,128)S(1)}, f32[385,128]{1,0:T(8,128)S(1)}, u32[]{:S(2)}, u32[]{:S(2)}) %collective-permute-start.47) | collective-permute-done | bytes 197152 | tf_op jit(solution)/shard_map/ppermute | solution.py:681
  152.5 4.3 %collective-permute-done.48.refs_3_ = f32[385,128]{1,0:T(8,128)S(1)} collective-permute-done((f32[385,128]{1,0:T(8,128)S(1)}, f32[385,128]{1,0:T(8,128)S(1)}, u32[]{:S(2)}, u32[]{:S(2)}) %collective-permute-start.48) | collective-permute-done | bytes 197152 | tf_op jit(solution)/shard_map/ppermute | solution.py:681
  165.0 3.3 %collective-permute-done.50.refs_1_ = f32[384,128]{1,0:T(8,128)S(1)} collective-permute-done((f32[384,128]{1,0:T(8,128)S(1)}, f32[384,128]{1,0:T(8,128)S(1)}, u32[]{:S(2)}, u32[]{:S(2)}) %collective-permute-start.50) | collective-permute-done | bytes 196640 | tf_op jit(solution)/shard_map/ppermute | solution.py:681
  169.0 4.8 %collective-permute-done.39.refs_2_ = f32[385,128]{1,0:T(8,128)S(1)} collective-permute-done((f32[385,128]{1,0:T(8,128)S(1)}, f32[385,128]{1,0:T(8,128)S(1)}, u32[]{:S(2)}, u32[]{:S(2)}) %collective-permute-start.39) | collective-permute-done | bytes 197152 | tf_op jit(solution)/shard_map/ppermute | solution.py:681
  173.8 3.4 %shard_map.125 = f32[3,8,128,128]{3,2,1,0:T(8,128)} custom-call(f32[385,128]{1,0:T(8,128)S(1)} %collective-permute-done.37.refs_0_, f32[385,128]{1,0:T(8,128)S(1)} %collective-permute-done.38.refs_1_, f32[385,128]{1,0:T(8,128)S(1)} %collective-permute-done.39.refs_2_, f32[384,128]{1,0:T(8,128)S(1)} %get-tuple-element.148.refs_0_.refs_3_, ...), custom_call_target="tpu_custom_call" | custom-call | flops 1 | bytes 1 | tf_op jit(solution)/shard_map/pallas_call | solution.py:476
  (128 shorter events, 77.2 us)
Async XLA Ops:
  7.1 27.1 %collective-permute-start.14 = (f32[384,128]{1,0:T(8,128)S(1)}, f32[384,128]{1,0:T(8,128)S(1)}, u32[]{:S(2)}, u32[]{:S(2)}) collective-permute-start(f32[384,128]{1,0:T(8,128)S(1)} %get-tuple-element.109), channel_id=1, source_target_pairs={{0,4},{1,5},{4,0},{5,1},{8,12},{9,13},{12,8},{13,9},{16,20},{17,21... | collective-permute-start | bytes 589832 | tf_op jit(solution)/shard_map/ppermute | solution.py:681
  10.2 24.0 %collective-permute-start.15 = (f32[384,128]{1,0:T(8,128)S(1)}, f32[384,128]{1,0:T(8,128)S(1)}, u32[]{:S(2)}, u32[]{:S(2)}) collective-permute-start(f32[384,128]{1,0:T(8,128)S(1)} %get-tuple-element.110), channel_id=1, source_target_pairs={{0,5},{1,4},{4,1},{5,0},{8,13},{9,12},{12,9},{13,8},{16,21},{17,20... | collective-permute-start | bytes 589832 | tf_op jit(solution)/shard_map/ppermute | solution.py:681
  13.8 17.8 %collective-permute-start.2 = (f32[385,128]{1,0:T(8,128)S(1)}, f32[385,128]{1,0:T(8,128)S(1)}, u32[]{:S(2)}, u32[]{:S(2)}) collective-permute-start(f32[385,128]{1,0:T(8,128)S(1)} %get-tuple-element.90), channel_id=1, source_target_pairs={{0,16},{1,17},{4,20},{5,21},{8,24},{9,25},{12,28},{13,29},{16,0},{... | collective-permute-start | bytes 591368 | tf_op jit(solution)/shard_map/ppermute | solution.py:681
  19.9 14.3 %collective-permute-start.16 = (f32[384,128]{1,0:T(8,128)S(1)}, f32[384,128]{1,0:T(8,128)S(1)}, u32[]{:S(2)}, u32[]{:S(2)}) collective-permute-start(f32[384,128]{1,0:T(8,128)S(1)} %get-tuple-element.111), channel_id=1, source_target_pairs={{0,1},{1,0},{4,5},{5,4},{8,9},{9,8},{12,13},{13,12},{16,17},{17,16... | collective-permute-start | bytes 589832 | tf_op jit(solution)/shard_map/ppermute | solution.py:681
  34.3 16.2 %collective-permute-start.17 = (f32[385,128]{1,0:T(8,128)S(1)}, f32[385,128]{1,0:T(8,128)S(1)}, u32[]{:S(2)}, u32[]{:S(2)}) collective-permute-start(f32[385,128]{1,0:T(8,128)S(1)} %get-tuple-element.113), channel_id=1, source_target_pairs={{0,24},{1,25},{4,28},{5,29},{8,16},{9,17},{12,20},{13,21},{16,8},{... | collective-permute-start | bytes 591368 | tf_op jit(solution)/shard_map/ppermute | solution.py:681
  36.9 13.7 %collective-permute-start.18 = (f32[385,128]{1,0:T(8,128)S(1)}, f32[385,128]{1,0:T(8,128)S(1)}, u32[]{:S(2)}, u32[]{:S(2)}) collective-permute-start(f32[385,128]{1,0:T(8,128)S(1)} %get-tuple-element.114), channel_id=1, source_target_pairs={{0,8},{1,9},{4,12},{5,13},{8,0},{9,1},{12,4},{13,5},{16,24},{17,25... | collective-permute-start | bytes 591368 | tf_op jit(solution)/shard_map/ppermute | solution.py:681
  36.9 16.3 %collective-permute-start.19 = (f32[385,128]{1,0:T(8,128)S(1)}, f32[385,128]{1,0:T(8,128)S(1)}, u32[]{:S(2)}, u32[]{:S(2)}) collective-permute-start(f32[385,128]{1,0:T(8,128)S(1)} %get-tuple-element.115), channel_id=1, source_target_pairs={{0,16},{1,17},{4,20},{5,21},{8,24},{9,25},{12,28},{13,29},{16,0},{... | collective-permute-start | bytes 591368 | tf_op jit(solution)/shard_map/ppermute | solution.py:681
  45.1 13.7 %collective-permute-start.9 = (f32[3,128,128]{2,1,0:T(8,128)S(1)}, f32[3,128,128]{2,1,0:T(8,128)S(1)}, u32[]{:S(2)}, u32[]{:S(2)}) collective-permute-start(f32[3,128,128]{2,1,0:T(8,128)S(1)} %slice_bitcast_fusion.1), channel_id=1, source_target_pairs={{1,0},{4,1},{5,4},{8,5},{9,8},{12,9},{13,12},{16,13},{17,16},{20,1... | collective-permute-start | bytes 589832 | tf_op jit(solution)/shard_map/ppermute | solution.py:25
  58.8 12.2 %collective-permute-start.21 = (f32[385,128]{1,0:T(8,128)S(1)}, f32[385,128]{1,0:T(8,128)S(1)}, u32[]{:S(2)}, u32[]{:S(2)}) collective-permute-start(f32[385,128]{1,0:T(8,128)S(1)} %get-tuple-element.120), channel_id=1, source_target_pairs={{0,8},{1,9},{4,12},{5,13},{8,0},{9,1},{12,4},{13,5},{16,24},{17,25... | collective-permute-start | bytes 591368 | tf_op jit(solution)/shard_map/ppermute | solution.py:681
  58.8 15.2 %collective-permute-start.22 = (f32[385,128]{1,0:T(8,128)S(1)}, f32[385,128]{1,0:T(8,128)S(1)}, u32[]{:S(2)}, u32[]{:S(2)}) collective-permute-start(f32[385,128]{1,0:T(8,128)S(1)} %get-tuple-element.121), channel_id=1, source_target_pairs={{0,16},{1,17},{4,20},{5,21},{8,24},{9,25},{12,28},{13,29},{16,0},{... | collective-permute-start | bytes 591368 | tf_op jit(solution)/shard_map/ppermute | solution.py:681
  74.2 12.0 %collective-permute-start.11 = (f32[385,128]{1,0:T(8,128)S(1)}, f32[385,128]{1,0:T(8,128)S(1)}, u32[]{:S(2)}, u32[]{:S(2)}) collective-permute-start(f32[385,128]{1,0:T(8,128)S(1)} %get-tuple-element.103), channel_id=1, source_target_pairs={{0,24},{1,25},{4,28},{5,29},{8,16},{9,17},{12,20},{13,21},{16,8},{... | collective-permute-start | bytes 591368 | tf_op jit(solution)/shard_map/ppermute | solution.py:681
  75.9 16.7 %collective-permute-start.13 = (f32[385,128]{1,0:T(8,128)S(1)}, f32[385,128]{1,0:T(8,128)S(1)}, u32[]{:S(2)}, u32[]{:S(2)}) collective-permute-start(f32[385,128]{1,0:T(8,128)S(1)} %get-tuple-element.105), channel_id=1, source_target_pairs={{0,16},{1,17},{4,20},{5,21},{8,24},{9,25},{12,28},{13,29},{16,0},{... | collective-permute-start | bytes 591368 | tf_op jit(solution)/shard_map/ppermute | solution.py:681
  100.9 15.3 %collective-permute-start.28 = (f32[385,128]{1,0:T(8,128)S(1)}, f32[385,128]{1,0:T(8,128)S(1)}, u32[]{:S(2)}, u32[]{:S(2)}) collective-permute-start(f32[385,128]{1,0:T(8,128)S(1)} %get-tuple-element.133), channel_id=1, source_target_pairs={{0,16},{1,17},{4,20},{5,21},{8,24},{9,25},{12,28},{13,29},{16,0},{... | collective-permute-start | bytes 591368 | tf_op jit(solution)/shard_map/ppermute | solution.py:681
  102.6 15.4 %collective-permute-start.40 = (f32[384,128]{1,0:T(8,128)S(1)}, f32[384,128]{1,0:T(8,128)S(1)}, u32[]{:S(2)}, u32[]{:S(2)}) collective-permute-start(f32[384,128]{1,0:T(8,128)S(1)} %get-tuple-element.149), channel_id=1, source_target_pairs={{0,4},{1,5},{4,0},{5,1},{8,12},{9,13},{12,8},{13,9},{16,20},{17,21... | collective-permute-start | bytes 589832 | tf_op jit(solution)/shard_map/ppermute | solution.py:681
  104.0 14.0 %collective-permute-start.41 = (f32[384,128]{1,0:T(8,128)S(1)}, f32[384,128]{1,0:T(8,128)S(1)}, u32[]{:S(2)}, u32[]{:S(2)}) collective-permute-start(f32[384,128]{1,0:T(8,128)S(1)} %get-tuple-element.150), channel_id=1, source_target_pairs={{0,5},{1,4},{4,1},{5,0},{8,13},{9,12},{12,9},{13,8},{16,21},{17,20... | collective-permute-start | bytes 589832 | tf_op jit(solution)/shard_map/ppermute | solution.py:681
  118.1 13.3 %collective-permute-start.43 = (f32[385,128]{1,0:T(8,128)S(1)}, f32[385,128]{1,0:T(8,128)S(1)}, u32[]{:S(2)}, u32[]{:S(2)}) collective-permute-start(f32[385,128]{1,0:T(8,128)S(1)} %get-tuple-element.153), channel_id=1, source_target_pairs={{0,24},{1,25},{4,28},{5,29},{8,16},{9,17},{12,20},{13,21},{16,8},{... | collective-permute-start | bytes 591368 | tf_op jit(solution)/shard_map/ppermute | solution.py:681
  119.7 13.1 %collective-permute-start.44 = (f32[385,128]{1,0:T(8,128)S(1)}, f32[385,128]{1,0:T(8,128)S(1)}, u32[]{:S(2)}, u32[]{:S(2)}) collective-permute-start(f32[385,128]{1,0:T(8,128)S(1)} %get-tuple-element.154), channel_id=1, source_target_pairs={{0,8},{1,9},{4,12},{5,13},{8,0},{9,1},{12,4},{13,5},{16,24},{17,25... | collective-permute-start | bytes 591368 | tf_op jit(solution)/shard_map/ppermute | solution.py:681
  122.2 12.4 %collective-permute-start.45 = (f32[385,128]{1,0:T(8,128)S(1)}, f32[385,128]{1,0:T(8,128)S(1)}, u32[]{:S(2)}, u32[]{:S(2)}) collective-permute-start(f32[385,128]{1,0:T(8,128)S(1)} %get-tuple-element.155), channel_id=1, source_target_pairs={{0,16},{1,17},{4,20},{5,21},{8,24},{9,25},{12,28},{13,29},{16,0},{... | collective-permute-start | bytes 591368 | tf_op jit(solution)/shard_map/ppermute | solution.py:681
  126.2 15.7 %collective-permute-start.35 = (f32[3,128,128]{2,1,0:T(8,128)S(1)}, f32[3,128,128]{2,1,0:T(8,128)S(1)}, u32[]{:S(2)}, u32[]{:S(2)}) collective-permute-start(f32[3,128,128]{2,1,0:T(8,128)S(1)} %get-tuple-element.143), channel_id=1, source_target_pairs={{1,0},{4,1},{5,4},{8,5},{9,8},{12,9},{13,12},{16,13},{17,16},{20,1... | collective-permute-start | bytes 589832 | tf_op jit(solution)/shard_map/ppermute | solution.py:25
  129.1 13.4 %collective-permute-start.36 = (f32[3,128,128]{2,1,0:T(8,128)S(1)}, f32[3,128,128]{2,1,0:T(8,128)S(1)}, u32[]{:S(2)}, u32[]{:S(2)}) collective-permute-start(f32[3,128,128]{2,1,0:T(8,128)S(1)} %get-tuple-element.144), channel_id=1, source_target_pairs={{29,0},{0,1},{1,4},{4,5},{5,8},{8,9},{9,12},{12,13},{13,16},{16,17... | collective-permute-start | bytes 589832 | tf_op jit(solution)/shard_map/ppermute | solution.py:25
  136.8 12.6 %collective-permute-start.46 = (f32[385,128]{1,0:T(8,128)S(1)}, f32[385,128]{1,0:T(8,128)S(1)}, u32[]{:S(2)}, u32[]{:S(2)}) collective-permute-start(f32[385,128]{1,0:T(8,128)S(1)} %get-tuple-element.157), channel_id=1, source_target_pairs={{0,24},{1,25},{4,28},{5,29},{8,16},{9,17},{12,20},{13,21},{16,8},{... | collective-permute-start | bytes 591368 | tf_op jit(solution)/shard_map/ppermute | solution.py:681
  141.8 15.1 %collective-permute-start.48 = (f32[385,128]{1,0:T(8,128)S(1)}, f32[385,128]{1,0:T(8,128)S(1)}, u32[]{:S(2)}, u32[]{:S(2)}) collective-permute-start(f32[385,128]{1,0:T(8,128)S(1)} %get-tuple-element.159), channel_id=1, source_target_pairs={{0,16},{1,17},{4,20},{5,21},{8,24},{9,25},{12,28},{13,29},{16,0},{... | collective-permute-start | bytes 591368 | tf_op jit(solution)/shard_map/ppermute | solution.py:681
  157.0 12.0 %collective-permute-start.37 = (f32[385,128]{1,0:T(8,128)S(1)}, f32[385,128]{1,0:T(8,128)S(1)}, u32[]{:S(2)}, u32[]{:S(2)}) collective-permute-start(f32[385,128]{1,0:T(8,128)S(1)} %get-tuple-element.145), channel_id=1, source_target_pairs={{0,24},{1,25},{4,28},{5,29},{8,16},{9,17},{12,20},{13,21},{16,8},{... | collective-permute-start | bytes 591368 | tf_op jit(solution)/shard_map/ppermute | solution.py:681
  158.8 15.0 %collective-permute-start.39 = (f32[385,128]{1,0:T(8,128)S(1)}, f32[385,128]{1,0:T(8,128)S(1)}, u32[]{:S(2)}, u32[]{:S(2)}) collective-permute-start(f32[385,128]{1,0:T(8,128)S(1)} %get-tuple-element.147), channel_id=1, source_target_pairs={{0,16},{1,17},{4,20},{5,21},{8,24},{9,25},{12,28},{13,29},{16,0},{... | collective-permute-start | bytes 591368 | tf_op jit(solution)/shard_map/ppermute | solution.py:681
  (39 other events, 472.0 us)

commit v4 on v3

--- a/solution.py
+++ b/solution.py
@@ -391,16 +391,20 @@
 
 
 def edge_planes(field_ref, bond_ref, first_ref, carried_ref):
-    bond = bond_ref[0, 0].astype(jnp.float32)
+    bond = bond_ref[...].astype(jnp.float32)
     for component in range(3):
         first_ref[component] = field_ref[component, 0]
         carried_ref[component] = bond * field_ref[component, field_ref.shape[1] - 1]
 
 
 def advance_kernel(edges, *refs):
-    refs, (out_ref, *edge_refs, dipole_ref) = refs[: -2 - 2 * edges], refs[-2 - 2 * edges :]
+    refs, (dipole_ref, *held) = refs[: -1 - 2 * edges], refs[-1 - 2 * edges :]
+    refs, (out_ref, *edge_refs) = refs[: -1 - 2 * edges], refs[-1 - 2 * edges :]
     in_refs, refs = refs[:-7], refs[-7:]
     table_ref, mask_ref, depth_ref, partial_ref, local_ref, field_ref, bond_ref = refs
+    if edges:
+        bond = pltpu.make_async_copy(bond_ref.at[0, bond_ref.shape[1] - 1], *held)
+        bond.start()
     _, planes, width, depth = out_ref.shape
     for component in range(3):
         mixed = gathered_columns(component, in_refs, mask_ref, table_ref, planes)
@@ -426,7 +430,8 @@
         for component in range(3):
             out_ref[component, plane] = stepped[component] * scale
     if edges:
-        edge_planes(out_ref, bond_ref, *edge_refs)
+        bond.wait()
+        edge_planes(out_ref, held[0], *edge_refs)
 
 
 def local_kernel(
@@ -521,6 +526,18 @@
     return jnp.concatenate([high, low, high], axis=1)
 
 
+def depth_table(cell, wave, depth):
+    half = depth // 2
+    cosine, sine = angles(cell, wave & (half - 1), depth)
+    middle = (1 - 2 * (cell & 1)).astype(jnp.float32)
+    return jnp.where(wave < half, cosine, jnp.where(wave == half, middle, -sine))
+
+
+def row_parts(table):
+    high, low = split(table)
+    return jnp.concatenate([high, low, high], axis=0)
+
+
 def iota(shape, axis):
     return lax.broadcasted_iota(jnp.int32, shape, axis)
 
@@ -541,9 +558,30 @@
         mask_ref[1] = jnp.where(above, 1.0, 0.0)
 
 
-def other_tables(routes, row_block, planes, me_ref, temps_ref, order_ref, accept_ref, *out_refs):
-    labels_ref, scale_ref, weight_ref, *out_refs = out_refs
+def first_kernel(routes, row_block, groups, me_ref, field_ref, *refs):
+    blocks, (depth_ref, *table_refs, first_ref, last_ref) = refs[:-7], refs[-7:]
+    depth = depth_ref.shape[1]
+    shape = (depth, depth)
+    depth_ref[...] = row_parts(depth_table(iota(shape, 0), iota(shape, 1), depth))
+    forward_tables(routes, row_block, me_ref, *table_refs)
+    forward_kernel(groups, field_ref, depth_ref, *table_refs, *blocks)
+    for component in range(3):
+        first_ref[component] = field_ref[component, 0]
+        last_ref[component] = field_ref[component, field_ref.shape[1] - 1]
+
+
+def other_tables(
+    routes, row_block, planes, me_ref, temps_ref, order_ref, accept_ref, last_ref, bond_ref, *out_refs
+):
+    labels_ref, scale_ref, carried_ref, weight_ref, depth_ref, *out_refs = out_refs
+    bond = bond_ref[0, planes - 1].astype(jnp.float32)
+    for component in range(3):
+        carried_ref[component] = bond * last_ref[component]
     me = me_ref[0]
+    shape = (weight_ref.shape[1], weight_ref.shape[1])
+    back = depth_table(iota(shape, 1), iota(shape, 0), shape[0])
+    share = jnp.where((iota(shape, 0) & (shape[0] // 2 - 1)) == 0, 1.0, 2.0) / shape[0]
+    depth_ref[...] = row_parts(back * share)
     for pair in range(order_ref.shape[0] // 2):
         left, right = order_ref[2 * pair], order_ref[2 * pair + 1]
         swapped = (accept_ref[left] == 1) & (accept_ref[right] == 1)
@@ -621,21 +659,6 @@
                 out_ref[place : place + unit, :] = in_ref[start : start + unit, :]
 
 
-def depth_tables(depth):
-    half = depth // 2
-    angle = 2.0 * np.pi / depth * np.outer(np.arange(depth), np.arange(half)) % (2.0 * np.pi)
-    middle = np.where(np.arange(depth) % 2 == 0, 1.0, -1.0)[:, None]
-    into = np.concatenate([np.cos(angle), middle, -np.sin(angle[:, 1:])], axis=1)
-    lane = np.arange(depth)
-    out_of = (into * np.where(lane % half == 0, 1.0, 2.0) / depth).T
-    tables = []
-    for table in (into, out_of):
-        high = table.astype(jnp.bfloat16)
-        low = (table - high.astype(np.float64)).astype(jnp.bfloat16)
-        tables.append(jnp.asarray(np.concatenate([high, low, high], axis=0)))
-    return tables
-
-
 def on_device(moments, couplings, noise, kernel, temps, order, accept):
     planes, width, depth = moments.shape[2:]
     row_block = kernel.shape[2]
@@ -647,31 +670,15 @@
     rows = row_block // 2
     routes = [Route(0, rows, far, near), Route(rows, rows, near, far)]
     me = jnp.stack([lax.axis_index(AXES), lax.axis_index("temp")]).astype(jnp.int32)
-    into_depth, out_of_depth = depth_tables(depth)
     lines = count * rows
     field = moments[0]
     whole = shape_of(*field.shape)
     plane_shape = shape_of(3, width, depth)
-    forward = call(
-        functools.partial(forward_tables, routes, row_block),
-        [shape_of(lines, 6 * width, dtype=jnp.bfloat16), shape_of(2, lines, depth)] * 2,
-        [me],
-        specs={0: SCALARS},
-    )
-    square = shape_of(width, 6 * width, dtype=jnp.bfloat16)
-    labels, scales, weights, *others = call(
-        functools.partial(other_tables, routes, row_block, planes),
-        [shape_of(*order.shape, dtype=jnp.int32), shape_of(2, depth), shape_of(6, depth)]
-        + [square, square, shape_of(width, 6 * lines, dtype=jnp.bfloat16), shape_of(4, lines, depth)]
-        * 2,
-        [me, temps, order, accept],
-        specs={i: SCALARS for i in range(4)},
-        out_specs={0: SCALARS},
-    )
-    others = [others[:4], others[4:]]
+    depth_shape = shape_of(3 * depth, depth, dtype=jnp.bfloat16)
+    in_hbm = pl.BlockSpec(memory_space=pltpu.HBM)
+    bond_held = pltpu.VMEM((width, depth), couplings.dtype)
     kernel_rows = kernel.reshape(6, width * row_block, depth)
     noise = noise[:, 0]
-    unread = pl.BlockSpec(memory_space=pl.ANY)
 
     def exchange(blocks, stage):
         size, stride = stage
@@ -694,14 +701,21 @@
         extras = FAR_EXTRA if stage is far else NEAR_EXTRA
         return [shape_of(size + (extras[i] if i < len(extras) else 0), depth) for i in range(stage[0])]
 
-    def forward_part(field):
-        groups = [route.first[0] for route in routes]
-        blocks = call(
-            functools.partial(forward_kernel, groups),
-            blocks_of(routes[0].first) + blocks_of(routes[1].first),
-            [field, into_depth, *forward],
-        )
-        return blocks[: groups[0]], blocks[groups[0] :]
+    groups = [route.first[0] for route in routes]
+    block_shapes = blocks_of(routes[0].first) + blocks_of(routes[1].first)
+
+    def first_part():
+        tables = [shape_of(lines, 6 * width, dtype=jnp.bfloat16), shape_of(2, lines, depth)] * 2
+        outs = call(
+            functools.partial(first_kernel, routes, row_block, groups),
+            block_shapes + [depth_shape] + tables + [plane_shape] * 2,
+            [me, field],
+            specs={0: SCALARS},
+        )
+        return outs[:-7], outs[-7:-2], outs[-2:]
+
+    def forward_part(field, tables):
+        return call(functools.partial(forward_kernel, groups), block_shapes, [field, *tables])
 
     def forward_repack(chunk, blocks, **order):
         first, second = routes[chunk].first, routes[chunk].second
@@ -723,10 +737,23 @@
         kernel_of = functools.partial(repack_backward, second[0], unit)
         return call(kernel_of, blocks_of(first), blocks, lead=waits(second), **order)
 
-    first_plane = field[:, 0]
-    carried = couplings[0, -1].astype(jnp.float32) * field[:, -1]
+    blocks, forward, (first_plane, last_plane) = first_part()
+    square = shape_of(width, 6 * width, dtype=jnp.bfloat16)
+    labels, scales, carried, weights, out_of_depth, *others = call(
+        functools.partial(other_tables, routes, row_block, planes),
+        [shape_of(*order.shape, dtype=jnp.int32), shape_of(2, depth), plane_shape]
+        + [shape_of(6, depth), depth_shape]
+        + [square, square, shape_of(width, 6 * lines, dtype=jnp.bfloat16), shape_of(4, lines, depth)]
+        * 2,
+        [me, temps, order, accept, last_plane, couplings],
+        specs={i: SCALARS for i in range(4)},
+        out_specs={0: SCALARS},
+    )
+    others = [others[:4], others[4:]]
     for step in range(2):
-        a_out, b_out = forward_part(field)
+        if step:
+            blocks = forward_part(field, forward)
+        a_out, b_out = blocks[: groups[0]], blocks[groups[0] :]
         a_far = exchange(a_out, far)
         b_near = exchange(b_out, near)
         b_packed = forward_repack(1, b_near)
@@ -748,7 +775,7 @@
             [whole],
             [scales, field, above, below, couplings, noise],
             scratch=[pltpu.VMEM(field.shape, noise.dtype), pltpu.SemaphoreType.DMA(())],
-            specs={5: unread},
+            specs={5: in_hbm},
             before=a_home[:1],
         )
         (sums,) = call(
@@ -763,9 +790,11 @@
             functools.partial(advance_kernel, edges),
             [whole] + [plane_shape] * 2 * edges,
             a_done
-            + [others[0][2], others[0][3], out_of_depth, sums, local, field, couplings[:1, -1:]],
+            + [others[0][2], others[0][3], out_of_depth, sums, local, field, couplings],
             lead=waits(far),
-            scratch=[pltpu.VMEM(whole.shape, jnp.float32)],
+            specs={len(a_done) + 6: in_hbm},
+            scratch=[pltpu.VMEM(whole.shape, jnp.float32)]
+            + [bond_held, pltpu.SemaphoreType.DMA(())] * edges,
         )
         if edges:
             first_plane, carried = planes_out

time: 177 us -> 174 us (0.983)
    ppermute x48, starting transfers between devices: 47.4 us -> 50.4 us  [exchange(): lax.ppermute(blocks[index], AXES, [(i, i ^ distance) for i in range(count)])]
    ppermute x4, starting transfers between devices: 5.96 us -> 4.11 us  [shifted(): return lax.ppermute(block, axis, route)]
    pallas_call x22 -> x21, Pallas kernels: 29.5 us -> 29.9 us  [call(): pl.pallas_call(body, out_shape=list(outs), in_specs=[unread] * len(before...]
  transfers between devices with their start and end apart: 52 -> 52, of which waited for: 25 -> 27; matrix products, arithmetic and copies ran while one was open for 1% -> 0% of each run, Pallas kernels for 9% -> 10%
where the time goes in v4:
time: 174 us
  waiting for transfers between devices  86.9 us (50%)
  starting transfers between devices  54.6 us (31%)
  Pallas kernels  29.9 us (17%)
    ppermute x48, waiting for transfers between devices, exchange(): lax.ppermute(blocks[index], AXES, [(i, i ^ distance) for i in range(count)])  86.9 us
    ppermute x48, starting transfers between devices, exchange(): lax.ppermute(blocks[index], AXES, [(i, i ^ distance) for i in range(count)])  50.4 us
    pallas_call x21, Pallas kernels, call(): pl.pallas_call(body, out_shape=list(outs), in_specs=[unread] * len(before...  29.9 us
    ppermute x4, starting transfers between devices, shifted(): return lax.ppermute(block, axis, route)  4.11 us
  transfers between devices with their start and end apart: 52, of which 27 were waited for; matrix products, arithmetic and copies ran while one was open for 0% of the time, Pallas kernels for 10%

profile of v4, /device:TPU:0, one launch (start us, length us, event | category | flops | bytes accessed | tf_op | source)
XLA Modules:
  0.0 173.9 jit_solution(6322471150126651452)
XLA Ops:
  2.2 4.2 %shard_map.86 = (f32[384,128]{1,0:T(8,128)S(1)}, f32[385,128]{1,0:T(8,128)S(1)}, f32[385,128]{1,0:T(8,128)S(1)}, f32[385,128]{1,0:T(8,128)S(1)}, f32[384,128]{1,...) custom-call(s32[2]{0:T(128)S(1)} %pad_add_fusion.refs_0_, ...), custom_call_target="tpu_custom_call" | custom-call | flops 1 | bytes 1 | tf_op jit(solution)/shard_map/pallas_call | solution.py:481
  6.4 5.1 %collective-permute-start = (f32[385,128]{1,0:T(8,128)S(1)}, f32[385,128]{1,0:T(8,128)S(1)}, u32[]{:S(2)}, u32[]{:S(2)}) collective-permute-start(f32[385,128]{1,0:T(8,128)S(1)} %get-tuple-element.89), channel_id=1, source_target_pairs={{0,24},{1,25},{4,28},{5,29},{8,16},{9,17},{12,20},{13,21},{16,8},{... | collective-permute-start | bytes 591368 | tf_op jit(solution)/shard_map/ppermute | solution.py:688
  13.9 3.6 %collective-permute-done.refs_0_ = f32[385,128]{1,0:T(8,128)S(1)} collective-permute-done((f32[385,128]{1,0:T(8,128)S(1)}, f32[385,128]{1,0:T(8,128)S(1)}, u32[]{:S(2)}, u32[]{:S(2)}) %collective-permute-start) | collective-permute-done | bytes 197152 | tf_op jit(solution)/shard_map/ppermute | solution.py:688
  17.4 4.5 %collective-permute-done.1.refs_1_ = f32[385,128]{1,0:T(8,128)S(1)} collective-permute-done((f32[385,128]{1,0:T(8,128)S(1)}, f32[385,128]{1,0:T(8,128)S(1)}, u32[]{:S(2)}, u32[]{:S(2)}) %collective-permute-start.1) | collective-permute-done | bytes 197152 | tf_op jit(solution)/shard_map/ppermute | solution.py:688
  22.0 6.6 %collective-permute-done.2.refs_2_ = f32[385,128]{1,0:T(8,128)S(1)} collective-permute-done((f32[385,128]{1,0:T(8,128)S(1)}, f32[385,128]{1,0:T(8,128)S(1)}, u32[]{:S(2)}, u32[]{:S(2)}) %collective-permute-start.2) | collective-permute-done | bytes 197152 | tf_op jit(solution)/shard_map/ppermute | solution.py:688
  38.7 3.0 %collective-permute-start.9 = (f32[3,128,128]{2,1,0:T(8,128)S(1)}, f32[3,128,128]{2,1,0:T(8,128)S(1)}, u32[]{:S(2)}, u32[]{:S(2)}) collective-permute-start(f32[3,128,128]{2,1,0:T(8,128)S(1)} %get-tuple-element.105), channel_id=1, source_target_pairs={{1,0},{4,1},{5,4},{8,5},{9,8},{12,9},{13,12},{16,13},{17,16},{20,1... | collective-permute-start | bytes 589832 | tf_op jit(solution)/shard_map/ppermute | solution.py:25
  46.9 3.1 %collective-permute-done.19.refs_3_ = f32[385,128]{1,0:T(8,128)S(1)} collective-permute-done((f32[385,128]{1,0:T(8,128)S(1)}, f32[385,128]{1,0:T(8,128)S(1)}, u32[]{:S(2)}, u32[]{:S(2)}) %collective-permute-start.19) | collective-permute-done | bytes 197152 | tf_op jit(solution)/shard_map/ppermute | solution.py:688
  52.2 3.4 %collective-permute-start.20 = (f32[385,128]{1,0:T(8,128)S(1)}, f32[385,128]{1,0:T(8,128)S(1)}, u32[]{:S(2)}, u32[]{:S(2)}) collective-permute-start(f32[385,128]{1,0:T(8,128)S(1)} %get-tuple-element.124), channel_id=1, source_target_pairs={{0,24},{1,25},{4,28},{5,29},{8,16},{9,17},{12,20},{13,21},{16,8},{... | collective-permute-start | bytes 591368 | tf_op jit(solution)/shard_map/ppermute | solution.py:688
  62.5 3.3 %collective-permute-done.21.refs_2_ = f32[385,128]{1,0:T(8,128)S(1)} collective-permute-done((f32[385,128]{1,0:T(8,128)S(1)}, f32[385,128]{1,0:T(8,128)S(1)}, u32[]{:S(2)}, u32[]{:S(2)}) %collective-permute-start.21) | collective-permute-done | bytes 197152 | tf_op jit(solution)/shard_map/ppermute | solution.py:688
  65.9 5.0 %collective-permute-done.22.refs_3_ = f32[385,128]{1,0:T(8,128)S(1)} collective-permute-done((f32[385,128]{1,0:T(8,128)S(1)}, f32[385,128]{1,0:T(8,128)S(1)}, u32[]{:S(2)}, u32[]{:S(2)}) %collective-permute-start.22) | collective-permute-done | bytes 197152 | tf_op jit(solution)/shard_map/ppermute | solution.py:688
  79.4 3.9 %collective-permute-done.24.refs_1_ = f32[384,128]{1,0:T(8,128)S(1)} collective-permute-done((f32[384,128]{1,0:T(8,128)S(1)}, f32[384,128]{1,0:T(8,128)S(1)}, u32[]{:S(2)}, u32[]{:S(2)}) %collective-permute-start.24) | collective-permute-done | bytes 196640 | tf_op jit(solution)/shard_map/ppermute | solution.py:688
  84.1 3.7 %collective-permute-done.12.refs_1_ = f32[385,128]{1,0:T(8,128)S(1)} collective-permute-done((f32[385,128]{1,0:T(8,128)S(1)}, f32[385,128]{1,0:T(8,128)S(1)}, u32[]{:S(2)}, u32[]{:S(2)}) %collective-permute-start.12) | collective-permute-done | bytes 197152 | tf_op jit(solution)/shard_map/ppermute | solution.py:688
  87.8 3.4 %collective-permute-done.13.refs_2_ = f32[385,128]{1,0:T(8,128)S(1)} collective-permute-done((f32[385,128]{1,0:T(8,128)S(1)}, f32[385,128]{1,0:T(8,128)S(1)}, u32[]{:S(2)}, u32[]{:S(2)}) %collective-permute-start.13) | collective-permute-done | bytes 197152 | tf_op jit(solution)/shard_map/ppermute | solution.py:688
  93.4 3.2 %shard_map.97 = (f32[384,128]{1,0:T(8,128)S(1)}, f32[385,128]{1,0:T(8,128)S(1)}, f32[385,128]{1,0:T(8,128)S(1)}, f32[385,128]{1,0:T(8,128)S(1)}, f32[384,128]{1,...) custom-call(f32[3,8,128,128]{3,2,1,0:T(8,128)S(1)} %get-tuple-element.135.refs_0_.refs_2_.ref, ...), custom_call_target="tpu_custom_call" | custom-call | flops 1 | bytes 1 | tf_op jit(solution)/shard_map/pallas_call | solution.py:481
  97.6 3.5 %collective-permute-start.28 = (f32[385,128]{1,0:T(8,128)S(1)}, f32[385,128]{1,0:T(8,128)S(1)}, u32[]{:S(2)}, u32[]{:S(2)}) collective-permute-start(f32[385,128]{1,0:T(8,128)S(1)} %get-tuple-element.143), channel_id=1, source_target_pairs={{0,16},{1,17},{4,20},{5,21},{8,24},{9,25},{12,28},{13,29},{16,0},{... | collective-permute-start | bytes 591368 | tf_op jit(solution)/shard_map/ppermute | solution.py:688
  101.2 5.4 %collective-permute-done.26.refs_0_ = f32[385,128]{1,0:T(8,128)S(1)} collective-permute-done((f32[385,128]{1,0:T(8,128)S(1)}, f32[385,128]{1,0:T(8,128)S(1)}, u32[]{:S(2)}, u32[]{:S(2)}) %collective-permute-start.26) | collective-permute-done | bytes 197152 | tf_op jit(solution)/shard_map/ppermute | solution.py:688
  107.4 6.9 %collective-permute-done.28.refs_2_ = f32[385,128]{1,0:T(8,128)S(1)} collective-permute-done((f32[385,128]{1,0:T(8,128)S(1)}, f32[385,128]{1,0:T(8,128)S(1)}, u32[]{:S(2)}, u32[]{:S(2)}) %collective-permute-start.28) | collective-permute-done | bytes 197152 | tf_op jit(solution)/shard_map/ppermute | solution.py:688
  118.2 2.8 %collective-permute-done.29.refs_0_ = f32[384,128]{1,0:T(8,128)S(1)} collective-permute-done((f32[384,128]{1,0:T(8,128)S(1)}, f32[384,128]{1,0:T(8,128)S(1)}, u32[]{:S(2)}, u32[]{:S(2)}) %collective-permute-start.29) | collective-permute-done | bytes 196640 | tf_op jit(solution)/shard_map/ppermute | solution.py:688
  134.2 3.6 %collective-permute-start.46 = (f32[385,128]{1,0:T(8,128)S(1)}, f32[385,128]{1,0:T(8,128)S(1)}, u32[]{:S(2)}, u32[]{:S(2)}) collective-permute-start(f32[385,128]{1,0:T(8,128)S(1)} %get-tuple-element.167), channel_id=1, source_target_pairs={{0,24},{1,25},{4,28},{5,29},{8,16},{9,17},{12,20},{13,21},{16,8},{... | collective-permute-start | bytes 591368 | tf_op jit(solution)/shard_map/ppermute | solution.py:688
  138.7 3.8 %collective-permute-start.34 = (f32[384,128]{1,0:T(8,128)S(1)}, f32[384,128]{1,0:T(8,128)S(1)}, u32[]{:S(2)}, u32[]{:S(2)}) collective-permute-start(f32[384,128]{1,0:T(8,128)S(1)} %get-tuple-element.151), channel_id=1, source_target_pairs={{0,1},{1,0},{4,5},{5,4},{8,9},{9,8},{12,13},{13,12},{16,17},{17,16... | collective-permute-start | bytes 589832 | tf_op jit(solution)/shard_map/ppermute | solution.py:688
  145.8 7.2 %collective-permute-done.48.refs_3_ = f32[385,128]{1,0:T(8,128)S(1)} collective-permute-done((f32[385,128]{1,0:T(8,128)S(1)}, f32[385,128]{1,0:T(8,128)S(1)}, u32[]{:S(2)}, u32[]{:S(2)}) %collective-permute-start.48) | collective-permute-done | bytes 197152 | tf_op jit(solution)/shard_map/ppermute | solution.py:688
  161.1 4.2 %collective-permute-done.50.refs_1_ = f32[384,128]{1,0:T(8,128)S(1)} collective-permute-done((f32[384,128]{1,0:T(8,128)S(1)}, f32[384,128]{1,0:T(8,128)S(1)}, u32[]{:S(2)}, u32[]{:S(2)}) %collective-permute-start.50) | collective-permute-done | bytes 196640 | tf_op jit(solution)/shard_map/ppermute | solution.py:688
  166.1 4.4 %collective-permute-done.39.refs_2_ = f32[385,128]{1,0:T(8,128)S(1)} collective-permute-done((f32[385,128]{1,0:T(8,128)S(1)}, f32[385,128]{1,0:T(8,128)S(1)}, u32[]{:S(2)}, u32[]{:S(2)}) %collective-permute-start.39) | collective-permute-done | bytes 197152 | tf_op jit(solution)/shard_map/ppermute | solution.py:688
  170.5 3.4 %shard_map.106 = f32[3,8,128,128]{3,2,1,0:T(8,128)} custom-call(f32[385,128]{1,0:T(8,128)S(1)} %collective-permute-done.37.refs_0_, f32[385,128]{1,0:T(8,128)S(1)} %collective-permute-done.38.refs_1_, f32[385,128]{1,0:T(8,128)S(1)} %collective-permute-done.39.refs_2_, f32[384,128]{1,0:T(8,128)S(1)} %get-tuple-element.158.refs_0_.refs_3_, ...), custom_call_target="tpu_custom_call" | custom-call | flops 1 | bytes 1 | tf_op jit(solution)/shard_map/pallas_call | solution.py:481
  (118 shorter events, 71.5 us)
Async XLA Ops:
  11.6 17.0 %collective-permute-start.2 = (f32[385,128]{1,0:T(8,128)S(1)}, f32[385,128]{1,0:T(8,128)S(1)}, u32[]{:S(2)}, u32[]{:S(2)}) collective-permute-start(f32[385,128]{1,0:T(8,128)S(1)} %get-tuple-element.91), channel_id=1, source_target_pairs={{0,16},{1,17},{4,20},{5,21},{8,24},{9,25},{12,28},{13,29},{16,0},{... | collective-permute-start | bytes 591368 | tf_op jit(solution)/shard_map/ppermute | solution.py:688
  12.2 18.0 %collective-permute-start.14 = (f32[384,128]{1,0:T(8,128)S(1)}, f32[384,128]{1,0:T(8,128)S(1)}, u32[]{:S(2)}, u32[]{:S(2)}) collective-permute-start(f32[384,128]{1,0:T(8,128)S(1)} %get-tuple-element.114), channel_id=1, source_target_pairs={{0,4},{1,5},{4,0},{5,1},{8,12},{9,13},{12,8},{13,9},{16,20},{17,21... | collective-permute-start | bytes 589832 | tf_op jit(solution)/shard_map/ppermute | solution.py:688
  13.9 16.4 %collective-permute-start.15 = (f32[384,128]{1,0:T(8,128)S(1)}, f32[384,128]{1,0:T(8,128)S(1)}, u32[]{:S(2)}, u32[]{:S(2)}) collective-permute-start(f32[384,128]{1,0:T(8,128)S(1)} %get-tuple-element.115), channel_id=1, source_target_pairs={{0,5},{1,4},{4,1},{5,0},{8,13},{9,12},{12,9},{13,8},{16,21},{17,20... | collective-permute-start | bytes 589832 | tf_op jit(solution)/shard_map/ppermute | solution.py:688
  17.4 12.8 %collective-permute-start.16 = (f32[384,128]{1,0:T(8,128)S(1)}, f32[384,128]{1,0:T(8,128)S(1)}, u32[]{:S(2)}, u32[]{:S(2)}) collective-permute-start(f32[384,128]{1,0:T(8,128)S(1)} %get-tuple-element.116), channel_id=1, source_target_pairs={{0,1},{1,0},{4,5},{5,4},{8,9},{9,8},{12,13},{13,12},{16,17},{17,16... | collective-permute-start | bytes 589832 | tf_op jit(solution)/shard_map/ppermute | solution.py:688
  30.4 13.7 %collective-permute-start.17 = (f32[385,128]{1,0:T(8,128)S(1)}, f32[385,128]{1,0:T(8,128)S(1)}, u32[]{:S(2)}, u32[]{:S(2)}) collective-permute-start(f32[385,128]{1,0:T(8,128)S(1)} %get-tuple-element.118), channel_id=1, source_target_pairs={{0,24},{1,25},{4,28},{5,29},{8,16},{9,17},{12,20},{13,21},{16,8},{... | collective-permute-start | bytes 591368 | tf_op jit(solution)/shard_map/ppermute | solution.py:688
  33.2 13.7 %collective-permute-start.18 = (f32[385,128]{1,0:T(8,128)S(1)}, f32[385,128]{1,0:T(8,128)S(1)}, u32[]{:S(2)}, u32[]{:S(2)}) collective-permute-start(f32[385,128]{1,0:T(8,128)S(1)} %get-tuple-element.119), channel_id=1, source_target_pairs={{0,8},{1,9},{4,12},{5,13},{8,0},{9,1},{12,4},{13,5},{16,24},{17,25... | collective-permute-start | bytes 591368 | tf_op jit(solution)/shard_map/ppermute | solution.py:688
  36.0 14.1 %collective-permute-start.19 = (f32[385,128]{1,0:T(8,128)S(1)}, f32[385,128]{1,0:T(8,128)S(1)}, u32[]{:S(2)}, u32[]{:S(2)}) collective-permute-start(f32[385,128]{1,0:T(8,128)S(1)} %get-tuple-element.120), channel_id=1, source_target_pairs={{0,16},{1,17},{4,20},{5,21},{8,24},{9,25},{12,28},{13,29},{16,0},{... | collective-permute-start | bytes 591368 | tf_op jit(solution)/shard_map/ppermute | solution.py:688
  38.7 16.9 %collective-permute-start.9 = (f32[3,128,128]{2,1,0:T(8,128)S(1)}, f32[3,128,128]{2,1,0:T(8,128)S(1)}, u32[]{:S(2)}, u32[]{:S(2)}) collective-permute-start(f32[3,128,128]{2,1,0:T(8,128)S(1)} %get-tuple-element.105), channel_id=1, source_target_pairs={{1,0},{4,1},{5,4},{8,5},{9,8},{12,9},{13,12},{16,13},{17,16},{20,1... | collective-permute-start | bytes 589832 | tf_op jit(solution)/shard_map/ppermute | solution.py:25
  41.8 14.9 %collective-permute-start.10 = (f32[3,128,128]{2,1,0:T(8,128)S(1)}, f32[3,128,128]{2,1,0:T(8,128)S(1)}, u32[]{:S(2)}, u32[]{:S(2)}) collective-permute-start(f32[3,128,128]{2,1,0:T(8,128)S(1)} %get-tuple-element.106), channel_id=1, source_target_pairs={{29,0},{0,1},{1,4},{4,5},{5,8},{8,9},{9,12},{12,13},{13,16},{16,17... | collective-permute-start | bytes 589832 | tf_op jit(solution)/shard_map/ppermute | solution.py:25
  44.1 14.0 %collective-permute-start.6 = (f32[384,128]{1,0:T(8,128)S(1)}, f32[384,128]{1,0:T(8,128)S(1)}, u32[]{:S(2)}, u32[]{:S(2)}) collective-permute-start(f32[384,128]{1,0:T(8,128)S(1)} %get-tuple-element.101), channel_id=1, source_target_pairs={{0,4},{1,5},{4,0},{5,1},{8,12},{9,13},{12,8},{13,9},{16,20},{17,21... | collective-permute-start | bytes 589832 | tf_op jit(solution)/shard_map/ppermute | solution.py:688
  55.7 15.2 %collective-permute-start.22 = (f32[385,128]{1,0:T(8,128)S(1)}, f32[385,128]{1,0:T(8,128)S(1)}, u32[]{:S(2)}, u32[]{:S(2)}) collective-permute-start(f32[385,128]{1,0:T(8,128)S(1)} %get-tuple-element.126), channel_id=1, source_target_pairs={{0,16},{1,17},{4,20},{5,21},{8,24},{9,25},{12,28},{13,29},{16,0},{... | collective-permute-start | bytes 591368 | tf_op jit(solution)/shard_map/ppermute | solution.py:688
  75.3 12.5 %collective-permute-start.12 = (f32[385,128]{1,0:T(8,128)S(1)}, f32[385,128]{1,0:T(8,128)S(1)}, u32[]{:S(2)}, u32[]{:S(2)}) collective-permute-start(f32[385,128]{1,0:T(8,128)S(1)} %get-tuple-element.108), channel_id=1, source_target_pairs={{0,8},{1,9},{4,12},{5,13},{8,0},{9,1},{12,4},{13,5},{16,24},{17,25... | collective-permute-start | bytes 591368 | tf_op jit(solution)/shard_map/ppermute | solution.py:688
  75.4 15.8 %collective-permute-start.13 = (f32[385,128]{1,0:T(8,128)S(1)}, f32[385,128]{1,0:T(8,128)S(1)}, u32[]{:S(2)}, u32[]{:S(2)}) collective-permute-start(f32[385,128]{1,0:T(8,128)S(1)} %get-tuple-element.109), channel_id=1, source_target_pairs={{0,16},{1,17},{4,20},{5,21},{8,24},{9,25},{12,28},{13,29},{16,0},{... | collective-permute-start | bytes 591368 | tf_op jit(solution)/shard_map/ppermute | solution.py:688
  97.6 16.7 %collective-permute-start.28 = (f32[385,128]{1,0:T(8,128)S(1)}, f32[385,128]{1,0:T(8,128)S(1)}, u32[]{:S(2)}, u32[]{:S(2)}) collective-permute-start(f32[385,128]{1,0:T(8,128)S(1)} %get-tuple-element.143), channel_id=1, source_target_pairs={{0,16},{1,17},{4,20},{5,21},{8,24},{9,25},{12,28},{13,29},{16,0},{... | collective-permute-start | bytes 591368 | tf_op jit(solution)/shard_map/ppermute | solution.py:688
  101.1 13.4 %collective-permute-start.40 = (f32[384,128]{1,0:T(8,128)S(1)}, f32[384,128]{1,0:T(8,128)S(1)}, u32[]{:S(2)}, u32[]{:S(2)}) collective-permute-start(f32[384,128]{1,0:T(8,128)S(1)} %get-tuple-element.159), channel_id=1, source_target_pairs={{0,4},{1,5},{4,0},{5,1},{8,12},{9,13},{12,8},{13,9},{16,20},{17,21... | collective-permute-start | bytes 589832 | tf_op jit(solution)/shard_map/ppermute | solution.py:688
  101.2 13.3 %collective-permute-start.41 = (f32[384,128]{1,0:T(8,128)S(1)}, f32[384,128]{1,0:T(8,128)S(1)}, u32[]{:S(2)}, u32[]{:S(2)}) collective-permute-start(f32[384,128]{1,0:T(8,128)S(1)} %get-tuple-element.160), channel_id=1, source_target_pairs={{0,5},{1,4},{4,1},{5,0},{8,13},{9,12},{12,9},{13,8},{16,21},{17,20... | collective-permute-start | bytes 589832 | tf_op jit(solution)/shard_map/ppermute | solution.py:688
  114.6 12.2 %collective-permute-start.43 = (f32[385,128]{1,0:T(8,128)S(1)}, f32[385,128]{1,0:T(8,128)S(1)}, u32[]{:S(2)}, u32[]{:S(2)}) collective-permute-start(f32[385,128]{1,0:T(8,128)S(1)} %get-tuple-element.163), channel_id=1, source_target_pairs={{0,24},{1,25},{4,28},{5,29},{8,16},{9,17},{12,20},{13,21},{16,8},{... | collective-permute-start | bytes 591368 | tf_op jit(solution)/shard_map/ppermute | solution.py:688
  118.2 11.5 %collective-permute-start.44 = (f32[385,128]{1,0:T(8,128)S(1)}, f32[385,128]{1,0:T(8,128)S(1)}, u32[]{:S(2)}, u32[]{:S(2)}) collective-permute-start(f32[385,128]{1,0:T(8,128)S(1)} %get-tuple-element.164), channel_id=1, source_target_pairs={{0,8},{1,9},{4,12},{5,13},{8,0},{9,1},{12,4},{13,5},{16,24},{17,25... | collective-permute-start | bytes 591368 | tf_op jit(solution)/shard_map/ppermute | solution.py:688
  123.4 14.5 %collective-permute-start.35 = (f32[3,128,128]{2,1,0:T(8,128)S(1)}, f32[3,128,128]{2,1,0:T(8,128)S(1)}, u32[]{:S(2)}, u32[]{:S(2)}) collective-permute-start(f32[3,128,128]{2,1,0:T(8,128)S(1)} %get-tuple-element.153), channel_id=1, source_target_pairs={{1,0},{4,1},{5,4},{8,5},{9,8},{12,9},{13,12},{16,13},{17,16},{20,1... | collective-permute-start | bytes 589832 | tf_op jit(solution)/shard_map/ppermute | solution.py:25
  124.2 14.5 %collective-permute-start.36 = (f32[3,128,128]{2,1,0:T(8,128)S(1)}, f32[3,128,128]{2,1,0:T(8,128)S(1)}, u32[]{:S(2)}, u32[]{:S(2)}) collective-permute-start(f32[3,128,128]{2,1,0:T(8,128)S(1)} %get-tuple-element.154), channel_id=1, source_target_pairs={{29,0},{0,1},{1,4},{4,5},{5,8},{8,9},{9,12},{12,13},{13,16},{16,17... | collective-permute-start | bytes 589832 | tf_op jit(solution)/shard_map/ppermute | solution.py:25
  126.8 11.9 %collective-permute-start.32 = (f32[384,128]{1,0:T(8,128)S(1)}, f32[384,128]{1,0:T(8,128)S(1)}, u32[]{:S(2)}, u32[]{:S(2)}) collective-permute-start(f32[384,128]{1,0:T(8,128)S(1)} %get-tuple-element.149), channel_id=1, source_target_pairs={{0,4},{1,5},{4,0},{5,1},{8,12},{9,13},{12,8},{13,9},{16,20},{17,21... | collective-permute-start | bytes 589832 | tf_op jit(solution)/shard_map/ppermute | solution.py:688
  137.8 15.1 %collective-permute-start.48 = (f32[385,128]{1,0:T(8,128)S(1)}, f32[385,128]{1,0:T(8,128)S(1)}, u32[]{:S(2)}, u32[]{:S(2)}) collective-permute-start(f32[385,128]{1,0:T(8,128)S(1)} %get-tuple-element.169), channel_id=1, source_target_pairs={{0,16},{1,17},{4,20},{5,21},{8,24},{9,25},{12,28},{13,29},{16,0},{... | collective-permute-start | bytes 591368 | tf_op jit(solution)/shard_map/ppermute | solution.py:688
  153.8 12.2 %collective-permute-start.37 = (f32[385,128]{1,0:T(8,128)S(1)}, f32[385,128]{1,0:T(8,128)S(1)}, u32[]{:S(2)}, u32[]{:S(2)}) collective-permute-start(f32[385,128]{1,0:T(8,128)S(1)} %get-tuple-element.155), channel_id=1, source_target_pairs={{0,24},{1,25},{4,28},{5,29},{8,16},{9,17},{12,20},{13,21},{16,8},{... | collective-permute-start | bytes 591368 | tf_op jit(solution)/shard_map/ppermute | solution.py:688
  155.6 14.9 %collective-permute-start.39 = (f32[385,128]{1,0:T(8,128)S(1)}, f32[385,128]{1,0:T(8,128)S(1)}, u32[]{:S(2)}, u32[]{:S(2)}) collective-permute-start(f32[385,128]{1,0:T(8,128)S(1)} %get-tuple-element.157), channel_id=1, source_target_pairs={{0,16},{1,17},{4,20},{5,21},{8,24},{9,25},{12,28},{13,29},{16,0},{... | collective-permute-start | bytes 591368 | tf_op jit(solution)/shard_map/ppermute | solution.py:688
  (36 other events, 460.4 us)

commit v5 on v4

--- a/solution.py
+++ b/solution.py
@@ -358,10 +358,10 @@
                     out_ref[place : place + planes, :] = value[begin : begin + planes]
 
 
-def gathered_columns(component, in_refs, mask_ref, table_ref, planes):
+def gathered_columns(component, in_refs, mask_ref, table_ref, planes, chosen=None):
     part = mask_ref.shape[1] // len(in_refs)
     columns = []
-    for plane in range(planes):
+    for plane in chosen or range(planes):
         start = component * part * planes + plane
         value = jnp.concatenate(
             [ref[pl.ds(start, part, stride=planes), :] for ref in in_refs], axis=0
@@ -398,7 +398,8 @@
 
 
 def advance_kernel(edges, *refs):
-    refs, (dipole_ref, *held) = refs[: -1 - 2 * edges], refs[-1 - 2 * edges :]
+    scratch = 3 if edges else 2
+    refs, (dipole_ref, *held) = refs[:-scratch], refs[-scratch:]
     refs, (out_ref, *edge_refs) = refs[: -1 - 2 * edges], refs[-1 - 2 * edges :]
     in_refs, refs = refs[:-7], refs[-7:]
     table_ref, mask_ref, depth_ref, partial_ref, local_ref, field_ref, bond_ref = refs
@@ -406,29 +407,41 @@
         bond = pltpu.make_async_copy(bond_ref.at[0, bond_ref.shape[1] - 1], *held)
         bond.start()
     _, planes, width, depth = out_ref.shape
-    for component in range(3):
-        mixed = gathered_columns(component, in_refs, mask_ref, table_ref, planes)
-        lines = jnp.concatenate(
-            [
-                mixed[:, plane * depth : (plane + 1) * depth] + partial_ref[component, plane]
-                for plane in range(planes)
-            ],
-            axis=0,
-        )
-        high, low = split(lines)
-        field = product(jnp.concatenate([high, high, low], axis=1), depth_ref[...])
-        dipole_ref[component] = field.reshape(planes, width, depth)
-    for plane in range(planes):
-        moment = [field_ref[component, plane] for component in range(3)]
-        effective = [local_ref[c, plane] + dipole_ref[c, plane] for c in range(3)]
-        torque = cross_parts(moment, effective)
-        twice = cross_parts(moment, torque)
-        stepped = [moment[c] - TIME_STEP * (torque[c] + DAMPING * twice[c]) for c in range(3)]
-        scale = lax.rsqrt(
-            stepped[0] * stepped[0] + stepped[1] * stepped[1] + stepped[2] * stepped[2]
-        )
+    copies = []
+    half = planes // 2
+    for chosen in (range(half), range(half, planes)):
         for component in range(3):
-            out_ref[component, plane] = stepped[component] * scale
+            mixed = gathered_columns(component, in_refs, mask_ref, table_ref, planes, chosen)
+            lines = jnp.concatenate(
+                [
+                    mixed[:, (plane - chosen[0]) * depth : (plane - chosen[0] + 1) * depth] + partial_ref[component, plane]
+                    for plane in chosen
+                ],
+                axis=0,
+            )
+            high, low = split(lines)
+            field = product(jnp.concatenate([high, high, low], axis=1), depth_ref[...])
+            dipole_ref[component, chosen[0] : chosen[-1] + 1] = field.reshape(len(chosen), width, depth)
+        for plane in chosen:
+            moment = [field_ref[component, plane] for component in range(3)]
+            effective = [local_ref[c, plane] + dipole_ref[c, plane] for c in range(3)]
+            torque = cross_parts(moment, effective)
+            twice = cross_parts(moment, torque)
+            stepped = [moment[c] - TIME_STEP * (torque[c] + DAMPING * twice[c]) for c in range(3)]
+            scale = lax.rsqrt(
+                stepped[0] * stepped[0] + stepped[1] * stepped[1] + stepped[2] * stepped[2]
+            )
+            for component in range(3):
+                target_ref = out_ref if edges else dipole_ref
+                target_ref[component, plane] = stepped[component] * scale
+            if not edges:
+                copy = pltpu.make_async_copy(
+                    dipole_ref.at[:, plane], out_ref.at[:, plane], held[0].at[plane]
+                )
+                copy.start()
+                copies.append(copy)
+    for copy in copies:
+        copy.wait()
     if edges:
         bond.wait()
         edge_planes(out_ref, held[0], *edge_refs)
@@ -794,7 +807,8 @@
             lead=waits(far),
             specs={len(a_done) + 6: in_hbm},
             scratch=[pltpu.VMEM(whole.shape, jnp.float32)]
-            + [bond_held, pltpu.SemaphoreType.DMA(())] * edges,
+            + ([bond_held, pltpu.SemaphoreType.DMA(())] if edges else [pltpu.SemaphoreType.DMA((planes,))]),
+            out_specs=None if edges else {0: in_hbm},
         )
         if edges:
             first_plane, carried = planes_out

time: 174 us -> 175 us (level)
  no operation moved by 1% of the time
where the time goes in v5:
time: 175 us; the launch traced here: 174 us
  waiting for transfers between devices  86.9 us (50%)
  starting transfers between devices  54.6 us (31%)
  Pallas kernels  30.2 us (17%)
    ppermute x48, waiting for transfers between devices, exchange(): lax.ppermute(blocks[index], AXES, [(i, i ^ distance) for i in range(count)])  86.9 us
    ppermute x48, starting transfers between devices, exchange(): lax.ppermute(blocks[index], AXES, [(i, i ^ distance) for i in range(count)])  50.5 us
    pallas_call x21, Pallas kernels, call(): pl.pallas_call(body, out_shape=list(outs), in_specs=[unread] * len(before...  30.2 us
    ppermute x4, starting transfers between devices, shifted(): return lax.ppermute(block, axis, route)  4.13 us
  transfers between devices with their start and end apart: 52, of which 27 were waited for; matrix products, arithmetic and copies ran while one was open for 0% of the time, Pallas kernels for 10%

profile of v5, /device:TPU:0, one launch (start us, length us, event | category | flops | bytes accessed | tf_op | source)
XLA Modules:
  0.0 174.4 jit_solution(8790097609520630268)
XLA Ops:
  2.2 4.2 %shard_map.86 = (f32[384,128]{1,0:T(8,128)S(1)}, f32[385,128]{1,0:T(8,128)S(1)}, f32[385,128]{1,0:T(8,128)S(1)}, f32[385,128]{1,0:T(8,128)S(1)}, f32[384,128]{1,...) custom-call(s32[2]{0:T(128)S(1)} %pad_add_fusion.refs_0_, ...), custom_call_target="tpu_custom_call" | custom-call | flops 1 | bytes 1 | tf_op jit(solution)/shard_map/pallas_call | solution.py:494
  6.4 5.1 %collective-permute-start = (f32[385,128]{1,0:T(8,128)S(1)}, f32[385,128]{1,0:T(8,128)S(1)}, u32[]{:S(2)}, u32[]{:S(2)}) collective-permute-start(f32[385,128]{1,0:T(8,128)S(1)} %get-tuple-element.89), channel_id=1, source_target_pairs={{0,24},{1,25},{4,28},{5,29},{8,16},{9,17},{12,20},{13,21},{16,8},{... | collective-permute-start | bytes 591368 | tf_op jit(solution)/shard_map/ppermute | solution.py:701
  13.9 3.6 %collective-permute-done.refs_0_ = f32[385,128]{1,0:T(8,128)S(1)} collective-permute-done((f32[385,128]{1,0:T(8,128)S(1)}, f32[385,128]{1,0:T(8,128)S(1)}, u32[]{:S(2)}, u32[]{:S(2)}) %collective-permute-start) | collective-permute-done | bytes 197152 | tf_op jit(solution)/shard_map/ppermute | solution.py:701
  17.4 4.5 %collective-permute-done.1.refs_1_ = f32[385,128]{1,0:T(8,128)S(1)} collective-permute-done((f32[385,128]{1,0:T(8,128)S(1)}, f32[385,128]{1,0:T(8,128)S(1)}, u32[]{:S(2)}, u32[]{:S(2)}) %collective-permute-start.1) | collective-permute-done | bytes 197152 | tf_op jit(solution)/shard_map/ppermute | solution.py:701
  22.0 6.6 %collective-permute-done.2.refs_2_ = f32[385,128]{1,0:T(8,128)S(1)} collective-permute-done((f32[385,128]{1,0:T(8,128)S(1)}, f32[385,128]{1,0:T(8,128)S(1)}, u32[]{:S(2)}, u32[]{:S(2)}) %collective-permute-start.2) | collective-permute-done | bytes 197152 | tf_op jit(solution)/shard_map/ppermute | solution.py:701
  38.7 3.0 %collective-permute-start.9 = (f32[3,128,128]{2,1,0:T(8,128)S(1)}, f32[3,128,128]{2,1,0:T(8,128)S(1)}, u32[]{:S(2)}, u32[]{:S(2)}) collective-permute-start(f32[3,128,128]{2,1,0:T(8,128)S(1)} %get-tuple-element.105), channel_id=1, source_target_pairs={{1,0},{4,1},{5,4},{8,5},{9,8},{12,9},{13,12},{16,13},{17,16},{20,1... | collective-permute-start | bytes 589832 | tf_op jit(solution)/shard_map/ppermute | solution.py:25
  46.9 3.1 %collective-permute-done.19.refs_3_ = f32[385,128]{1,0:T(8,128)S(1)} collective-permute-done((f32[385,128]{1,0:T(8,128)S(1)}, f32[385,128]{1,0:T(8,128)S(1)}, u32[]{:S(2)}, u32[]{:S(2)}) %collective-permute-start.19) | collective-permute-done | bytes 197152 | tf_op jit(solution)/shard_map/ppermute | solution.py:701
  52.2 3.4 %collective-permute-start.20 = (f32[385,128]{1,0:T(8,128)S(1)}, f32[385,128]{1,0:T(8,128)S(1)}, u32[]{:S(2)}, u32[]{:S(2)}) collective-permute-start(f32[385,128]{1,0:T(8,128)S(1)} %get-tuple-element.124), channel_id=1, source_target_pairs={{0,24},{1,25},{4,28},{5,29},{8,16},{9,17},{12,20},{13,21},{16,8},{... | collective-permute-start | bytes 591368 | tf_op jit(solution)/shard_map/ppermute | solution.py:701
  62.5 3.3 %collective-permute-done.21.refs_2_ = f32[385,128]{1,0:T(8,128)S(1)} collective-permute-done((f32[385,128]{1,0:T(8,128)S(1)}, f32[385,128]{1,0:T(8,128)S(1)}, u32[]{:S(2)}, u32[]{:S(2)}) %collective-permute-start.21) | collective-permute-done | bytes 197152 | tf_op jit(solution)/shard_map/ppermute | solution.py:701
  65.9 5.0 %collective-permute-done.22.refs_3_ = f32[385,128]{1,0:T(8,128)S(1)} collective-permute-done((f32[385,128]{1,0:T(8,128)S(1)}, f32[385,128]{1,0:T(8,128)S(1)}, u32[]{:S(2)}, u32[]{:S(2)}) %collective-permute-start.22) | collective-permute-done | bytes 197152 | tf_op jit(solution)/shard_map/ppermute | solution.py:701
  79.4 3.9 %collective-permute-done.24.refs_1_ = f32[384,128]{1,0:T(8,128)S(1)} collective-permute-done((f32[384,128]{1,0:T(8,128)S(1)}, f32[384,128]{1,0:T(8,128)S(1)}, u32[]{:S(2)}, u32[]{:S(2)}) %collective-permute-start.24) | collective-permute-done | bytes 196640 | tf_op jit(solution)/shard_map/ppermute | solution.py:701
  84.1 3.7 %collective-permute-done.12.refs_1_ = f32[385,128]{1,0:T(8,128)S(1)} collective-permute-done((f32[385,128]{1,0:T(8,128)S(1)}, f32[385,128]{1,0:T(8,128)S(1)}, u32[]{:S(2)}, u32[]{:S(2)}) %collective-permute-start.12) | collective-permute-done | bytes 197152 | tf_op jit(solution)/shard_map/ppermute | solution.py:701
  87.8 3.4 %collective-permute-done.13.refs_2_ = f32[385,128]{1,0:T(8,128)S(1)} collective-permute-done((f32[385,128]{1,0:T(8,128)S(1)}, f32[385,128]{1,0:T(8,128)S(1)}, u32[]{:S(2)}, u32[]{:S(2)}) %collective-permute-start.13) | collective-permute-done | bytes 197152 | tf_op jit(solution)/shard_map/ppermute | solution.py:701
  93.7 3.2 %shard_map.97 = (f32[384,128]{1,0:T(8,128)S(1)}, f32[385,128]{1,0:T(8,128)S(1)}, f32[385,128]{1,0:T(8,128)S(1)}, f32[385,128]{1,0:T(8,128)S(1)}, f32[384,128]{1,...) custom-call(f32[3,8,128,128]{3,2,1,0:T(8,128)S(1)} %get-tuple-element.135.refs_0_.refs_2_.ref, ...), custom_call_target="tpu_custom_call" | custom-call | flops 1 | bytes 1 | tf_op jit(solution)/shard_map/pallas_call | solution.py:494
  97.9 3.5 %collective-permute-start.28 = (f32[385,128]{1,0:T(8,128)S(1)}, f32[385,128]{1,0:T(8,128)S(1)}, u32[]{:S(2)}, u32[]{:S(2)}) collective-permute-start(f32[385,128]{1,0:T(8,128)S(1)} %get-tuple-element.143), channel_id=1, source_target_pairs={{0,16},{1,17},{4,20},{5,21},{8,24},{9,25},{12,28},{13,29},{16,0},{... | collective-permute-start | bytes 591368 | tf_op jit(solution)/shard_map/ppermute | solution.py:701
  101.4 5.4 %collective-permute-done.26.refs_0_ = f32[385,128]{1,0:T(8,128)S(1)} collective-permute-done((f32[385,128]{1,0:T(8,128)S(1)}, f32[385,128]{1,0:T(8,128)S(1)}, u32[]{:S(2)}, u32[]{:S(2)}) %collective-permute-start.26) | collective-permute-done | bytes 197152 | tf_op jit(solution)/shard_map/ppermute | solution.py:701
  107.6 6.9 %collective-permute-done.28.refs_2_ = f32[385,128]{1,0:T(8,128)S(1)} collective-permute-done((f32[385,128]{1,0:T(8,128)S(1)}, f32[385,128]{1,0:T(8,128)S(1)}, u32[]{:S(2)}, u32[]{:S(2)}) %collective-permute-start.28) | collective-permute-done | bytes 197152 | tf_op jit(solution)/shard_map/ppermute | solution.py:701
  118.4 2.9 %collective-permute-done.29.refs_0_ = f32[384,128]{1,0:T(8,128)S(1)} collective-permute-done((f32[384,128]{1,0:T(8,128)S(1)}, f32[384,128]{1,0:T(8,128)S(1)}, u32[]{:S(2)}, u32[]{:S(2)}) %collective-permute-start.29) | collective-permute-done | bytes 196640 | tf_op jit(solution)/shard_map/ppermute | solution.py:701
  134.5 3.6 %collective-permute-start.46 = (f32[385,128]{1,0:T(8,128)S(1)}, f32[385,128]{1,0:T(8,128)S(1)}, u32[]{:S(2)}, u32[]{:S(2)}) collective-permute-start(f32[385,128]{1,0:T(8,128)S(1)} %get-tuple-element.167), channel_id=1, source_target_pairs={{0,24},{1,25},{4,28},{5,29},{8,16},{9,17},{12,20},{13,21},{16,8},{... | collective-permute-start | bytes 591368 | tf_op jit(solution)/shard_map/ppermute | solution.py:701
  138.9 3.7 %collective-permute-start.34 = (f32[384,128]{1,0:T(8,128)S(1)}, f32[384,128]{1,0:T(8,128)S(1)}, u32[]{:S(2)}, u32[]{:S(2)}) collective-permute-start(f32[384,128]{1,0:T(8,128)S(1)} %get-tuple-element.151), channel_id=1, source_target_pairs={{0,1},{1,0},{4,5},{5,4},{8,9},{9,8},{12,13},{13,12},{16,17},{17,16... | collective-permute-start | bytes 589832 | tf_op jit(solution)/shard_map/ppermute | solution.py:701
  145.9 7.3 %collective-permute-done.48.refs_3_ = f32[385,128]{1,0:T(8,128)S(1)} collective-permute-done((f32[385,128]{1,0:T(8,128)S(1)}, f32[385,128]{1,0:T(8,128)S(1)}, u32[]{:S(2)}, u32[]{:S(2)}) %collective-permute-start.48) | collective-permute-done | bytes 197152 | tf_op jit(solution)/shard_map/ppermute | solution.py:701
  161.3 4.2 %collective-permute-done.50.refs_1_ = f32[384,128]{1,0:T(8,128)S(1)} collective-permute-done((f32[384,128]{1,0:T(8,128)S(1)}, f32[384,128]{1,0:T(8,128)S(1)}, u32[]{:S(2)}, u32[]{:S(2)}) %collective-permute-start.50) | collective-permute-done | bytes 196640 | tf_op jit(solution)/shard_map/ppermute | solution.py:701
  166.2 4.5 %collective-permute-done.39.refs_2_ = f32[385,128]{1,0:T(8,128)S(1)} collective-permute-done((f32[385,128]{1,0:T(8,128)S(1)}, f32[385,128]{1,0:T(8,128)S(1)}, u32[]{:S(2)}, u32[]{:S(2)}) %collective-permute-start.39) | collective-permute-done | bytes 197152 | tf_op jit(solution)/shard_map/ppermute | solution.py:701
  170.7 3.4 %shard_map.106 = f32[3,8,128,128]{3,2,1,0:T(8,128)} custom-call(f32[385,128]{1,0:T(8,128)S(1)} %collective-permute-done.37.refs_0_, f32[385,128]{1,0:T(8,128)S(1)} %collective-permute-done.38.refs_1_, f32[385,128]{1,0:T(8,128)S(1)} %collective-permute-done.39.refs_2_, f32[384,128]{1,0:T(8,128)S(1)} %get-tuple-element.158.refs_0_.refs_3_, ...), custom_call_target="tpu_custom_call" | custom-call | flops 1 | bytes 1 | tf_op jit(solution)/shard_map/pallas_call | solution.py:494
  (118 shorter events, 71.8 us)
Async XLA Ops:
  11.6 17.0 %collective-permute-start.2 = (f32[385,128]{1,0:T(8,128)S(1)}, f32[385,128]{1,0:T(8,128)S(1)}, u32[]{:S(2)}, u32[]{:S(2)}) collective-permute-start(f32[385,128]{1,0:T(8,128)S(1)} %get-tuple-element.91), channel_id=1, source_target_pairs={{0,16},{1,17},{4,20},{5,21},{8,24},{9,25},{12,28},{13,29},{16,0},{... | collective-permute-start | bytes 591368 | tf_op jit(solution)/shard_map/ppermute | solution.py:701
  12.2 18.0 %collective-permute-start.14 = (f32[384,128]{1,0:T(8,128)S(1)}, f32[384,128]{1,0:T(8,128)S(1)}, u32[]{:S(2)}, u32[]{:S(2)}) collective-permute-start(f32[384,128]{1,0:T(8,128)S(1)} %get-tuple-element.114), channel_id=1, source_target_pairs={{0,4},{1,5},{4,0},{5,1},{8,12},{9,13},{12,8},{13,9},{16,20},{17,21... | collective-permute-start | bytes 589832 | tf_op jit(solution)/shard_map/ppermute | solution.py:701
  13.9 16.4 %collective-permute-start.15 = (f32[384,128]{1,0:T(8,128)S(1)}, f32[384,128]{1,0:T(8,128)S(1)}, u32[]{:S(2)}, u32[]{:S(2)}) collective-permute-start(f32[384,128]{1,0:T(8,128)S(1)} %get-tuple-element.115), channel_id=1, source_target_pairs={{0,5},{1,4},{4,1},{5,0},{8,13},{9,12},{12,9},{13,8},{16,21},{17,20... | collective-permute-start | bytes 589832 | tf_op jit(solution)/shard_map/ppermute | solution.py:701
  17.4 12.8 %collective-permute-start.16 = (f32[384,128]{1,0:T(8,128)S(1)}, f32[384,128]{1,0:T(8,128)S(1)}, u32[]{:S(2)}, u32[]{:S(2)}) collective-permute-start(f32[384,128]{1,0:T(8,128)S(1)} %get-tuple-element.116), channel_id=1, source_target_pairs={{0,1},{1,0},{4,5},{5,4},{8,9},{9,8},{12,13},{13,12},{16,17},{17,16... | collective-permute-start | bytes 589832 | tf_op jit(solution)/shard_map/ppermute | solution.py:701
  30.4 13.7 %collective-permute-start.17 = (f32[385,128]{1,0:T(8,128)S(1)}, f32[385,128]{1,0:T(8,128)S(1)}, u32[]{:S(2)}, u32[]{:S(2)}) collective-permute-start(f32[385,128]{1,0:T(8,128)S(1)} %get-tuple-element.118), channel_id=1, source_target_pairs={{0,24},{1,25},{4,28},{5,29},{8,16},{9,17},{12,20},{13,21},{16,8},{... | collective-permute-start | bytes 591368 | tf_op jit(solution)/shard_map/ppermute | solution.py:701
  33.2 13.7 %collective-permute-start.18 = (f32[385,128]{1,0:T(8,128)S(1)}, f32[385,128]{1,0:T(8,128)S(1)}, u32[]{:S(2)}, u32[]{:S(2)}) collective-permute-start(f32[385,128]{1,0:T(8,128)S(1)} %get-tuple-element.119), channel_id=1, source_target_pairs={{0,8},{1,9},{4,12},{5,13},{8,0},{9,1},{12,4},{13,5},{16,24},{17,25... | collective-permute-start | bytes 591368 | tf_op jit(solution)/shard_map/ppermute | solution.py:701
  36.0 14.1 %collective-permute-start.19 = (f32[385,128]{1,0:T(8,128)S(1)}, f32[385,128]{1,0:T(8,128)S(1)}, u32[]{:S(2)}, u32[]{:S(2)}) collective-permute-start(f32[385,128]{1,0:T(8,128)S(1)} %get-tuple-element.120), channel_id=1, source_target_pairs={{0,16},{1,17},{4,20},{5,21},{8,24},{9,25},{12,28},{13,29},{16,0},{... | collective-permute-start | bytes 591368 | tf_op jit(solution)/shard_map/ppermute | solution.py:701
  38.7 16.9 %collective-permute-start.9 = (f32[3,128,128]{2,1,0:T(8,128)S(1)}, f32[3,128,128]{2,1,0:T(8,128)S(1)}, u32[]{:S(2)}, u32[]{:S(2)}) collective-permute-start(f32[3,128,128]{2,1,0:T(8,128)S(1)} %get-tuple-element.105), channel_id=1, source_target_pairs={{1,0},{4,1},{5,4},{8,5},{9,8},{12,9},{13,12},{16,13},{17,16},{20,1... | collective-permute-start | bytes 589832 | tf_op jit(solution)/shard_map/ppermute | solution.py:25
  41.8 14.9 %collective-permute-start.10 = (f32[3,128,128]{2,1,0:T(8,128)S(1)}, f32[3,128,128]{2,1,0:T(8,128)S(1)}, u32[]{:S(2)}, u32[]{:S(2)}) collective-permute-start(f32[3,128,128]{2,1,0:T(8,128)S(1)} %get-tuple-element.106), channel_id=1, source_target_pairs={{29,0},{0,1},{1,4},{4,5},{5,8},{8,9},{9,12},{12,13},{13,16},{16,17... | collective-permute-start | bytes 589832 | tf_op jit(solution)/shard_map/ppermute | solution.py:25
  44.1 14.0 %collective-permute-start.6 = (f32[384,128]{1,0:T(8,128)S(1)}, f32[384,128]{1,0:T(8,128)S(1)}, u32[]{:S(2)}, u32[]{:S(2)}) collective-permute-start(f32[384,128]{1,0:T(8,128)S(1)} %get-tuple-element.101), channel_id=1, source_target_pairs={{0,4},{1,5},{4,0},{5,1},{8,12},{9,13},{12,8},{13,9},{16,20},{17,21... | collective-permute-start | bytes 589832 | tf_op jit(solution)/shard_map/ppermute | solution.py:701
  55.7 15.2 %collective-permute-start.22 = (f32[385,128]{1,0:T(8,128)S(1)}, f32[385,128]{1,0:T(8,128)S(1)}, u32[]{:S(2)}, u32[]{:S(2)}) collective-permute-start(f32[385,128]{1,0:T(8,128)S(1)} %get-tuple-element.126), channel_id=1, source_target_pairs={{0,16},{1,17},{4,20},{5,21},{8,24},{9,25},{12,28},{13,29},{16,0},{... | collective-permute-start | bytes 591368 | tf_op jit(solution)/shard_map/ppermute | solution.py:701
  75.3 12.5 %collective-permute-start.12 = (f32[385,128]{1,0:T(8,128)S(1)}, f32[385,128]{1,0:T(8,128)S(1)}, u32[]{:S(2)}, u32[]{:S(2)}) collective-permute-start(f32[385,128]{1,0:T(8,128)S(1)} %get-tuple-element.108), channel_id=1, source_target_pairs={{0,8},{1,9},{4,12},{5,13},{8,0},{9,1},{12,4},{13,5},{16,24},{17,25... | collective-permute-start | bytes 591368 | tf_op jit(solution)/shard_map/ppermute | solution.py:701
  75.4 15.8 %collective-permute-start.13 = (f32[385,128]{1,0:T(8,128)S(1)}, f32[385,128]{1,0:T(8,128)S(1)}, u32[]{:S(2)}, u32[]{:S(2)}) collective-permute-start(f32[385,128]{1,0:T(8,128)S(1)} %get-tuple-element.109), channel_id=1, source_target_pairs={{0,16},{1,17},{4,20},{5,21},{8,24},{9,25},{12,28},{13,29},{16,0},{... | collective-permute-start | bytes 591368 | tf_op jit(solution)/shard_map/ppermute | solution.py:701
  97.9 16.7 %collective-permute-start.28 = (f32[385,128]{1,0:T(8,128)S(1)}, f32[385,128]{1,0:T(8,128)S(1)}, u32[]{:S(2)}, u32[]{:S(2)}) collective-permute-start(f32[385,128]{1,0:T(8,128)S(1)} %get-tuple-element.143), channel_id=1, source_target_pairs={{0,16},{1,17},{4,20},{5,21},{8,24},{9,25},{12,28},{13,29},{16,0},{... | collective-permute-start | bytes 591368 | tf_op jit(solution)/shard_map/ppermute | solution.py:701
  101.3 13.4 %collective-permute-start.40 = (f32[384,128]{1,0:T(8,128)S(1)}, f32[384,128]{1,0:T(8,128)S(1)}, u32[]{:S(2)}, u32[]{:S(2)}) collective-permute-start(f32[384,128]{1,0:T(8,128)S(1)} %get-tuple-element.159), channel_id=1, source_target_pairs={{0,4},{1,5},{4,0},{5,1},{8,12},{9,13},{12,8},{13,9},{16,20},{17,21... | collective-permute-start | bytes 589832 | tf_op jit(solution)/shard_map/ppermute | solution.py:701
  101.4 13.3 %collective-permute-start.41 = (f32[384,128]{1,0:T(8,128)S(1)}, f32[384,128]{1,0:T(8,128)S(1)}, u32[]{:S(2)}, u32[]{:S(2)}) collective-permute-start(f32[384,128]{1,0:T(8,128)S(1)} %get-tuple-element.160), channel_id=1, source_target_pairs={{0,5},{1,4},{4,1},{5,0},{8,13},{9,12},{12,9},{13,8},{16,21},{17,20... | collective-permute-start | bytes 589832 | tf_op jit(solution)/shard_map/ppermute | solution.py:701
  114.8 12.2 %collective-permute-start.43 = (f32[385,128]{1,0:T(8,128)S(1)}, f32[385,128]{1,0:T(8,128)S(1)}, u32[]{:S(2)}, u32[]{:S(2)}) collective-permute-start(f32[385,128]{1,0:T(8,128)S(1)} %get-tuple-element.163), channel_id=1, source_target_pairs={{0,24},{1,25},{4,28},{5,29},{8,16},{9,17},{12,20},{13,21},{16,8},{... | collective-permute-start | bytes 591368 | tf_op jit(solution)/shard_map/ppermute | solution.py:701
  118.4 11.5 %collective-permute-start.44 = (f32[385,128]{1,0:T(8,128)S(1)}, f32[385,128]{1,0:T(8,128)S(1)}, u32[]{:S(2)}, u32[]{:S(2)}) collective-permute-start(f32[385,128]{1,0:T(8,128)S(1)} %get-tuple-element.164), channel_id=1, source_target_pairs={{0,8},{1,9},{4,12},{5,13},{8,0},{9,1},{12,4},{13,5},{16,24},{17,25... | collective-permute-start | bytes 591368 | tf_op jit(solution)/shard_map/ppermute | solution.py:701
  123.6 14.5 %collective-permute-start.35 = (f32[3,128,128]{2,1,0:T(8,128)S(1)}, f32[3,128,128]{2,1,0:T(8,128)S(1)}, u32[]{:S(2)}, u32[]{:S(2)}) collective-permute-start(f32[3,128,128]{2,1,0:T(8,128)S(1)} %get-tuple-element.153), channel_id=1, source_target_pairs={{1,0},{4,1},{5,4},{8,5},{9,8},{12,9},{13,12},{16,13},{17,16},{20,1... | collective-permute-start | bytes 589832 | tf_op jit(solution)/shard_map/ppermute | solution.py:25
  124.4 14.5 %collective-permute-start.36 = (f32[3,128,128]{2,1,0:T(8,128)S(1)}, f32[3,128,128]{2,1,0:T(8,128)S(1)}, u32[]{:S(2)}, u32[]{:S(2)}) collective-permute-start(f32[3,128,128]{2,1,0:T(8,128)S(1)} %get-tuple-element.154), channel_id=1, source_target_pairs={{29,0},{0,1},{1,4},{4,5},{5,8},{8,9},{9,12},{12,13},{13,16},{16,17... | collective-permute-start | bytes 589832 | tf_op jit(solution)/shard_map/ppermute | solution.py:25
  127.0 11.9 %collective-permute-start.32 = (f32[384,128]{1,0:T(8,128)S(1)}, f32[384,128]{1,0:T(8,128)S(1)}, u32[]{:S(2)}, u32[]{:S(2)}) collective-permute-start(f32[384,128]{1,0:T(8,128)S(1)} %get-tuple-element.149), channel_id=1, source_target_pairs={{0,4},{1,5},{4,0},{5,1},{8,12},{9,13},{12,8},{13,9},{16,20},{17,21... | collective-permute-start | bytes 589832 | tf_op jit(solution)/shard_map/ppermute | solution.py:701
  138.0 15.1 %collective-permute-start.48 = (f32[385,128]{1,0:T(8,128)S(1)}, f32[385,128]{1,0:T(8,128)S(1)}, u32[]{:S(2)}, u32[]{:S(2)}) collective-permute-start(f32[385,128]{1,0:T(8,128)S(1)} %get-tuple-element.169), channel_id=1, source_target_pairs={{0,16},{1,17},{4,20},{5,21},{8,24},{9,25},{12,28},{13,29},{16,0},{... | collective-permute-start | bytes 591368 | tf_op jit(solution)/shard_map/ppermute | solution.py:701
  154.2 12.0 %collective-permute-start.37 = (f32[385,128]{1,0:T(8,128)S(1)}, f32[385,128]{1,0:T(8,128)S(1)}, u32[]{:S(2)}, u32[]{:S(2)}) collective-permute-start(f32[385,128]{1,0:T(8,128)S(1)} %get-tuple-element.155), channel_id=1, source_target_pairs={{0,24},{1,25},{4,28},{5,29},{8,16},{9,17},{12,20},{13,21},{16,8},{... | collective-permute-start | bytes 591368 | tf_op jit(solution)/shard_map/ppermute | solution.py:701
  155.8 15.0 %collective-permute-start.39 = (f32[385,128]{1,0:T(8,128)S(1)}, f32[385,128]{1,0:T(8,128)S(1)}, u32[]{:S(2)}, u32[]{:S(2)}) collective-permute-start(f32[385,128]{1,0:T(8,128)S(1)} %get-tuple-element.157), channel_id=1, source_target_pairs={{0,16},{1,17},{4,20},{5,21},{8,24},{9,25},{12,28},{13,29},{16,0},{... | collective-permute-start | bytes 591368 | tf_op jit(solution)/shard_map/ppermute | solution.py:701
  (36 other events, 460.0 us)
